TPU v7x, 32 devices: a whole 2x2x4 slice. The times are simulated.
32 devices in a mesh: groups: 2 (over x), scan: 8 (over z, y), tile: 2 (over core).
Axes of the slice: x: 2, y: 2, z: 4, core: 2. Of those that a mesh axis runs over, the one named last changes fastest.
Arguments:
- object_field: float32 [2, 10240, 384], P(None, ('groups', 'scan', 'tile')), parts along dimension 1, may hold values from -6 to 6
- probe_modes: float32 [2, 32, 65536], P(None, 'groups', ('scan', 'tile')), parts along dimension 1, may hold values from -6 to 6
- weights: float32 [2, 256, 16], P(None, ('groups', 'scan', 'tile')), parts along dimension 1, may hold values from -1.2 to 1.2
- amplitude: bfloat16 [256, 256, 256], P(('groups', 'scan', 'tile')), parts along dimension 0, may hold values from 0 to 3
- slot_count: int32 [32], P(('groups', 'scan')), parts along dimension 0, may hold values from 1 to 8, 96 in all
- tile_owner: int32 [256], P(('groups', 'scan')), parts along dimension 0, may hold values from 0 to 1
- corner_row: int32 [256], P(('groups', 'scan')), parts along dimension 0, may hold values from 0 to 64
- corner_col: int32 [256], P(('groups', 'scan')), parts along dimension 0, may hold values from 0 to 128
Outputs:
- new_object: float32 [2, 10240, 384], P(None, ('groups', 'scan', 'tile')), parts along dimension 1
- new_modes: float32 [2, 32, 65536], P(None, 'groups', ('scan', 'tile')), parts along dimension 1
- new_weights: float32 [2, 256, 16], P(None, ('groups', 'scan', 'tile')), parts along dimension 1
There are 2 independent parts, one for each index of `groups`. A program takes and returns all parts, laid end to end along the dimension named above; each array names one. Nothing has to cross between parts.
Inputs may be any that keep to these rules, and one draw needn't show every extreme that they name: slot_count[d] positions live on device d, in its slots 0 to slot_count[d] - 1; some device of every part holds 8. `tile_owner`: the tile, among the 2 tiles of the same scan index, whose rows hold the position's patch. `corner_row`: a patch lies wholly inside its tile's rows. `corner_col`: a patch lies wholly inside the object's columns.
All inputs are finite; a program needn't handle non-finite values.
Results may differ from a plain program's by a relative error of at most 0.0097.
Values may be sent and summed in bfloat16 or wider, within the bound.
No kernel may reach another device: no remote copies, remote signals or barrier semaphores. Data moves between devices by JAX's collectives and lax.ppermute only.
A program may use at most 128 MiB of HBM per device.

v0:
```python
import math

import jax
import jax.numpy as jnp
from jax import lax
from jax.sharding import PartitionSpec as P

OBJ_STEP = 0.125
PROBE_STEP = 0.5
best_precision = lax.Precision.HIGHEST


def joined(value, axis, join):
    pieces = jax.tree.map(lambda part: lax.all_gather(part, axis), value)
    head = jax.tree.map(lambda part: part[0], pieces)
    tail = jax.tree.map(lambda part: part[1:], pieces)
    running, _ = lax.scan(lambda running, piece: (join(running, piece), None), head, tail)
    return running


def dft_tables(length):
    pixel_ids = jnp.arange(length, dtype=jnp.int32)
    phase_ids = pixel_ids[:, None] * pixel_ids[None, :] % length
    angles = phase_ids.astype(jnp.float32) * (2.0 * math.pi / length)
    norm_scale = 1.0 / math.sqrt(length)
    cos_tab = (jnp.cos(angles) * norm_scale).astype(jnp.bfloat16)
    sin_tab = (jnp.sin(angles) * norm_scale).astype(jnp.bfloat16)
    forward_rows = jnp.concatenate(
        [jnp.concatenate([cos_tab, sin_tab], axis=1), jnp.concatenate([-sin_tab, cos_tab], axis=1)],
        axis=0,
    )
    inverse_rows = jnp.concatenate(
        [jnp.concatenate([cos_tab, -sin_tab], axis=1), jnp.concatenate([sin_tab, cos_tab], axis=1)],
        axis=0,
    )
    return (cos_tab, sin_tab, forward_rows, inverse_rows)


def rows_pass(row_table, planes):
    count_pos = planes.shape[0]
    length = planes.shape[2]
    flat_planes = planes.reshape(count_pos, 2 * length, length)
    result = jnp.einsum("ij,njb->nib", row_table, flat_planes, preferred_element_type=jnp.float32)
    return result.reshape(count_pos, 2, length, length)


def cols_pass(cos_tab, sin_tab, planes, direction):
    real_part = planes[:, 0]
    imag_part = planes[:, 1]
    out_real = jnp.dot(
        real_part, cos_tab, preferred_element_type=jnp.float32
    ) + direction * jnp.dot(imag_part, sin_tab, preferred_element_type=jnp.float32)
    out_imag = jnp.dot(
        imag_part, cos_tab, preferred_element_type=jnp.float32
    ) - direction * jnp.dot(real_part, sin_tab, preferred_element_type=jnp.float32)
    return jnp.stack([out_real, out_imag], axis=1)


def relax_positions(patch_b, probe_field, amp_block, live_mask, tables):
    cos_tab, sin_tab, forward_rows, inverse_rows = tables
    obj_real = patch_b[:, 0].astype(jnp.float32)
    obj_imag = patch_b[:, 1].astype(jnp.float32)
    probe_real = probe_field[:, 0]
    probe_imag = probe_field[:, 1]
    exit_wave = jnp.stack(
        [
            probe_real * obj_real - probe_imag * obj_imag,
            probe_real * obj_imag + probe_imag * obj_real,
        ],
        axis=1,
    ).astype(jnp.bfloat16)
    sectioned = rows_pass(forward_rows, exit_wave).astype(jnp.bfloat16)
    far_field = cols_pass(cos_tab, sin_tab, sectioned, 1.0)
    power = far_field[:, 0] * far_field[:, 0] + far_field[:, 1] * far_field[:, 1]
    scale_map = amp_block.astype(jnp.float32) / jnp.sqrt(power + 1.0)
    revised = (far_field * scale_map[:, None]).astype(jnp.bfloat16)
    came_back = rows_pass(inverse_rows, revised).astype(jnp.bfloat16)
    near_field = cols_pass(cos_tab, sin_tab, came_back, -1.0)
    delta_field = near_field - exit_wave.astype(jnp.float32)
    delta_real = delta_field[:, 0]
    delta_imag = delta_field[:, 1]
    mask_wide = live_mask[:, None, None, None]
    grad_field = (
        jnp.stack(
            [
                probe_real * delta_real + probe_imag * delta_imag,
                probe_real * delta_imag - probe_imag * delta_real,
            ],
            axis=1,
        )
        * mask_wide
    )
    change = jnp.stack(
        [
            obj_real * delta_real + obj_imag * delta_imag,
            obj_real * delta_imag - obj_imag * delta_real,
        ],
        axis=1,
    )
    updated = (probe_field + PROBE_STEP * change) * mask_wide
    return (grad_field.astype(jnp.bfloat16), updated.astype(jnp.bfloat16))


def probe_mixing(weights_b):
    wt_real = weights_b[0]
    wt_imag = weights_b[1]
    slot_cap = wt_real.shape[0]
    mode_count = wt_real.shape[1]
    upper_rows = jnp.concatenate([wt_real, -wt_imag], axis=1)
    lower_rows = jnp.concatenate([wt_imag, wt_real], axis=1)
    return jnp.stack([upper_rows, lower_rows], axis=1).reshape(2 * slot_cap, 2 * mode_count)


def gather_mixing(weights_b):
    wt_real = weights_b[0]
    wt_imag = weights_b[1]
    slot_cap = wt_real.shape[0]
    mode_count = wt_real.shape[1]
    real_rows = jnp.stack([wt_real.T, wt_imag.T], axis=2)
    imag_rows = jnp.stack([-wt_imag.T, wt_real.T], axis=2)
    return jnp.stack([real_rows, imag_rows], axis=0).reshape(2 * mode_count, 2 * slot_cap)


def project_weights(updated_flat, basis_flat, slot_cap, mode_count, pixels):
    table_full = jnp.einsum(
        "ip,jp->ij", updated_flat, basis_flat, preferred_element_type=jnp.float32
    )
    table_full = table_full.reshape(slot_cap, 2, 2, mode_count)
    new_real = table_full[:, 0, 0] + table_full[:, 1, 1]
    new_imag = table_full[:, 1, 0] - table_full[:, 0, 1]
    return jnp.stack([new_real, new_imag], axis=0) / pixels


def orthogonal_factor(mat_real, mat_imag):
    width = mat_real.shape[1]
    col_ids = jnp.arange(width, dtype=jnp.int32)
    work_real = mat_real
    work_imag = mat_imag
    rows_real = []
    rows_imag = []
    for pivot in range(width):
        col_real = work_real[:, pivot]
        col_imag = work_imag[:, pivot]
        col_norm = jnp.sqrt(jnp.sum(col_real * col_real + col_imag * col_imag))
        unit_real = col_real / col_norm
        unit_imag = col_imag / col_norm
        dot_real = jnp.dot(unit_real, work_real, precision=best_precision) + jnp.dot(
            unit_imag, work_imag, precision=best_precision
        )
        dot_imag = jnp.dot(unit_real, work_imag, precision=best_precision) - jnp.dot(
            unit_imag, work_real, precision=best_precision
        )
        later = col_ids > pivot
        dot_real = jnp.where(later, dot_real, 0.0)
        dot_imag = jnp.where(later, dot_imag, 0.0)
        rows_real.append(jnp.where(col_ids == pivot, col_norm, dot_real))
        rows_imag.append(dot_imag)
        work_real = work_real - (
            unit_real[:, None] * dot_real[None, :] - unit_imag[:, None] * dot_imag[None, :]
        )
        work_imag = work_imag - (
            unit_real[:, None] * dot_imag[None, :] + unit_imag[:, None] * dot_real[None, :]
        )
    return (jnp.stack(rows_real), jnp.stack(rows_imag))


def stack_factors(first_fac, second_fac):
    return orthogonal_factor(
        jnp.concatenate([first_fac[0], second_fac[0]], axis=0),
        jnp.concatenate([first_fac[1], second_fac[1]], axis=0),
    )


def solve_rows(mode_real, mode_imag, fac_real, fac_imag):
    width = mode_real.shape[0]
    solved_real = []
    solved_imag = []
    for pivot in range(width):
        acc_real = mode_real[pivot]
        acc_imag = mode_imag[pivot]
        for earlier in range(pivot):
            coef_real = fac_real[earlier, pivot]
            coef_imag = fac_imag[earlier, pivot]
            acc_real = acc_real - (
                coef_real * solved_real[earlier] - coef_imag * solved_imag[earlier]
            )
            acc_imag = acc_imag - (
                coef_real * solved_imag[earlier] + coef_imag * solved_real[earlier]
            )
        solved_real.append(acc_real / fac_real[pivot, pivot])
        solved_imag.append(acc_imag / fac_real[pivot, pivot])
    return jnp.stack([jnp.stack(solved_real), jnp.stack(solved_imag)])


def local(
    object_field, probe_modes, weights, amplitude, slot_count, tile_owner, corner_row, corner_col
):
    tile_count = lax.axis_size("tile")
    my_tile = lax.axis_index("tile")
    slot_cap = amplitude.shape[0]
    length = amplitude.shape[1]
    mode_count = probe_modes.shape[1]
    pixels = length * length
    tables = dft_tables(length)
    zero_index = jnp.zeros((), jnp.int32)
    slot_ids = jnp.arange(slot_cap, dtype=jnp.int32)
    pair_live = (slot_ids[None, :] < slot_count[:, None]).astype(jnp.float32)
    pair_owner = tile_owner.reshape(tile_count, slot_cap)
    pair_row = corner_row.reshape(tile_count, slot_cap)
    pair_col = corner_col.reshape(tile_count, slot_cap)
    live_mask = lax.dynamic_index_in_dim(pair_live, my_tile, 0, keepdims=False)
    my_owner = lax.dynamic_index_in_dim(pair_owner, my_tile, 0, keepdims=False)
    tile_b = object_field.astype(jnp.bfloat16)
    modes_b = lax.all_gather(probe_modes.astype(jnp.bfloat16), ("scan", "tile"), axis=2, tiled=True)
    basis_flat = modes_b.reshape(2 * mode_count, pixels)
    weights_b = weights.astype(jnp.bfloat16)
    probe_field = jnp.dot(
        probe_mixing(weights_b), basis_flat, preferred_element_type=jnp.float32
    ).reshape(slot_cap, 2, length, length)
    wanted = ((pair_owner == my_tile) & (pair_live > 0.0)).astype(jnp.bfloat16)

    def cut_piece(row_at, col_at, flag):
        return lax.dynamic_slice(tile_b, (zero_index, row_at, col_at), (2, length, length)) * flag

    cut_patches = jax.vmap(jax.vmap(cut_piece))(pair_row, pair_col, wanted)
    arrived = lax.all_to_all(cut_patches, "tile", split_axis=0, concat_axis=0, tiled=True)
    patch_b = jnp.sum(arrived, axis=0)
    grad_b, updated_b = relax_positions(patch_b, probe_field, amplitude, live_mask, tables)
    target_ids = jnp.arange(tile_count, dtype=jnp.int32)[:, None]
    route_mask = (my_owner[None, :] == target_ids).astype(jnp.bfloat16)
    outgoing = grad_b[None] * route_mask[:, :, None, None, None]
    returned = lax.all_to_all(outgoing, "tile", split_axis=0, concat_axis=0, tiled=True)
    flat_back = returned.reshape(tile_count * slot_cap, 2, length, length)
    flat_rows = pair_row.reshape(tile_count * slot_cap)
    flat_cols = pair_col.reshape(tile_count * slot_cap)

    def add_back(position, grad_accum):
        grad_piece = lax.dynamic_index_in_dim(flat_back, position, 0, keepdims=False).astype(
            jnp.float32
        )
        row_at = lax.dynamic_index_in_dim(flat_rows, position, 0, keepdims=False)
        col_at = lax.dynamic_index_in_dim(flat_cols, position, 0, keepdims=False)
        old_block = lax.dynamic_slice(grad_accum, (zero_index, row_at, col_at), (2, length, length))
        return lax.dynamic_update_slice(
            grad_accum, old_block + grad_piece, (zero_index, row_at, col_at)
        )

    grad_accum = lax.fori_loop(
        0, tile_count * slot_cap, add_back, jnp.zeros(object_field.shape, jnp.float32)
    )
    new_object = object_field + OBJ_STEP * grad_accum
    updated_flat = updated_b.reshape(2 * slot_cap, pixels)
    new_weights = project_weights(updated_flat, basis_flat, slot_cap, mode_count, pixels)
    mode_term = jnp.dot(
        gather_mixing(weights_b), updated_flat, preferred_element_type=jnp.float32
    ).reshape(2, mode_count, pixels)
    local_modes = lax.psum_scatter(mode_term, ("scan", "tile"), scatter_dimension=2, tiled=True)
    local_real = local_modes[0]
    local_imag = local_modes[1]
    start_fac = orthogonal_factor(local_real.T, local_imag.T)
    fac_real, fac_imag = joined((start_fac[0], start_fac[1]), ("scan", "tile"), stack_factors)
    new_modes = solve_rows(local_real, local_imag, fac_real, fac_imag) * math.sqrt(pixels)
    return (new_object, new_modes, new_weights)


def solution(mesh):
    in_specs = (
        P(None, ("groups", "scan", "tile"), None),
        P(None, "groups", ("scan", "tile")),
        P(None, ("groups", "scan", "tile"), None),
        P(("groups", "scan", "tile"), None, None),
        P(("groups", "scan")),
        P(("groups", "scan")),
        P(("groups", "scan")),
        P(("groups", "scan")),
    )
    out_specs = (
        P(None, ("groups", "scan", "tile"), None),
        P(None, "groups", ("scan", "tile")),
        P(None, ("groups", "scan", "tile"), None),
    )
    return jax.shard_map(local, mesh=mesh, in_specs=in_specs, out_specs=out_specs, check_vma=False)
```

profile of v0, /device:TPU:0, one launch (start us, length us, event | category | flops | bytes accessed | tf_op | source)
XLA Modules:
  0.0 1273.0 jit_solution(12766804896217780601)
XLA Ops:
  12.7 44.1 %while.28 = (s32[]{:T(128)}, bf16[2,320,384]{2,1,0:T(8,128)(2,1)S(1)}, s32[16,3]{0,1:T(4,128)S(1)}, bf16[16,2,256,256]{3,2,1,0:T(8,128)(2,1)}, s32[]{:T(128)}) while((s32[]{:T(128)}, bf16[2,320,384]{2,1,0:T(8,128)(2,1)S(1)}, s32[16,3]{0,1:T(4,128)S(1)}, bf16[16,2,256,256]{3,2,1,0:T(8,128)(2,1)}, s32[]{:T(128)}) %tuple.412), condition=%wide.while_cond, body=%wide.while_body.sunk | while | flops 2 | bytes 525929 | solution.py:223
  56.8 4.5 broadcast_multiply_fusion.1
  61.3 5.7 all-to-all-start
  67.3 4.2 all-to-all-done
  71.5 5.0 reduce_sum.300
  80.4 3.2 fusion.152
  86.9 2.7 convert_bitcast_fusion.1
  89.6 2.5 convert_element_type.185
  92.2 4.2 fusion.444
  96.4 4.5 copy.72
  100.9 2.7 fusion.246
  103.7 4.7 copy.73
  114.2 2.7 convert_bitcast_fusion
  116.8 2.5 convert_element_type.191
  119.4 4.2 fusion.443
  123.6 3.0 copy.76
  126.6 2.7 fusion.240
  129.4 3.4 copy.77
  139.8 3.0 fusion.163
  142.8 3.6 fusion.158
  148.2 3.2 reshape.5862
  151.4 6.0 fusion.365
  159.5 2.3 broadcast_multiply_fusion
  161.8 5.6 all-to-all-start.1
  167.5 7.6 fusion.159
  175.8 214.7 %while.26 = (s32[]{:T(128)}, f32[2,320,384]{2,1,0:T(8,128)S(1)}, s32[16]{0:T(128)S(1)}, s32[16]{0:T(128)S(1)}, bf16[16,2,256,256]{3,2,1,0:T(8,128)(2,1)}, /*index=5*/s32[]{:T(128)}, s32[]{:T(128)}, s32[]{:T(128)}, s32[]{:T(128)}) while((s32[]{:T(128)}, f32[2,320,384]{2,1,0:T(8,128)S(1)}, s32[16]{0:T(128)S(1)}, s32[16]{0:T(128)S(1)}, ...), condition=%wide.region_2.3_spmd, body=%wide.region_1.2_spmd.sunk | while | flops 262152 | bytes 2359497 | solution.py:248
  182.1 7.0 dynamic_update_slice.8
  195.5 6.9 dynamic_update_slice.8
  208.7 7.3 dynamic_update_slice.8
  222.2 7.2 dynamic_update_slice.8
  235.7 7.0 dynamic_update_slice.8
  249.0 7.0 dynamic_update_slice.8
  262.2 6.9 dynamic_update_slice.8
  275.4 7.2 dynamic_update_slice.8
  288.8 7.0 dynamic_update_slice.8
  302.1 7.2 dynamic_update_slice.8
  315.5 7.2 dynamic_update_slice.8
  329.0 7.0 dynamic_update_slice.8
  342.3 7.3 dynamic_update_slice.8
  355.9 7.5 dynamic_update_slice.8
  369.6 7.5 dynamic_update_slice.8
  383.4 6.9 dynamic_update_slice.8
  447.2 21.6 %all-gather.1 = f32[256,16]{1,0:T(8,128)S(1)} all-gather(f32[16,16]{1,0:T(8,128)S(1)} %stack.301), channel_id=3, replica_groups=mesh['groups'=2,'scan'=8,'tile'=2] {'scan','tile'}, dimensions={0}, use_global_device_ids=true | all-gather | bytes 17408 | tf_op jit(solution)/shard_map/all_gather | solution.py:14
  469.9 18.2 %all-gather = f32[256,16]{1,0:T(8,128)S(1)} all-gather(f32[16,16]{1,0:T(8,128)S(1)} %stack.299), channel_id=2, replica_groups=mesh['groups'=2,'scan'=8,'tile'=2] {'scan','tile'}, dimensions={0}, use_global_device_ids=true | all-gather | bytes 17408 | tf_op jit(solution)/shard_map/all_gather | solution.py:14
  488.1 570.8 %while.27 = (s32[]{:T(128)}, f32[16,16]{1,0:T(8,128)S(1)}, f32[16,16]{1,0:T(8,128)S(1)}, f32[15,16,16]{2,1,0:T(8,128)S(1)}, f32[15,16,16]{2,1,0:T(8,128)S(1)}, /*index=5*/s32[]{:T(128)}) while((s32[]{:T(128)}, f32[16,16]{1,0:T(8,128)S(1)}, f32[16,16]{1,0:T(8,128)S(1)}, f32[15,16,16]{2,1,0:T(8,128)S(1)}, f32[15,16,16]{2,1,0:T(8,128)S(1)}, ...), condition=%wide.region_37.38_spmd, body=%wide.region_20.37_spmd.sunk | while | flops 462962 | bytes 304585 | solution.py:17
  1069.7 31.1 %subtract_divide_fusion.18 = (f32[1,4096]{1,0:T(1,128)S(1)}, f32[1,4096]{1,0:T(1,128)S(1)}, f32[1,4096]{1,0:T(1,128)S(1)}, f32[1,4096]{1,0:T(1,128)S(1)}, f32[1,...) fusion(f32[2,16,4096]{2,1,0:T(8,128)S(1)} %copy-done.2, ...), kind=kLoop, calls=%fused_computation.707 | loop fusion | flops 643072 | bytes 426180 | tf_op jit(solution)/shard_map/div | solution.py:191
  1100.8 143.6 %subtract_divide_fusion.1 = (f32[1,4096]{1,0:T(1,128)S(1)}, f32[1,4096]{1,0:T(1,128)S(1)}, f32[1,4096]{1,0:T(1,128)S(1)}, f32[1,4096]{1,0:T(1,128)S(1)}, f32[1,4...) fusion(f32[1,4096]{1,0:T(1,128)S(1)} %get-tuple-element.182, ...), kind=kLoop, calls=%fused_computation.690 | loop fusion | flops 3170304 | bytes 803696 | tf_op jit(solution)/shard_map/div | solution.py:190
  1244.9 19.7 %subtract_divide_fusion = f32[1,4096]{1,0:T(1,128)S(1)} fusion(f32[1,4096]{1,0:T(1,128)S(1)} %get-tuple-element.165, f32[1,4096]{1,0:T(1,128)S(1)} %get-tuple-element.166, f32[1,4096]{1,0:T(1,128)S(1)} %get-tuple-element.167, f32[1,4096]{1,0:T(1,128)S(1)} %get-tuple-element.168, f32[1,4096]{1,0:T(1,128)S(1)} %get-tuple-element.169, ...), kind=kLoop, calls=%fused_computation.689 | loop fusion | flops 249856 | bytes 524412 | tf_op jit(solution)/shard_map/div | solution.py:191
  (2521 shorter events, 570.4 us)
Async XLA Ops:
  7.2 5.4 copy-start.14
  7.2 73.3 %all-gather.4.cloned.1.call-start = ((), (), s32[]{:S(2)}) async-start(), calls=%async_computation.3 | async-start | bytes 4456448 | tf_op jit(solution)/shard_map/all_gather | solution.py:214
  61.3 5.8 copy-start.13
  61.3 10.2 all-to-all-start
  67.0 324.5 %reduce-scatter.2.cloned.1.call-start = ((), (), s32[]{:S(2)}) async-start(), calls=%async_computation.4 | async-start | bytes 8912896 | tf_op jit(solution)/shard_map/reduce_scatter | solution.py:257
  80.4 3.3 copy-start.3
  83.7 1.9 copy-start
  85.6 1.0 copy-start.5
  85.6 1.3 copy-start.7
  108.4 1.6 copy-start.9
  110.0 1.4 copy-start.12
  132.8 1.6 copy-start.10
  135.8 1.4 copy-start.6
  135.8 1.5 copy-start.8
  137.3 2.2 copy-start.1
  137.3 2.5 copy-start.4
  161.8 13.9 %all-to-all-start.1 = ((bf16[2,8,2,256,256]{4,3,2,1,0:T(8,128)(2,1)}), bf16[2,8,2,256,256]{4,3,2,1,0:T(8,128)(2,1)}, u32[]{:S(2)}, u32[]{:S(2)}) async-start(bf16[2,8,2,256,256]{4,3,2,1,0:T(8,128)(2,1)} %broadcast_multiply_fusion), calls=%async_computation.1 | async-start | bytes 8388608 | tf_op jit(solution)/shard_map/all_to_all | solution.py:232
  167.4 8.4 copy-start.15
  167.5 8.4 copy-start.16
  175.8 214.7 %copy-start.11 = (f32[2,320,384]{2,1,0:T(8,128)S(1)}, f32[2,320,384]{2,1,0:T(8,128)}, u32[]{:S(2)}) copy-start(f32[2,320,384]{2,1,0:T(8,128)} %param.12) | copy-start | bytes 2949124
  391.5 8.0 copy-start.2
Sparse Core Ops, SparseCore 0:
  10.8 53.4 all-gather.3
  157.6 109.5 reduce-scatter.1
where the time goes:
time: 1290 us; the launch traced here: 1270 us
  other arithmetic  524 us (41%)
  local copies, waits for them, and re-layouts  237 us (18%)
  loops' own time  233 us (18%)
  matrix products  197 us (15%)
  blocking collectives  39.8 us (3%)
  between operations  26.6 us (2%)
    reduce_sum x256, other arithmetic, orthogonal_factor(): col_norm = jnp.sqrt(jnp.sum(col_real * col_real + col_imag * col_imag))  175 us
    another operation x1, loops' own time, joined(): lax.scan(lambda running, piece: (join(running, piece), None), head, tail)  171 us
    div x1, other arithmetic, solve_rows(): solved_real.append(acc_real / fac_real[pivot, pivot])  144 us
    dynamic_update_slice x16, local copies, waits for them, and re-layouts, add_back(): lax.dynamic_update_slice(grad_accum, old_block + grad_piece, (zero_index,...  114 us
    another operation x1, loops' own time, local(): lax.fori_loop(0, tile_count * slot_cap, add_back, jnp.zeros(object_field....  62.9 us
    div x2, other arithmetic, solve_rows(): solved_imag.append(acc_imag / fac_real[pivot, pivot])  50.8 us
    gather x48, local copies, waits for them, and re-layouts  44.1 us
    div x255, other arithmetic, orthogonal_factor(): unit_imag = col_imag / col_norm  43.9 us
  transfers between devices with their start and end apart: 4, of which 1 were waited for; matrix products, arithmetic and copies ran while one was open for 18% of the time, Pallas kernels for 0%

commit v1 on v0

v1 whole, which is shorter than its diff:
```python
import math

import jax
import jax.numpy as jnp
import numpy as np
from jax import lax
from jax.experimental import pallas as pl
from jax.experimental.pallas import tpu as pltpu
from jax.sharding import PartitionSpec as P

OBJ_STEP = 0.125
PROBE_STEP = 0.5
RB = 16
f32 = jnp.float32
bf16 = jnp.bfloat16
HI = lax.Precision.HIGHEST


def transform_tables(length):
    ids = np.arange(length)
    angles = (ids[:, None] * ids[None, :] % length) * (2.0 * math.pi / length)
    cos_tab = np.cos(angles) / math.sqrt(length)
    sin_tab = np.sin(angles) / math.sqrt(length)
    forward = np.block([[cos_tab, sin_tab], [-sin_tab, cos_tab]])
    inverse = np.block([[cos_tab, -sin_tab], [sin_tab, cos_tab]])
    return jnp.asarray(forward, dtype=bf16), jnp.asarray(inverse, dtype=bf16)


def iota(shape, dim):
    return lax.broadcasted_iota(jnp.int32, shape, dim)


def widen_kernel(tab_ref, out_ref):
    rows, cols = tab_ref.shape[1:]
    tall, wide = out_ref.shape[1:]
    up = (iota((tall, rows), 0) // RB == iota((tall, rows), 1)).astype(bf16)
    across = (iota((cols, wide), 1) // RB == iota((cols, wide), 0)).astype(bf16)
    same = iota((tall, wide), 0) % RB == iota((tall, wide), 1) % RB
    for at in range(tab_ref.shape[0]):
        left = jnp.dot(up, tab_ref[at], preferred_element_type=f32).astype(bf16)
        full = jnp.dot(left, across, preferred_element_type=f32)
        out_ref[at] = jnp.where(same, full, 0.0).astype(bf16)


def widen(tables):
    count, rows, cols = tables.shape
    return pl.pallas_call(
        widen_kernel,
        out_shape=jax.ShapeDtypeStruct((count, rows * RB, cols * RB), bf16),
        compiler_params=pltpu.CompilerParams(vmem_limit_bytes=32 << 20),
        cost_estimate=pl.CostEstimate(flops=1 << 28, bytes_accessed=1 << 20, transcendentals=0),
        name="widen",
    )(tables)


def cut_kernel(sel_ref, row_ref, col_ref, obj_ref, out_ref):
    spot = pl.program_id(0)
    length = out_ref.shape[2]
    height, width = obj_ref.shape[2:]
    row_at, col_at, sel = row_ref[spot], col_ref[spot], sel_ref[spot]
    rows = (iota((length, height), 1) == iota((length, height), 0) + row_at).astype(bf16)
    cols = (iota((width, length), 0) == iota((width, length), 1) + col_at).astype(bf16)
    for part in range(2):
        band = jnp.dot(rows, obj_ref[sel, part], preferred_element_type=f32).astype(bf16)
        out_ref[0, part] = jnp.dot(band, cols, preferred_element_type=f32).astype(bf16)


def cut_patches(obj_pair, sel, row_at, col_at, length):
    cap = sel.shape[0]
    grid_spec = pltpu.PrefetchScalarGridSpec(
        num_scalar_prefetch=3,
        grid=(cap,),
        in_specs=[pl.BlockSpec(obj_pair.shape, lambda i, *_: (0, 0, 0, 0))],
        out_specs=pl.BlockSpec((1, 2, length, length), lambda i, *_: (i, 0, 0, 0)),
    )
    return pl.pallas_call(
        cut_kernel,
        grid_spec=grid_spec,
        out_shape=jax.ShapeDtypeStruct((cap, 2, length, length), bf16),
        compiler_params=pltpu.CompilerParams(vmem_limit_bytes=32 << 20),
        cost_estimate=pl.CostEstimate(flops=4 << 30, bytes_accessed=4 << 20, transcendentals=0),
        name="cut_patches",
    )(sel, row_at, col_at, obj_pair)


def relax_kernel(tab_ref, meta_ref, mix_ref, *refs):
    blocks = refs[:-8]
    patch_ref, amp_ref, fwd_ref, inv_ref, upd0_ref, upd1_ref, grad_ref, probe_ref = refs[-8:]
    spot = pl.program_id(0)
    length = patch_ref.shape[2]
    half = len(blocks) // 2

    @pl.when(spot == 0)
    def _():
        mix = mix_ref[0]
        for j, block_ref in enumerate(blocks):
            block = block_ref[...].reshape(block_ref.shape[0] * RB, length)
            mixed = jnp.dot(mix, block, preferred_element_type=f32)
            side = meta_ref[1] if j < half else 1 - meta_ref[1]
            at = pl.multiple_of((2 * tab_ref[j] + side) * RB, RB)
            probe_ref[:, pl.ds(at, RB), :] = mixed.reshape(mixed.shape[0] // RB, RB, length)

    live = (spot < meta_ref[0]).astype(f32)
    probe_r, probe_i = probe_ref[2 * spot], probe_ref[2 * spot + 1]
    obj_r, obj_i = patch_ref[0, 0].astype(f32), patch_ref[0, 1].astype(f32)
    exit_r = (probe_r * obj_r - probe_i * obj_i).astype(bf16)
    exit_i = (probe_r * obj_i + probe_i * obj_r).astype(bf16)
    stacked = jnp.concatenate([exit_r, exit_i], axis=0)
    section = jnp.dot(fwd_ref[...], stacked, preferred_element_type=f32).astype(bf16)
    section = jnp.concatenate([section[:length], section[length:]], axis=1)
    far = jnp.dot(section, inv_ref[...], preferred_element_type=f32)
    far_r, far_i = far[:, :length], far[:, length:]
    scale = amp_ref[0].astype(f32) * lax.rsqrt(far_r * far_r + far_i * far_i + 1.0)
    revised = jnp.concatenate([(far_r * scale).astype(bf16), (far_i * scale).astype(bf16)], axis=0)
    back = jnp.dot(inv_ref[...], revised, preferred_element_type=f32).astype(bf16)
    back = jnp.concatenate([back[:length], back[length:]], axis=1)
    near = jnp.dot(back, fwd_ref[...], preferred_element_type=f32)
    delta_r = near[:, :length] - exit_r.astype(f32)
    delta_i = near[:, length:] - exit_i.astype(f32)
    grad_ref[0, 0] = ((probe_r * delta_r + probe_i * delta_i) * live).astype(bf16)
    grad_ref[0, 1] = ((probe_r * delta_i - probe_i * delta_r) * live).astype(bf16)
    change_r = obj_r * delta_r + obj_i * delta_i
    change_i = obj_r * delta_i - obj_i * delta_r
    new_r = ((probe_r + PROBE_STEP * change_r) * live).astype(bf16)
    new_i = ((probe_i + PROBE_STEP * change_i) * live).astype(bf16)
    flip = meta_ref[1] > 0
    for part, value in ((0, new_r), (1, new_i)):
        rows = value.reshape(half, 2, RB, length)
        even, odd = rows[:, 0], rows[:, 1]
        upd0_ref[:, part] = jnp.where(flip, odd, even)
        upd1_ref[:, part] = jnp.where(flip, even, odd)


def whole(arr):
    return pl.BlockSpec(arr.shape, lambda *_: (0,) * arr.ndim)


def relax(tab, meta, mix, blocks, patches, amplitude, forward, inverse):
    cap, _, length, _ = patches.shape
    half = len(blocks) // 2
    plane = pl.BlockSpec((1, 2, length, length), lambda i, *_: (i, 0, 0, 0))
    strip = pl.BlockSpec((half, 2, RB, length), lambda i, *_: (0, i, 0, 0))
    grid_spec = pltpu.PrefetchScalarGridSpec(
        num_scalar_prefetch=2,
        grid=(cap,),
        in_specs=[
            whole(mix), *[whole(block) for block in blocks], plane,
            pl.BlockSpec((1, length, length), lambda i, *_: (i, 0, 0)),
            whole(forward), whole(inverse),
        ],
        out_specs=[strip, strip, plane],
        scratch_shapes=[pltpu.VMEM((2 * cap, length, length), f32)],
    )
    strips = jax.ShapeDtypeStruct((half, 2 * cap, RB, length), bf16)
    return pl.pallas_call(
        relax_kernel,
        grid_spec=grid_spec,
        out_shape=[strips, strips, jax.ShapeDtypeStruct((cap, 2, length, length), bf16)],
        compiler_params=pltpu.CompilerParams(vmem_limit_bytes=48 << 20),
        cost_estimate=pl.CostEstimate(flops=8 << 30, bytes_accessed=16 << 20, transcendentals=1 << 19),
        name="relax_positions",
    )(tab, meta, mix, *blocks, patches, amplitude, forward, inverse)


def settle_kernel(sel_ref, row_ref, col_ref, grad_ref, mine_ref, other_ref):
    spot = pl.program_id(0)
    length = grad_ref.shape[2]
    height, width = mine_ref.shape[1:]
    row_at, col_at, sel = row_ref[spot], col_ref[spot], sel_ref[spot]

    @pl.when(spot == 0)
    def _():
        mine_ref[...] = jnp.zeros_like(mine_ref)
        other_ref[...] = jnp.zeros_like(other_ref)

    cols = (iota((length, width), 1) == iota((length, width), 0) + col_at).astype(bf16)
    rows = (iota((height, length), 0) == iota((height, length), 1) + row_at).astype(bf16)

    def put(ref):
        for part in range(2):
            band = jnp.dot(grad_ref[0, part], cols, preferred_element_type=f32).astype(bf16)
            ref[part] += jnp.dot(rows, band, preferred_element_type=f32)

    @pl.when(sel == 0)
    def _():
        put(mine_ref)

    @pl.when(sel != 0)
    def _():
        put(other_ref)


def settle(sel, row_at, col_at, grads, height, width):
    cap, _, length, _ = grads.shape
    tile = pl.BlockSpec((2, height, width), lambda i, *_: (0, 0, 0))
    grid_spec = pltpu.PrefetchScalarGridSpec(
        num_scalar_prefetch=3,
        grid=(cap,),
        in_specs=[pl.BlockSpec((1, 2, length, length), lambda i, *_: (i, 0, 0, 0))],
        out_specs=[tile, tile],
    )
    shape = jax.ShapeDtypeStruct((2, height, width), f32)
    return pl.pallas_call(
        settle_kernel,
        grid_spec=grid_spec,
        out_shape=[shape, shape],
        compiler_params=pltpu.CompilerParams(vmem_limit_bytes=48 << 20),
        cost_estimate=pl.CostEstimate(flops=4 << 30, bytes_accessed=4 << 20, transcendentals=0),
        name="settle",
    )(sel, row_at, col_at, grads)


def weights_kernel(tab_ref, upd0_ref, upd1_ref, *refs):
    blocks, nw_ref = refs[:-1], refs[-1]
    half = len(blocks) // 2
    lanes = upd0_ref.shape[3]
    tall = upd0_ref.shape[1] * RB
    wide = blocks[0].shape[0] * RB
    table = jnp.zeros((tall, wide), f32)
    for j, block_ref in enumerate(blocks):
        side = upd0_ref if j < half else upd1_ref
        mine = side[tab_ref[j]].reshape(tall, lanes)
        table += lax.dot_general(mine, block_ref[...].reshape(wide, lanes),
                                 (((1,), (1,)), ((), ())), preferred_element_type=f32)
    same = (iota((tall, wide), 0) % RB) == (iota((tall, wide), 1) % RB)
    table = jnp.where(same, table, 0.0)
    slots, modes = tall // (2 * RB), wide // (2 * RB)

    def mul(left, right):
        return jnp.dot(left, right, precision=HI, preferred_element_type=f32)

    def gather_rows(which):
        pick = iota((slots, tall), 1) // RB == 2 * iota((slots, tall), 0) + which
        return mul(pick.astype(f32), table)

    def pick_cols(which):
        pick = iota((wide, modes), 0) // RB == which * modes + iota((wide, modes), 1)
        return pick.astype(f32)

    low, high = gather_rows(0), gather_rows(1)
    cols_r, cols_i = pick_cols(0), pick_cols(1)
    norm = 1.0 / (2 * half * RB * lanes)
    nw_ref[0] = (mul(low, cols_r) + mul(high, cols_i)) * norm
    nw_ref[1] = (mul(high, cols_r) - mul(low, cols_i)) * norm


def new_weights_of(tab, upd0, upd1, blocks):
    grid_spec = pltpu.PrefetchScalarGridSpec(
        num_scalar_prefetch=1,
        grid=(1,),
        in_specs=[whole(upd0), whole(upd1), *[whole(block) for block in blocks]],
        out_specs=pl.BlockSpec((2, upd0.shape[1] // 2, blocks[0].shape[0] // 2), lambda *_: (0, 0, 0)),
    )
    return pl.pallas_call(
        weights_kernel,
        grid_spec=grid_spec,
        out_shape=jax.ShapeDtypeStruct((2, upd0.shape[1] // 2, blocks[0].shape[0] // 2), f32),
        compiler_params=pltpu.CompilerParams(vmem_limit_bytes=48 << 20),
        cost_estimate=pl.CostEstimate(flops=2 << 30, bytes_accessed=6 << 20, transcendentals=0),
        name="new_weights",
    )(tab, upd0, upd1, *blocks)


def sums_kernel(at_ref, wide_ref, near_ref, twin_ref, far_ref, out_ref):
    lanes = near_ref.shape[-1]

    def flat(value):
        return value.reshape(-1, lanes)

    total = jnp.dot(wide_ref[0], flat(near_ref[0]), preferred_element_type=f32)
    total += jnp.dot(wide_ref[1], flat(twin_ref[0]), preferred_element_type=f32)
    total += jnp.dot(wide_ref[2], flat(far_ref[0]), preferred_element_type=f32)
    total += jnp.dot(wide_ref[3], flat(far_ref[1]), preferred_element_type=f32)
    out_ref[...] = total.reshape(out_ref.shape).astype(out_ref.dtype)


def pair_sums(at, wide, near, twin, far, kind):
    lanes = near.shape[-1]
    strip = pl.BlockSpec((1,) + near.shape[1:], lambda i, at: (at[0], 0, 0, 0))
    tall = wide.shape[1] // RB
    grid_spec = pltpu.PrefetchScalarGridSpec(
        num_scalar_prefetch=1,
        grid=(1,),
        in_specs=[whole(wide), strip, strip, whole(far)],
        out_specs=pl.BlockSpec((tall, RB, lanes), lambda *_: (0, 0, 0)),
    )
    return pl.pallas_call(
        sums_kernel,
        grid_spec=grid_spec,
        out_shape=jax.ShapeDtypeStruct((tall, RB, lanes), kind),
        compiler_params=pltpu.CompilerParams(vmem_limit_bytes=16 << 20),
        cost_estimate=pl.CostEstimate(flops=1 << 29, bytes_accessed=2 << 20, transcendentals=0),
        name="mode_sums",
    )(at.reshape(1), wide, near, twin, far)


def finish_kernel(*refs):
    own_ref, others = refs[0], refs[1:-3]
    sum_ref, gram_ref, acc_ref = refs[-3:]
    lanes = own_ref.shape[-1]
    total = own_ref[...]
    for other in others:
        total = total + other[...].astype(f32)
    acc_ref[...] = total
    for row in range(RB):
        sum_ref[:, row * lanes:(row + 1) * lanes] = acc_ref[:, row, :]
    modes = sum_ref.shape[0] // 2
    flat = sum_ref[...]
    full = lax.dot_general(flat, flat, (((1,), (1,)), ((), ())), precision=HI,
                           preferred_element_type=f32)
    gram_ref[0] = full[:modes, :modes] + full[modes:, modes:]
    gram_ref[1] = full[modes:, :modes] - full[:modes, modes:]


def finish_sums(own, others):
    tall, _, lanes = own.shape
    return pl.pallas_call(
        finish_kernel,
        out_shape=[
            jax.ShapeDtypeStruct((tall, RB * lanes), f32),
            jax.ShapeDtypeStruct((2, tall // 2, tall // 2), f32),
        ],
        scratch_shapes=[pltpu.VMEM((tall, RB, lanes), f32)],
        compiler_params=pltpu.CompilerParams(vmem_limit_bytes=16 << 20),
        cost_estimate=pl.CostEstimate(flops=1 << 28, bytes_accessed=2 << 20, transcendentals=0),
        name="finish_sums",
    )(own, *others)


def modes_kernel(norm, gram_ref, sum_ref, out_ref):
    count = gram_ref.shape[1]
    gram_r, gram_i = gram_ref[0], gram_ref[1]
    eye = (iota((count, count), 0) == iota((count, count), 1)).astype(f32)
    zero = jnp.zeros((count, count), f32)
    work = jnp.concatenate([gram_r, gram_i, eye, zero], axis=1)
    turned = jnp.concatenate([-gram_i, gram_r, zero, eye], axis=1)
    row_ids = iota((count, 1), 0)
    roots = jnp.zeros((count, 1), f32)
    for pivot in range(count):
        lead = work[pivot:pivot + 1, pivot:pivot + 1]
        roots = jnp.where(row_ids == pivot, lead, roots)
        if pivot + 1 < count:
            below = jnp.where(row_ids > pivot, 1.0 / lead, 0.0)
            coef_r = work[:, pivot:pivot + 1] * below
            coef_i = work[:, count + pivot:count + pivot + 1] * below
            row, row_t = work[pivot:pivot + 1], turned[pivot:pivot + 1]
            work = work - (coef_r * row + coef_i * row_t)
            turned = turned - (coef_r * row_t - coef_i * row)
    back = work[:, 2 * count:] * (norm * lax.rsqrt(roots))
    back_r, back_i = back[:, :count], back[:, count:]
    full = jnp.concatenate([
        jnp.concatenate([back_r, -back_i], axis=1),
        jnp.concatenate([back_i, back_r], axis=1)], axis=0)
    out_ref[...] = jnp.dot(full, sum_ref[...], precision=HI, preferred_element_type=f32)


def new_modes_of(gram, summed, norm):
    def kernel(gram_ref, sum_ref, out_ref):
        modes_kernel(norm, gram_ref, sum_ref, out_ref)

    return pl.pallas_call(
        kernel,
        out_shape=jax.ShapeDtypeStruct(summed.shape, f32),
        compiler_params=pltpu.CompilerParams(vmem_limit_bytes=32 << 20),
        cost_estimate=pl.CostEstimate(flops=1 << 27, bytes_accessed=1 << 20, transcendentals=256),
        name="orthonormal_modes",
    )(gram, summed)


def swap_tiles(value):
    count = lax.axis_size("tile")
    return lax.ppermute(value, "tile", [(i, (i + 1) % count) for i in range(count)])


def turn(value, step):
    count = lax.axis_size("scan")
    return lax.ppermute(value, "scan", [(i, (i + 2 * step) % count) for i in range(count)])


def across(value):
    count = lax.axis_size("scan")
    return lax.ppermute(value, "scan", [(i, i ^ 1) for i in range(count)])


def gather_blocks(own):
    scan = lax.axis_index("scan")
    z, y = scan // 2, scan % 2
    come = {step: turn(own, step) for step in (2, 1, 3)}
    row = [own] + [come[step] for step in (2, 1, 3)]
    side = [across(value) for value in row]
    mine = row + side
    other = [swap_tiles(value) for value in mine]
    order = jnp.stack([z, (z + 2) % 4, (z + 3) % 4, (z + 1) % 4])
    tab = jnp.concatenate([2 * order + y, 2 * order + 1 - y])
    return mine + other, jnp.concatenate([tab, tab])


def gather_any(own):
    rows = own.shape[1]
    every = lax.all_gather(own, ("scan", "tile"))
    every = every.reshape((-1, RB // rows) + own.shape).transpose(0, 2, 1, 3, 4)
    every = every.reshape(-1, own.shape[0], RB, own.shape[2])
    half = every.shape[0] // 2
    tab = jnp.arange(half, dtype=jnp.int32)
    return [every[i] for i in (*range(0, 2 * half, 2), *range(1, 2 * half, 2))], jnp.concatenate([tab, tab])


def gather_mixing(weights_b):
    wt_r, wt_i = jnp.swapaxes(weights_b[0], 0, 1), jnp.swapaxes(weights_b[1], 0, 1)
    real_rows = jnp.stack([wt_r, wt_i], axis=2)
    imag_rows = jnp.stack([-wt_i, wt_r], axis=2)
    count, cap = wt_r.shape
    return jnp.stack([real_rows, imag_rows], axis=0).reshape(2 * count, 2 * cap)


def scatter_sums(weights_b, upd0, upd1):
    scan = lax.axis_index("scan")
    z, y = scan // 2, scan % 2
    pair = jnp.stack([weights_b, swap_tiles(weights_b)])
    quad = jnp.concatenate([pair, across(pair)])
    wide = widen(jax.vmap(gather_mixing)(quad))
    twin = swap_tiles(upd1)
    far = {}
    for step in (2, 1, 3, 0):
        at = 2 * ((z + step) % 4) + 1 - y
        far[step] = across(jnp.stack([
            lax.dynamic_index_in_dim(upd0, at, 0, keepdims=False),
            lax.dynamic_index_in_dim(twin, at, 0, keepdims=False)]))
    come = []
    for step in (2, 1, 3):
        part = pair_sums(2 * ((z + step) % 4) + y, wide, upd0, twin, far[step], bf16)
        come.append(turn(part, step))
    own = pair_sums(2 * z + y, wide, upd0, twin, far[0], f32)
    return finish_sums(own, come)


def scatter_any(weights_b, upd0, upd1):
    devices = lax.axis_size("scan") * lax.axis_size("tile")
    half, slots, _, length = upd0.shape
    every = lax.all_gather(weights_b, ("scan", "tile"))
    rows = 2 * half * RB // devices
    parts = jnp.stack([upd0, upd1], axis=1).reshape(2 * half, slots, RB // rows, rows, length)
    parts = parts.transpose(0, 2, 1, 3, 4).reshape(devices, slots, rows, length)
    arrived = lax.all_to_all(parts, ("scan", "tile"), split_axis=0, concat_axis=0, tiled=True)
    flat = arrived.reshape(devices, slots // 2, 2, rows * length).astype(f32)
    wt_r, wt_i = every[:, 0].astype(f32), every[:, 1].astype(f32)
    up_r, up_i = flat[:, :, 0], flat[:, :, 1]

    def mul(left, right):
        return jnp.einsum("dpk,dpx->kx", left, right, precision=HI)

    sum_r = mul(wt_r, up_r) + mul(wt_i, up_i)
    sum_i = mul(wt_r, up_i) - mul(wt_i, up_r)

    def pair(left, right):
        return jnp.dot(left, right.T, precision=HI)

    gram = jnp.stack([pair(sum_r, sum_r) + pair(sum_i, sum_i),
                      pair(sum_i, sum_r) - pair(sum_r, sum_i)])
    return jnp.concatenate([sum_r, sum_i]), gram


def sum_everywhere(value):
    value = value + swap_tiles(value)
    count = lax.axis_size("scan")
    step = 1
    while step < count:
        value = value + lax.ppermute(value, "scan", [(i, i ^ step) for i in range(count)])
        step *= 2
    return value


def local(
    object_field, probe_modes, weights, amplitude, slot_count, tile_owner, corner_row, corner_col
):
    n_tile = lax.axis_size("tile")
    devices = lax.axis_size("scan") * n_tile
    tile = lax.axis_index("tile")
    cap, length, _ = amplitude.shape
    count = probe_modes.shape[1]
    pixels = length * length
    rows = length // devices
    forward, inverse = transform_tables(length)

    def mine(value):
        return lax.dynamic_slice_in_dim(value, tile * cap, cap)

    owner, row_at, col_at = mine(tile_owner), mine(corner_row), mine(corner_col)
    sel = jnp.where(owner == tile, 0, 1).astype(jnp.int32)
    live_n = lax.dynamic_index_in_dim(slot_count, tile, 0, keepdims=False)

    own = probe_modes.astype(bf16).reshape(2 * count, rows, length)
    obj_b = object_field.astype(bf16)
    obj_pair = jnp.stack([obj_b, swap_tiles(obj_b)])
    weights_b = weights.astype(bf16)
    planned = lax.axis_size("scan") == 8 and n_tile == 2 and rows == RB
    blocks, tab = gather_blocks(own) if planned else gather_any(own)
    patches = cut_patches(obj_pair, sel, row_at, col_at, length)

    wt_r, wt_i = weights_b[0], weights_b[1]
    mix = jnp.stack([jnp.concatenate([wt_r, -wt_i], axis=1),
                     jnp.concatenate([wt_i, wt_r], axis=1)], axis=1)
    mix = widen(mix.reshape(1, 2 * cap, 2 * count))
    meta = jnp.stack([live_n, tile if planned else jnp.zeros_like(tile)])
    upd0, upd1, grads = relax(tab, meta, mix, blocks, patches, amplitude, forward, inverse)

    summed, gram = (scatter_sums if planned else scatter_any)(weights_b, upd0, upd1)
    mine_sum, other_sum = settle(sel, row_at, col_at, grads, *object_field.shape[1:])
    new_object = object_field + OBJ_STEP * (mine_sum + swap_tiles(other_sum))
    new_weights = new_weights_of(tab, upd0, upd1, blocks)
    gram = sum_everywhere(gram)
    new_modes = new_modes_of(gram, summed, math.sqrt(pixels)).reshape(probe_modes.shape)
    return (new_object, new_modes, new_weights)


def solution(mesh):
    in_specs = (
        P(None, ("groups", "scan", "tile"), None),
        P(None, "groups", ("scan", "tile")),
        P(None, ("groups", "scan", "tile"), None),
        P(("groups", "scan", "tile"), None, None),
        P(("groups", "scan")),
        P(("groups", "scan")),
        P(("groups", "scan")),
        P(("groups", "scan")),
    )
    out_specs = (
        P(None, ("groups", "scan", "tile"), None),
        P(None, "groups", ("scan", "tile")),
        P(None, ("groups", "scan", "tile"), None),
    )
    return jax.shard_map(local, mesh=mesh, in_specs=in_specs, out_specs=out_specs, check_vma=False)
```

time: 1290 us -> 142 us (0.11); the launches traced: 1270 us -> 141 us
  other arithmetic: 524 us -> 11.9 us
  loops' own time: 233 us -> 0 us
  local copies, waits for them, and re-layouts: 237 us -> 5.47 us
  matrix products: 197 us -> 0 us
  Pallas kernels: 0 us -> 48.8 us
  waiting for transfers between devices: 4.25 us -> 44.9 us
  blocking collectives: 39.8 us -> 0 us
  between operations: 26.6 us -> 1.43 us
  starting transfers between devices: 11.5 us -> 28.9 us
    div x499 -> x0, other arithmetic: 279 us -> none  [the longest x1 144 us: solve_rows(): solved_real.append(acc_real / fac_real[pivot, pivot])]
    another operation x3 -> x0, loops' own time: 233 us -> none  [the longest x1 171 us: joined(): lax.scan(lambda running, piece: (join(running, piece), None), head, tail)]
    dot_general x1037 -> x0, matrix products: 197 us -> none  [the longest x256 41.6 us: orthogonal_factor(): jnp.dot(unit_imag, work_imag, precision=best_precision)]
    reduce_sum x257 -> x0, other arithmetic: 180 us -> none  [the longest x256 175 us: orthogonal_factor(): col_norm = jnp.sqrt(jnp.sum(col_real * col_real + col_imag * col_imag))]
    dynamic_update_slice x16 -> x0, local copies, waits for them, and re-layouts: 114 us -> none  [add_back(): lax.dynamic_update_slice(grad_accum, old_block + grad_piece, (zero_index,...]
    pallas_call x0 -> x12, Pallas kernels: none -> 48.8 us  [the longest x1 16.1 us: relax(): pl.pallas_call(relax_kernel, grid_spec=grid_spec, out_shape=[strips, stri...]
    ppermute x0 -> x31, waiting for transfers between devices: none -> 44.9 us  [the longest x9 23.7 us: across(): return lax.ppermute(value, 'scan', [(i, i ^ 1) for i in range(count)])]
    gather x48 -> x0, local copies, waits for them, and re-layouts: 44.1 us -> none
  transfers between devices with their start and end apart: 4 -> 31, of which waited for: 1 -> 13; matrix products, arithmetic and copies ran while one was open for 18% -> 9% of each run, Pallas kernels for 0% -> 20%
where the time goes in v1:
time: 142 us; the launch traced here: 141 us
  Pallas kernels  48.8 us (34%)
  waiting for transfers between devices  44.9 us (32%)
  starting transfers between devices  28.9 us (20%)
  other arithmetic  11.9 us (8%)
  local copies, waits for them, and re-layouts  5.47 us (4%)
  between operations  1.43 us (1%)
    ppermute x9, waiting for transfers between devices, across(): return lax.ppermute(value, 'scan', [(i, i ^ 1) for i in range(count)])  23.7 us
    ppermute x6, waiting for transfers between devices, turn(): lax.ppermute(value, 'scan', [(i, (i + 2 * step) % count) for i in range(c...  16.4 us
    pallas_call x1, Pallas kernels, relax(): pl.pallas_call(relax_kernel, grid_spec=grid_spec, out_shape=[strips, stri...  16.1 us
    ppermute x6, starting transfers between devices, turn(): lax.ppermute(value, 'scan', [(i, (i + 2 * step) % count) for i in range(c...  11.7 us
    ppermute x9, starting transfers between devices, across(): return lax.ppermute(value, 'scan', [(i, i ^ 1) for i in range(count)])  11 us
    pallas_call x1, Pallas kernels, settle(): pl.pallas_call(settle_kernel, grid_spec=grid_spec, out_shape=[shape, shap...  8.3 us
    pallas_call x4, Pallas kernels, pair_sums(): pl.pallas_call(sums_kernel, grid_spec=grid_spec, out_shape=jax.ShapeDtype...  6.87 us
    pallas_call x1, Pallas kernels, cut_patches(): pl.pallas_call(cut_kernel, grid_spec=grid_spec, out_shape=jax.ShapeDtypeS...  6.1 us
  transfers between devices with their start and end apart: 31, of which 13 were waited for; matrix products, arithmetic and copies ran while one was open for 9% of the time, Pallas kernels for 20%

profile of v1, /device:TPU:0, one launch (start us, length us, event | category | flops | bytes accessed | tf_op | source)
XLA Modules:
  0.0 141.4 jit_solution(4220638039089227467)
XLA Ops:
  0.7 1.1 convert_element_type.10
  1.9 4.1 %collective-permute-start = (bf16[32,16,256]{2,1,0:T(8,128)(2,1)S(1)}, bf16[32,16,256]{2,1,0:T(8,128)(2,1)S(1)}, u32[]{:S(2)}, u32[]{:S(2)}) collective-permute-start(bf16[32,16,256]{2,1,0:T(8,128)(2,1)S(1)} %bitcast.57), channel_id=1, source_target_pairs={{0,8},{2,10},{4,12},{6,14},{8,0},{10,2},{12,4},{14,6},{1,9},{3,11}... | collective-permute-start | bytes 786440 | tf_op jit(solution)/shard_map/ppermute | solution.py:377
  6.0 1.6 %collective-permute-start.1 = (bf16[32,16,256]{2,1,0:T(8,128)(2,1)S(1)}, bf16[32,16,256]{2,1,0:T(8,128)(2,1)S(1)}, u32[]{:S(2)}, u32[]{:S(2)}) collective-permute-start(bf16[32,16,256]{2,1,0:T(8,128)(2,1)S(1)} %bitcast.58), channel_id=1, source_target_pairs={{0,4},{2,6},{4,8},{6,10},{8,12},{10,14},{12,0},{14,2},{1,5},{3,7},... | collective-permute-start | bytes 786440 | tf_op jit(solution)/shard_map/ppermute | solution.py:377
  7.6 2.2 %collective-permute-start.2 = (bf16[32,16,256]{2,1,0:T(8,128)(2,1)S(1)}, bf16[32,16,256]{2,1,0:T(8,128)(2,1)S(1)}, u32[]{:S(2)}, u32[]{:S(2)}) collective-permute-start(bf16[32,16,256]{2,1,0:T(8,128)(2,1)S(1)} %bitcast.59), channel_id=1, source_target_pairs={{0,12},{2,14},{4,0},{6,2},{8,4},{10,6},{12,8},{14,10},{1,13},{3,15... | collective-permute-start | bytes 786440 | tf_op jit(solution)/shard_map/ppermute | solution.py:377
  9.8 1.3 convert_element_type.11
  12.0 1.1 collective-permute-done.17
  13.0 1.5 %collective-permute-start.18 = (bf16[2,2,8,16]{3,2,1,0:T(8,128)(2,1)S(1)}, bf16[2,2,8,16]{3,2,1,0:T(8,128)(2,1)S(1)}, u32[]{:S(2)}, u32[]{:S(2)}) collective-permute-start(bf16[2,2,8,16]{3,2,1,0:T(8,128)(2,1)S(1)} %pad_maximum_fusion.6), channel_id=1, source_target_pairs={{0,2},{2,0},{4,6},{6,4},{8,10},{10,8},{12,14},{14,12},{1,3},{3,1},... | collective-permute-start | bytes 3080 | tf_op jit(solution)/shard_map/ppermute | solution.py:382
  15.2 1.5 %collective-permute-done.18 = bf16[2,2,8,16]{3,2,1,0:T(8,128)(2,1)S(1)} collective-permute-done((bf16[2,2,8,16]{3,2,1,0:T(8,128)(2,1)S(1)}, bf16[2,2,8,16]{3,2,1,0:T(8,128)(2,1)S(1)}, u32[]{:S(2)}, u32[]{:S(2)}) %collective-permute-start.18) | collective-permute-done | bytes 1056 | tf_op jit(solution)/shard_map/ppermute | solution.py:382
  16.7 1.5 %collective-permute-start.3 = (bf16[32,16,256]{2,1,0:T(8,128)(2,1)S(1)}, bf16[32,16,256]{2,1,0:T(8,128)(2,1)S(1)}, u32[]{:S(2)}, u32[]{:S(2)}) collective-permute-start(bf16[32,16,256]{2,1,0:T(8,128)(2,1)S(1)} %bitcast.60), channel_id=1, source_target_pairs={{0,2},{2,0},{4,6},{6,4},{8,10},{10,8},{12,14},{14,12},{1,3},{3,1},... | collective-permute-start | bytes 786440 | tf_op jit(solution)/shard_map/ppermute | solution.py:382
  18.2 6.2 %collective-permute-done.refs_1_ = bf16[32,16,256]{2,1,0:T(8,128)(2,1)S(1)} collective-permute-done((bf16[32,16,256]{2,1,0:T(8,128)(2,1)S(1)}, bf16[32,16,256]{2,1,0:T(8,128)(2,1)S(1)}, u32[]{:S(2)}, u32[]{:S(2)}) %collective-permute-start) | collective-permute-done | bytes 262176 | tf_op jit(solution)/shard_map/ppermute | solution.py:377
  24.4 0.7 pad_add_fusion.1.meta_ref
  25.2 0.8 convert_bitcast_fusion.1
  26.0 1.9 %collective-permute-start.6 = (bf16[32,16,256]{2,1,0:T(8,128)(2,1)S(1)}, bf16[32,16,256]{2,1,0:T(8,128)(2,1)S(1)}, u32[]{:S(2)}, u32[]{:S(2)}) collective-permute-start(bf16[32,16,256]{2,1,0:T(8,128)(2,1)S(1)} %collective-permute-done.2.refs_3_), channel_id=1, source_target_pairs={{0,2},{2,0},{4,6},{6,4},{8,10},{10,8},{12,14},{14,12},{1,3},{3,1},... | collective-permute-start | bytes 786440 | tf_op jit(solution)/shard_map/ppermute | solution.py:382
  28.5 1.7 %collective-permute-start.5 = (bf16[32,16,256]{2,1,0:T(8,128)(2,1)S(1)}, bf16[32,16,256]{2,1,0:T(8,128)(2,1)S(1)}, u32[]{:S(2)}, u32[]{:S(2)}) collective-permute-start(bf16[32,16,256]{2,1,0:T(8,128)(2,1)S(1)} %collective-permute-done.1.refs_2_), channel_id=1, source_target_pairs={{0,2},{2,0},{4,6},{6,4},{8,10},{10,8},{12,14},{14,12},{1,3},{3,1},... | collective-permute-start | bytes 786440 | tf_op jit(solution)/shard_map/ppermute | solution.py:382
  30.8 1.3 pad_maximum_fusion.obj_ref
  32.1 8.7 %collective-permute-done.4.refs_5_ = bf16[32,16,256]{2,1,0:T(8,128)(2,1)S(1)} collective-permute-done((bf16[32,16,256]{2,1,0:T(8,128)(2,1)S(1)}, bf16[32,16,256]{2,1,0:T(8,128)(2,1)S(1)}, u32[]{:S(2)}, u32[]{:S(2)}) %collective-permute-start.4) | collective-permute-done | bytes 262176 | tf_op jit(solution)/shard_map/ppermute | solution.py:382
  40.8 5.3 %collective-permute-done.5.refs_6_ = bf16[32,16,256]{2,1,0:T(8,128)(2,1)S(1)} collective-permute-done((bf16[32,16,256]{2,1,0:T(8,128)(2,1)S(1)}, bf16[32,16,256]{2,1,0:T(8,128)(2,1)S(1)}, u32[]{:S(2)}, u32[]{:S(2)}) %collective-permute-start.5) | collective-permute-done | bytes 262176 | tf_op jit(solution)/shard_map/ppermute | solution.py:382
  47.1 6.1 %cut_patches.1.refs_16_ = bf16[8,2,256,256]{3,2,1,0:T(8,128)(2,1)S(1)} custom-call(s32[8]{0:T(128)S(1)} %compare_select_fusion.sel_ref, s32[8]{0:T(128)S(1)} %dynamic_slice.39.row_ref, s32[8]{0:T(128)S(1)} %dynamic_slice.40.col_ref, bf16[2,2,320,384]{3,2,1,0:T(8,128)(2,1)S(1)} %pad_maximum_fusion.obj_ref), custom_call_target="tpu_custom_call" | custom-call | flops 4294967296 | bytes 4194304 | tf_op jit(solution)/shard_map/cut_patches/pallas_call | solution.py:76
  53.2 1.3 copy-done.37
  54.7 16.1 %relax_positions.1 = (bf16[8,16,16,256]{3,2,1,0:T(8,128)(2,1)}, bf16[8,16,16,256]{3,2,1,0:T(8,128)(2,1)}, bf16[8,2,256,256]{3,2,1,0:T(8,128)(2,1)}) custom-call(s32[16]{0:T(128)S(1)} %pad_add_fusion.tab_ref, s32[2]{0:T(128)S(1)} %pad_add_fusion.1.meta_ref, bf16[1,256,512]{2,1,0:T(8,128)(2,1)S(1)} %widen.2.mix_ref, bf16[32,16,256]{2,1,0:T(8,128)(2,1)S(1)} %bitcast.62, ...), custom_call_target="tpu_custom_call" | custom-call | flops 8589934592 | bytes 16777216 | tf_op jit(solution)/shard_map/relax_positions/pallas_call | solution.py:155
  71.1 1.6 %copy-done.38 = bf16[8,2,256,256]{3,2,1,0:T(8,128)(2,1)S(1)} copy-done((bf16[8,2,256,256]{3,2,1,0:T(8,128)(2,1)S(1)}, bf16[8,2,256,256]{3,2,1,0:T(8,128)(2,1)}, u32[]{:S(2)}) %copy-start.38) | copy-done | bytes 2097176
  72.7 8.3 %settle.1 = (f32[2,320,384]{2,1,0:T(8,128)S(1)}, f32[2,320,384]{2,1,0:T(8,128)}) custom-call(s32[8]{0:T(128)S(1)} %compare_select_fusion.sel_ref, s32[8]{0:T(128)S(1)} %dynamic_slice.39.row_ref, s32[8]{0:T(128)S(1)} %dynamic_slice.40.col_ref, bf16[8,2,256,256]{3,2,1,0:T(8,128)(2,1)S(1)} %copy-done.38), custom_call_target="tpu_custom_call" | custom-call | flops 4294967296 | bytes 4194304 | tf_op jit(solution)/shard_map/settle/pallas_call | solution.py:203
  82.8 0.7 pad_maximum_fusion.4
  83.6 1.7 %collective-permute-start.25 = (bf16[2,16,16,256]{3,2,1,0:T(8,128)(2,1)}, bf16[2,16,16,256]{3,2,1,0:T(8,128)(2,1)S(1)}, u32[]{:S(2)}, u32[]{:S(2)}) collective-permute-start(bf16[2,16,16,256]{3,2,1,0:T(8,128)(2,1)} %pad_maximum_fusion.4), channel_id=1, source_target_pairs={{0,2},{2,0},{4,6},{6,4},{8,10},{10,8},{12,14},{14,12},{1,3},{3,1},... | collective-permute-start | bytes 786440 | tf_op jit(solution)/shard_map/ppermute | solution.py:382
  85.3 0.7 pad_maximum_fusion.3
  86.3 0.7 pad_maximum_fusion.2
  87.0 1.7 %collective-permute-start.21 = (bf16[2,16,16,256]{3,2,1,0:T(8,128)(2,1)}, bf16[2,16,16,256]{3,2,1,0:T(8,128)(2,1)}, u32[]{:S(2)}, u32[]{:S(2)}) collective-permute-start(bf16[2,16,16,256]{3,2,1,0:T(8,128)(2,1)} %pad_maximum_fusion.2), channel_id=1, source_target_pairs={{0,2},{2,0},{4,6},{6,4},{8,10},{10,8},{12,14},{14,12},{1,3},{3,1},... | collective-permute-start | bytes 786440 | tf_op jit(solution)/shard_map/ppermute | solution.py:382
  89.0 0.8 widen.3.wide_ref
  89.8 1.7 %pad_maximum_fusion.1 = bf16[2,16,16,256]{3,2,1,0:T(8,128)(2,1)} fusion(bf16[1,16,16,256]{3,2,1,0:T(8,128)(2,1)} %get-tuple-element.26, bf16[1,16,16,256]{3,2,1,0:T(8,128)(2,1)} %get-tuple-element.22), kind=kLoop, calls=%fused_computation.2 | loop fusion | flops 131072 | bytes 524288 | tf_op jit(solution)/shard_map/stack | solution.py:426
  91.8 1.1 collective-permute-done.25.far_ref
  92.9 1.1 mode_sums.7
  94.0 4.6 %collective-permute-done.23.far_ref = bf16[2,16,16,256]{3,2,1,0:T(8,128)(2,1)} collective-permute-done((bf16[2,16,16,256]{3,2,1,0:T(8,128)(2,1)}, bf16[2,16,16,256]{3,2,1,0:T(8,128)(2,1)}, u32[]{:S(2)}, u32[]{:S(2)}) %collective-permute-start.23) | collective-permute-done | bytes 262176 | tf_op jit(solution)/shard_map/ppermute | solution.py:382
  98.6 2.1 %mode_sums.6 = bf16[32,16,256]{2,1,0:T(8,128)(2,1)} custom-call(s32[1]{0:T(128)} %bitcast.29.at_ref, bf16[4,512,256]{2,1,0:T(8,128)(2,1)S(1)} %widen.3.wide_ref, bf16[8,16,16,256]{3,2,1,0:T(8,128)(2,1)S(1)} %copy-done, bf16[8,16,16,256]{3,2,1,0:T(8,128)(2,1)S(1)} %collective-permute-done.19.twin_ref, bf16[2,16,16,256]{3,2,1,0:T(8,128)(2,1)} %collective-permute-done.23.far_ref), custom_call_target="tpu_custom_call" | custom-call | flops 536870912 | bytes 2097152 | tf_op jit(solution)/shard_map/mode_sums/pallas_call | solution.py:287
  100.7 2.4 %collective-permute-start.24 = (bf16[32,16,256]{2,1,0:T(8,128)(2,1)}, bf16[32,16,256]{2,1,0:T(8,128)(2,1)}, u32[]{:S(2)}, u32[]{:S(2)}) collective-permute-start(bf16[32,16,256]{2,1,0:T(8,128)(2,1)} %mode_sums.6), channel_id=1, source_target_pairs={{0,4},{2,6},{4,8},{6,10},{8,12},{10,14},{12,0},{14,2},{1,5},{3,7},... | collective-permute-start | bytes 786440 | tf_op jit(solution)/shard_map/ppermute | solution.py:377
  103.1 1.1 collective-permute-done.21.far_ref
  104.2 2.1 %mode_sums.5 = bf16[32,16,256]{2,1,0:T(8,128)(2,1)} custom-call(s32[1]{0:T(128)} %bitcast.28.at_ref, bf16[4,512,256]{2,1,0:T(8,128)(2,1)S(1)} %widen.3.wide_ref, bf16[8,16,16,256]{3,2,1,0:T(8,128)(2,1)S(1)} %copy-done, bf16[8,16,16,256]{3,2,1,0:T(8,128)(2,1)S(1)} %collective-permute-done.19.twin_ref, bf16[2,16,16,256]{3,2,1,0:T(8,128)(2,1)} %collective-permute-done.21.far_ref), custom_call_target="tpu_custom_call" | custom-call | flops 536870912 | bytes 2097152 | tf_op jit(solution)/shard_map/mode_sums/pallas_call | solution.py:287
  106.3 1.4 collective-permute-start.22
  107.7 1.5 %collective-permute-done.20.far_ref = bf16[2,16,16,256]{3,2,1,0:T(8,128)(2,1)} collective-permute-done((bf16[2,16,16,256]{3,2,1,0:T(8,128)(2,1)}, bf16[2,16,16,256]{3,2,1,0:T(8,128)(2,1)}, u32[]{:S(2)}, u32[]{:S(2)}) %collective-permute-start.20) | collective-permute-done | bytes 262176 | tf_op jit(solution)/shard_map/ppermute | solution.py:382
  109.4 1.5 %mode_sums.4.refs_0_ = f32[32,16,256]{2,1,0:T(8,128)S(1)} custom-call(s32[1]{0:T(128)} %bitcast.12.at_ref, bf16[4,512,256]{2,1,0:T(8,128)(2,1)S(1)} %widen.3.wide_ref, bf16[8,16,16,256]{3,2,1,0:T(8,128)(2,1)S(1)} %copy-done, bf16[8,16,16,256]{3,2,1,0:T(8,128)(2,1)S(1)} %collective-permute-done.19.twin_ref, ...), custom_call_target="tpu_custom_call" | custom-call | flops 536870912 | bytes 2097152 | tf_op jit(solution)/shard_map/mode_sums/pallas_call | solution.py:287
  110.9 10.2 %collective-permute-done.22.refs_1_ = bf16[32,16,256]{2,1,0:T(8,128)(2,1)} collective-permute-done((bf16[32,16,256]{2,1,0:T(8,128)(2,1)}, bf16[32,16,256]{2,1,0:T(8,128)(2,1)}, u32[]{:S(2)}, u32[]{:S(2)}) %collective-permute-start.22) | collective-permute-done | bytes 262176 | tf_op jit(solution)/shard_map/ppermute | solution.py:377
  121.1 1.9 %finish_sums.1 = (f32[32,4096]{1,0:T(8,128)S(1)}, f32[2,16,16]{2,1,0:T(8,128)S(1)}) custom-call(f32[32,16,256]{2,1,0:T(8,128)S(1)} %mode_sums.4.refs_0_, bf16[32,16,256]{2,1,0:T(8,128)(2,1)} %collective-permute-done.22.refs_1_, bf16[32,16,256]{2,1,0:T(8,128)(2,1)} %collective-permute-done.24.refs_2_, bf16[32,16,256]{2,1,0:T(8,128)(2,1)S(1)} %collective-permute-done.26.refs_3_), custom_call_target="tpu_custom_call" | custom-call | flops 268435456 | bytes 2097152 | tf_op jit(solution)/shard_map/finish_sums/pallas_call | solution.py:317
  123.0 1.2 collective-permute-done.27
  124.2 1.7 %collective-permute-start.28 = (f32[2,16,16]{2,1,0:T(8,128)S(1)}, f32[2,16,16]{2,1,0:T(8,128)S(1)}, u32[]{:S(2)}, u32[]{:S(2)}) collective-permute-start(f32[2,16,16]{2,1,0:T(8,128)S(1)} %add.143), channel_id=1, source_target_pairs={{0,2},{2,0},{4,6},{6,4},{8,10},{10,8},{12,14},{14,12},{1,3},{3,1},... | collective-permute-start | bytes 6152 | tf_op jit(solution)/shard_map/ppermute | solution.py:468
  125.9 2.0 %collective-permute-done.28 = f32[2,16,16]{2,1,0:T(8,128)S(1)} collective-permute-done((f32[2,16,16]{2,1,0:T(8,128)S(1)}, f32[2,16,16]{2,1,0:T(8,128)S(1)}, u32[]{:S(2)}, u32[]{:S(2)}) %collective-permute-start.28) | collective-permute-done | bytes 2080 | tf_op jit(solution)/shard_map/ppermute | solution.py:468
  128.2 4.7 %new_weights.1 = f32[2,8,16]{2,1,0:T(8,128)} custom-call(s32[16]{0:T(128)S(1)} %pad_add_fusion.tab_ref, bf16[8,16,16,256]{3,2,1,0:T(8,128)(2,1)S(1)} %copy-done, bf16[8,16,16,256]{3,2,1,0:T(8,128)(2,1)} %get-tuple-element.14.upd1_ref, bf16[32,16,256]{2,1,0:T(8,128)(2,1)S(1)} %bitcast.63, bf16[32,16,256]{2,1,0:T(8,128)(2,1)S(1)} %copy-done.6, ...), custom_call_target="tpu_custom_call" | custom-call | flops 2147483648 | bytes 6291456 | tf_op jit(solution)/shard_map/new_weights/pallas_call | solution.py:254
  132.8 1.9 %collective-permute-start.30 = (f32[2,16,16]{2,1,0:T(8,128)S(1)}, f32[2,16,16]{2,1,0:T(8,128)S(1)}, u32[]{:S(2)}, u32[]{:S(2)}) collective-permute-start(f32[2,16,16]{2,1,0:T(8,128)S(1)} %add.145), channel_id=1, source_target_pairs={{0,8},{2,10},{4,12},{6,14},{8,0},{10,2},{12,4},{14,6},{1,9},{3,11}... | collective-permute-start | bytes 6152 | tf_op jit(solution)/shard_map/ppermute | solution.py:468
  134.7 2.4 %multiply_add_fusion = f32[2,320,384]{2,1,0:T(8,128)} fusion(f32[2,320,384]{2,1,0:T(8,128)S(1)} %copy-done.40, f32[2,320,384]{2,1,0:T(8,128)S(1)} %copy-done.2, f32[2,320,384]{2,1,0:T(8,128)} %collective-permute-done.16), kind=kLoop, calls=%fused_computation.1 | loop fusion | flops 737280 | bytes 3932160 | tf_op jit(solution)/shard_map/add | solution.py:509
  137.6 3.8 %orthonormal_modes.1 = f32[32,4096]{1,0:T(8,128)} custom-call(f32[2,16,16]{2,1,0:T(8,128)S(1)} %add.146.gram_ref, f32[32,4096]{1,0:T(8,128)S(1)} %get-tuple-element.16.sum_ref), custom_call_target="tpu_custom_call" | custom-call | flops 134217728 | bytes 1048576 | tf_op jit(solution)/shard_map/orthonormal_modes/pallas_call | solution.py:361
  (158 shorter events, 7.3 us)
Async XLA Ops:
  0.6 24.5 %copy-start.39 = (f32[2,320,384]{2,1,0:T(8,128)S(1)}, f32[2,320,384]{2,1,0:T(8,128)}, u32[]{:S(2)}) copy-start(f32[2,320,384]{2,1,0:T(8,128)} %param.10) | copy-start | bytes 2949124
  1.9 52.7 %copy-start.3 = (bf16[4,8,16,256]{3,2,1,0:T(8,128)(2,1)}, bf16[4,8,16,256]{3,2,1,0:T(8,128)(2,1)S(1)}, u32[]{:S(2)}) copy-start(bf16[4,8,16,256]{3,2,1,0:T(8,128)(2,1)S(1)} %copy.21) | copy-start | bytes 786436
  1.9 28.7 %copy-start.44 = (s32[16]{0:T(128)S(1)}, s32[16]{0:T(128)}, u32[]{:S(2)}) copy-start(s32[16]{0:T(128)} %param.16) | copy-start | bytes 196
  1.9 28.8 %copy-start.45 = (s32[16]{0:T(128)S(1)}, s32[16]{0:T(128)}, u32[]{:S(2)}) copy-start(s32[16]{0:T(128)} %param.17) | copy-start | bytes 196
  1.9 22.5 %collective-permute-start = (bf16[32,16,256]{2,1,0:T(8,128)(2,1)S(1)}, bf16[32,16,256]{2,1,0:T(8,128)(2,1)S(1)}, u32[]{:S(2)}, u32[]{:S(2)}) collective-permute-start(bf16[32,16,256]{2,1,0:T(8,128)(2,1)S(1)} %bitcast.57), channel_id=1, source_target_pairs={{0,8},{2,10},{4,12},{6,14},{8,0},{10,2},{12,4},{14,6},{1,9},{3,11}... | collective-permute-start | bytes 786440 | tf_op jit(solution)/shard_map/ppermute | solution.py:377
  6.0 21.9 %collective-permute-start.1 = (bf16[32,16,256]{2,1,0:T(8,128)(2,1)S(1)}, bf16[32,16,256]{2,1,0:T(8,128)(2,1)S(1)}, u32[]{:S(2)}, u32[]{:S(2)}) collective-permute-start(bf16[32,16,256]{2,1,0:T(8,128)(2,1)S(1)} %bitcast.58), channel_id=1, source_target_pairs={{0,4},{2,6},{4,8},{6,10},{8,12},{10,14},{12,0},{14,2},{1,5},{3,7},... | collective-permute-start | bytes 786440 | tf_op jit(solution)/shard_map/ppermute | solution.py:377
  7.6 18.4 %collective-permute-start.2 = (bf16[32,16,256]{2,1,0:T(8,128)(2,1)S(1)}, bf16[32,16,256]{2,1,0:T(8,128)(2,1)S(1)}, u32[]{:S(2)}, u32[]{:S(2)}) collective-permute-start(bf16[32,16,256]{2,1,0:T(8,128)(2,1)S(1)} %bitcast.59), channel_id=1, source_target_pairs={{0,12},{2,14},{4,0},{6,2},{8,4},{10,6},{12,8},{14,10},{1,13},{3,15... | collective-permute-start | bytes 786440 | tf_op jit(solution)/shard_map/ppermute | solution.py:377
  11.1 17.4 %collective-permute-start.15 = (bf16[2,320,384]{2,1,0:T(8,128)(2,1)S(1)}, bf16[2,320,384]{2,1,0:T(8,128)(2,1)}, u32[]{:S(2)}, u32[]{:S(2)}) collective-permute-start(bf16[2,320,384]{2,1,0:T(8,128)(2,1)S(1)} %convert_element_type.11), channel_id=1, source_target_pairs={{0,1},{1,0},{2,3},{3,2},{4,5},{5,4},{6,7},{7,6},{8,9},{9,8},{10,11... | collective-permute-start | bytes 1474568 | tf_op jit(solution)/shard_map/ppermute | solution.py:372
  11.2 1.8 %collective-permute-start.17 = (bf16[2,8,16]{2,1,0:T(8,128)(2,1)S(1)}, bf16[2,8,16]{2,1,0:T(8,128)(2,1)S(1)}, u32[]{:S(2)}, u32[]{:S(2)}) collective-permute-start(bf16[2,8,16]{2,1,0:T(8,128)(2,1)S(1)} %convert_element_type.9), channel_id=1, source_target_pairs={{0,1},{1,0},{2,3},{3,2},{4,5},{5,4},{6,7},{7,6},{8,9},{9,8},{10,11... | collective-permute-start | bytes 1544 | tf_op jit(solution)/shard_map/ppermute | solution.py:372
  13.0 3.7 %collective-permute-start.18 = (bf16[2,2,8,16]{3,2,1,0:T(8,128)(2,1)S(1)}, bf16[2,2,8,16]{3,2,1,0:T(8,128)(2,1)S(1)}, u32[]{:S(2)}, u32[]{:S(2)}) collective-permute-start(bf16[2,2,8,16]{3,2,1,0:T(8,128)(2,1)S(1)} %pad_maximum_fusion.6), channel_id=1, source_target_pairs={{0,2},{2,0},{4,6},{6,4},{8,10},{10,8},{12,14},{14,12},{1,3},{3,1},... | collective-permute-start | bytes 3080 | tf_op jit(solution)/shard_map/ppermute | solution.py:382
  16.7 11.4 %collective-permute-start.3 = (bf16[32,16,256]{2,1,0:T(8,128)(2,1)S(1)}, bf16[32,16,256]{2,1,0:T(8,128)(2,1)S(1)}, u32[]{:S(2)}, u32[]{:S(2)}) collective-permute-start(bf16[32,16,256]{2,1,0:T(8,128)(2,1)S(1)} %bitcast.60), channel_id=1, source_target_pairs={{0,2},{2,0},{4,6},{6,4},{8,10},{10,8},{12,14},{14,12},{1,3},{3,1},... | collective-permute-start | bytes 786440 | tf_op jit(solution)/shard_map/ppermute | solution.py:382
  24.4 30.2 %copy-start.5 = (bf16[32,16,256]{2,1,0:T(8,128)(2,1)}, bf16[32,16,256]{2,1,0:T(8,128)(2,1)S(1)}, u32[]{:S(2)}) copy-start(bf16[32,16,256]{2,1,0:T(8,128)(2,1)S(1)} %collective-permute-done.refs_1_) | copy-start | bytes 786436
  24.4 4.0 %collective-permute-start.7 = (bf16[32,16,256]{2,1,0:T(8,128)(2,1)S(1)}, bf16[32,16,256]{2,1,0:T(8,128)(2,1)S(1)}, u32[]{:S(2)}, u32[]{:S(2)}) collective-permute-start(bf16[32,16,256]{2,1,0:T(8,128)(2,1)S(1)} %bitcast.61), channel_id=1, source_target_pairs={{0,1},{1,0},{2,3},{3,2},{4,5},{5,4},{6,7},{7,6},{8,9},{9,8},{10,11... | collective-permute-start | bytes 786440 | tf_op jit(solution)/shard_map/ppermute | solution.py:372
  26.0 28.6 %copy-start.9 = (bf16[32,16,256]{2,1,0:T(8,128)(2,1)}, bf16[32,16,256]{2,1,0:T(8,128)(2,1)S(1)}, u32[]{:S(2)}) copy-start(bf16[32,16,256]{2,1,0:T(8,128)(2,1)S(1)} %collective-permute-done.2.refs_3_) | copy-start | bytes 786436
  26.0 20.1 %collective-permute-start.6 = (bf16[32,16,256]{2,1,0:T(8,128)(2,1)S(1)}, bf16[32,16,256]{2,1,0:T(8,128)(2,1)S(1)}, u32[]{:S(2)}, u32[]{:S(2)}) collective-permute-start(bf16[32,16,256]{2,1,0:T(8,128)(2,1)S(1)} %collective-permute-done.2.refs_3_), channel_id=1, source_target_pairs={{0,2},{2,0},{4,6},{6,4},{8,10},{10,8},{12,14},{14,12},{1,3},{3,1},... | collective-permute-start | bytes 786440 | tf_op jit(solution)/shard_map/ppermute | solution.py:382
  27.9 26.8 %copy-start.7 = (bf16[32,16,256]{2,1,0:T(8,128)(2,1)}, bf16[32,16,256]{2,1,0:T(8,128)(2,1)S(1)}, u32[]{:S(2)}) copy-start(bf16[32,16,256]{2,1,0:T(8,128)(2,1)S(1)} %collective-permute-done.1.refs_2_) | copy-start | bytes 786436
  27.9 18.7 %collective-permute-start.10 = (bf16[32,16,256]{2,1,0:T(8,128)(2,1)S(1)}, bf16[32,16,256]{2,1,0:T(8,128)(2,1)S(1)}, u32[]{:S(2)}, u32[]{:S(2)}) collective-permute-start(bf16[32,16,256]{2,1,0:T(8,128)(2,1)S(1)} %collective-permute-done.2.refs_3_), channel_id=1, source_target_pairs={{0,1},{1,0},{2,3},{3,2},{4,5},{5,4},{6,7},{7,6},{8,9},{9,8},{10,11... | collective-permute-start | bytes 786440 | tf_op jit(solution)/shard_map/ppermute | solution.py:372
  28.1 26.5 %copy-start.11 = (bf16[32,16,256]{2,1,0:T(8,128)(2,1)}, bf16[32,16,256]{2,1,0:T(8,128)(2,1)S(1)}, u32[]{:S(2)}) copy-start(bf16[32,16,256]{2,1,0:T(8,128)(2,1)S(1)} %collective-permute-done.3.refs_4_) | copy-start | bytes 786436
  28.1 12.7 %collective-permute-start.4 = (bf16[32,16,256]{2,1,0:T(8,128)(2,1)S(1)}, bf16[32,16,256]{2,1,0:T(8,128)(2,1)S(1)}, u32[]{:S(2)}, u32[]{:S(2)}) collective-permute-start(bf16[32,16,256]{2,1,0:T(8,128)(2,1)S(1)} %collective-permute-done.refs_1_), channel_id=1, source_target_pairs={{0,2},{2,0},{4,6},{6,4},{8,10},{10,8},{12,14},{14,12},{1,3},{3,1},... | collective-permute-start | bytes 786440 | tf_op jit(solution)/shard_map/ppermute | solution.py:382
  28.5 26.2 %copy-start.13 = (bf16[32,16,256]{2,1,0:T(8,128)(2,1)}, bf16[32,16,256]{2,1,0:T(8,128)(2,1)S(1)}, u32[]{:S(2)}) copy-start(bf16[32,16,256]{2,1,0:T(8,128)(2,1)S(1)} %collective-permute-done.7.refs_8_) | copy-start | bytes 786436
  28.5 18.2 %collective-permute-start.8 = (bf16[32,16,256]{2,1,0:T(8,128)(2,1)S(1)}, bf16[32,16,256]{2,1,0:T(8,128)(2,1)S(1)}, u32[]{:S(2)}, u32[]{:S(2)}) collective-permute-start(bf16[32,16,256]{2,1,0:T(8,128)(2,1)S(1)} %collective-permute-done.refs_1_), channel_id=1, source_target_pairs={{0,1},{1,0},{2,3},{3,2},{4,5},{5,4},{6,7},{7,6},{8,9},{9,8},{10,11... | collective-permute-start | bytes 786440 | tf_op jit(solution)/shard_map/ppermute | solution.py:372
  28.5 17.6 %collective-permute-start.5 = (bf16[32,16,256]{2,1,0:T(8,128)(2,1)S(1)}, bf16[32,16,256]{2,1,0:T(8,128)(2,1)S(1)}, u32[]{:S(2)}, u32[]{:S(2)}) collective-permute-start(bf16[32,16,256]{2,1,0:T(8,128)(2,1)S(1)} %collective-permute-done.1.refs_2_), channel_id=1, source_target_pairs={{0,2},{2,0},{4,6},{6,4},{8,10},{10,8},{12,14},{14,12},{1,3},{3,1},... | collective-permute-start | bytes 786440 | tf_op jit(solution)/shard_map/ppermute | solution.py:382
  32.1 22.6 %copy-start.35 = (bf16[512,512]{1,0:T(8,128)(2,1)S(1)}, bf16[512,512]{1,0:T(8,128)(2,1)}, u32[]{:S(2)}) copy-start(bf16[512,512]{1,0:T(8,128)(2,1)} %constant.107.clone.refs_18_) | copy-start | bytes 1572868
  32.1 22.6 %copy-start.36 = (bf16[512,512]{1,0:T(8,128)(2,1)S(1)}, bf16[512,512]{1,0:T(8,128)(2,1)}, u32[]{:S(2)}) copy-start(bf16[512,512]{1,0:T(8,128)(2,1)} %constant.108.clone.refs_19_) | copy-start | bytes 1572868
  40.8 13.7 %collective-permute-start.9 = (bf16[32,16,256]{2,1,0:T(8,128)(2,1)S(1)}, bf16[32,16,256]{2,1,0:T(8,128)(2,1)S(1)}, u32[]{:S(2)}, u32[]{:S(2)}) collective-permute-start(bf16[32,16,256]{2,1,0:T(8,128)(2,1)S(1)} %collective-permute-done.1.refs_2_), channel_id=1, source_target_pairs={{0,1},{1,0},{2,3},{3,2},{4,5},{5,4},{6,7},{7,6},{8,9},{9,8},{10,11... | collective-permute-start | bytes 786440 | tf_op jit(solution)/shard_map/ppermute | solution.py:372
  46.1 8.5 %collective-permute-start.11 = (bf16[32,16,256]{2,1,0:T(8,128)(2,1)S(1)}, bf16[32,16,256]{2,1,0:T(8,128)(2,1)S(1)}, u32[]{:S(2)}, u32[]{:S(2)}) collective-permute-start(bf16[32,16,256]{2,1,0:T(8,128)(2,1)S(1)} %collective-permute-done.3.refs_4_), channel_id=1, source_target_pairs={{0,1},{1,0},{2,3},{3,2},{4,5},{5,4},{6,7},{7,6},{8,9},{9,8},{10,11... | collective-permute-start | bytes 786440 | tf_op jit(solution)/shard_map/ppermute | solution.py:372
  46.1 8.5 %collective-permute-start.12 = (bf16[32,16,256]{2,1,0:T(8,128)(2,1)S(1)}, bf16[32,16,256]{2,1,0:T(8,128)(2,1)S(1)}, u32[]{:S(2)}, u32[]{:S(2)}) collective-permute-start(bf16[32,16,256]{2,1,0:T(8,128)(2,1)S(1)} %collective-permute-done.4.refs_5_), channel_id=1, source_target_pairs={{0,1},{1,0},{2,3},{3,2},{4,5},{5,4},{6,7},{7,6},{8,9},{9,8},{10,11... | collective-permute-start | bytes 786440 | tf_op jit(solution)/shard_map/ppermute | solution.py:372
  46.6 8.0 %collective-permute-start.13 = (bf16[32,16,256]{2,1,0:T(8,128)(2,1)S(1)}, bf16[32,16,256]{2,1,0:T(8,128)(2,1)S(1)}, u32[]{:S(2)}, u32[]{:S(2)}) collective-permute-start(bf16[32,16,256]{2,1,0:T(8,128)(2,1)S(1)} %collective-permute-done.5.refs_6_), channel_id=1, source_target_pairs={{0,1},{1,0},{2,3},{3,2},{4,5},{5,4},{6,7},{7,6},{8,9},{9,8},{10,11... | collective-permute-start | bytes 786440 | tf_op jit(solution)/shard_map/ppermute | solution.py:372
  46.7 7.9 %collective-permute-start.14 = (bf16[32,16,256]{2,1,0:T(8,128)(2,1)S(1)}, bf16[32,16,256]{2,1,0:T(8,128)(2,1)S(1)}, u32[]{:S(2)}, u32[]{:S(2)}) collective-permute-start(bf16[32,16,256]{2,1,0:T(8,128)(2,1)S(1)} %collective-permute-done.6.refs_7_), channel_id=1, source_target_pairs={{0,1},{1,0},{2,3},{3,2},{4,5},{5,4},{6,7},{7,6},{8,9},{9,8},{10,11... | collective-permute-start | bytes 786440 | tf_op jit(solution)/shard_map/ppermute | solution.py:372
  70.9 11.2 %collective-permute-start.19 = (bf16[8,16,16,256]{3,2,1,0:T(8,128)(2,1)}, bf16[8,16,16,256]{3,2,1,0:T(8,128)(2,1)S(1)}, u32[]{:S(2)}, u32[]{:S(2)}) collective-permute-start(bf16[8,16,16,256]{3,2,1,0:T(8,128)(2,1)} %get-tuple-element.14.upd1_ref), channel_id=1, source_target_pairs={{0,1},{1,0},{2,3},{3,2},{4,5},{5,4},{6,7},{7,6},{8,9},{9,8},{10,11... | collective-permute-start | bytes 3145736 | tf_op jit(solution)/shard_map/ppermute | solution.py:372
  81.0 53.7 %collective-permute-start.16 = (f32[2,320,384]{2,1,0:T(8,128)}, f32[2,320,384]{2,1,0:T(8,128)}, u32[]{:S(2)}, u32[]{:S(2)}) collective-permute-start(f32[2,320,384]{2,1,0:T(8,128)} %get-tuple-element.12), channel_id=1, source_target_pairs={{0,1},{1,0},{2,3},{3,2},{4,5},{5,4},{6,7},{7,6},{8,9},{9,8},{10,11... | collective-permute-start | bytes 2949128 | tf_op jit(solution)/shard_map/ppermute | solution.py:372
  83.6 9.3 %collective-permute-start.25 = (bf16[2,16,16,256]{3,2,1,0:T(8,128)(2,1)}, bf16[2,16,16,256]{3,2,1,0:T(8,128)(2,1)S(1)}, u32[]{:S(2)}, u32[]{:S(2)}) collective-permute-start(bf16[2,16,16,256]{3,2,1,0:T(8,128)(2,1)} %pad_maximum_fusion.4), channel_id=1, source_target_pairs={{0,2},{2,0},{4,6},{6,4},{8,10},{10,8},{12,14},{14,12},{1,3},{3,1},... | collective-permute-start | bytes 786440 | tf_op jit(solution)/shard_map/ppermute | solution.py:382
  86.0 12.6 %collective-permute-start.23 = (bf16[2,16,16,256]{3,2,1,0:T(8,128)(2,1)}, bf16[2,16,16,256]{3,2,1,0:T(8,128)(2,1)}, u32[]{:S(2)}, u32[]{:S(2)}) collective-permute-start(bf16[2,16,16,256]{3,2,1,0:T(8,128)(2,1)} %pad_maximum_fusion.3), channel_id=1, source_target_pairs={{0,2},{2,0},{4,6},{6,4},{8,10},{10,8},{12,14},{14,12},{1,3},{3,1},... | collective-permute-start | bytes 786440 | tf_op jit(solution)/shard_map/ppermute | solution.py:382
  87.0 17.2 %collective-permute-start.21 = (bf16[2,16,16,256]{3,2,1,0:T(8,128)(2,1)}, bf16[2,16,16,256]{3,2,1,0:T(8,128)(2,1)}, u32[]{:S(2)}, u32[]{:S(2)}) collective-permute-start(bf16[2,16,16,256]{3,2,1,0:T(8,128)(2,1)} %pad_maximum_fusion.2), channel_id=1, source_target_pairs={{0,2},{2,0},{4,6},{6,4},{8,10},{10,8},{12,14},{14,12},{1,3},{3,1},... | collective-permute-start | bytes 786440 | tf_op jit(solution)/shard_map/ppermute | solution.py:382
  91.5 17.7 %collective-permute-start.20 = (bf16[2,16,16,256]{3,2,1,0:T(8,128)(2,1)}, bf16[2,16,16,256]{3,2,1,0:T(8,128)(2,1)}, u32[]{:S(2)}, u32[]{:S(2)}) collective-permute-start(bf16[2,16,16,256]{3,2,1,0:T(8,128)(2,1)} %pad_maximum_fusion.1), channel_id=1, source_target_pairs={{0,2},{2,0},{4,6},{6,4},{8,10},{10,8},{12,14},{14,12},{1,3},{3,1},... | collective-permute-start | bytes 786440 | tf_op jit(solution)/shard_map/ppermute | solution.py:382
  94.0 16.9 %collective-permute-start.26 = (bf16[32,16,256]{2,1,0:T(8,128)(2,1)}, bf16[32,16,256]{2,1,0:T(8,128)(2,1)S(1)}, u32[]{:S(2)}, u32[]{:S(2)}) collective-permute-start(bf16[32,16,256]{2,1,0:T(8,128)(2,1)} %mode_sums.7), channel_id=1, source_target_pairs={{0,12},{2,14},{4,0},{6,2},{8,4},{10,6},{12,8},{14,10},{1,13},{3,15... | collective-permute-start | bytes 786440 | tf_op jit(solution)/shard_map/ppermute | solution.py:377
  100.7 10.2 %collective-permute-start.24 = (bf16[32,16,256]{2,1,0:T(8,128)(2,1)}, bf16[32,16,256]{2,1,0:T(8,128)(2,1)}, u32[]{:S(2)}, u32[]{:S(2)}) collective-permute-start(bf16[32,16,256]{2,1,0:T(8,128)(2,1)} %mode_sums.6), channel_id=1, source_target_pairs={{0,4},{2,6},{4,8},{6,10},{8,12},{10,14},{12,0},{14,2},{1,5},{3,7},... | collective-permute-start | bytes 786440 | tf_op jit(solution)/shard_map/ppermute | solution.py:377
  106.3 14.8 %collective-permute-start.22 = (bf16[32,16,256]{2,1,0:T(8,128)(2,1)}, bf16[32,16,256]{2,1,0:T(8,128)(2,1)}, u32[]{:S(2)}, u32[]{:S(2)}) collective-permute-start(bf16[32,16,256]{2,1,0:T(8,128)(2,1)} %mode_sums.5), channel_id=1, source_target_pairs={{0,8},{2,10},{4,12},{6,14},{8,0},{10,2},{12,4},{14,6},{1,9},{3,11}... | collective-permute-start | bytes 786440 | tf_op jit(solution)/shard_map/ppermute | solution.py:377
  109.2 18.8 %copy-start.12 = (bf16[32,16,256]{2,1,0:T(8,128)(2,1)S(1)}, bf16[32,16,256]{2,1,0:T(8,128)(2,1)}, u32[]{:S(2)}) copy-start(bf16[32,16,256]{2,1,0:T(8,128)(2,1)} %copy-done.11) | copy-start | bytes 786436
  109.2 18.8 %copy-start.14 = (bf16[32,16,256]{2,1,0:T(8,128)(2,1)S(1)}, bf16[32,16,256]{2,1,0:T(8,128)(2,1)}, u32[]{:S(2)}) copy-start(bf16[32,16,256]{2,1,0:T(8,128)(2,1)} %copy-done.13) | copy-start | bytes 786436
  109.3 18.8 %copy-start.16 = (bf16[32,16,256]{2,1,0:T(8,128)(2,1)S(1)}, bf16[32,16,256]{2,1,0:T(8,128)(2,1)}, u32[]{:S(2)}) copy-start(bf16[32,16,256]{2,1,0:T(8,128)(2,1)} %copy-done.15) | copy-start | bytes 786436
  109.3 18.8 %copy-start.18 = (bf16[32,16,256]{2,1,0:T(8,128)(2,1)S(1)}, bf16[32,16,256]{2,1,0:T(8,128)(2,1)}, u32[]{:S(2)}) copy-start(bf16[32,16,256]{2,1,0:T(8,128)(2,1)} %copy-done.17) | copy-start | bytes 786436
  109.3 18.8 %copy-start.20 = (bf16[32,16,256]{2,1,0:T(8,128)(2,1)S(1)}, bf16[32,16,256]{2,1,0:T(8,128)(2,1)}, u32[]{:S(2)}) copy-start(bf16[32,16,256]{2,1,0:T(8,128)(2,1)} %copy-done.19) | copy-start | bytes 786436
  109.3 18.8 %copy-start.22 = (bf16[32,16,256]{2,1,0:T(8,128)(2,1)S(1)}, bf16[32,16,256]{2,1,0:T(8,128)(2,1)}, u32[]{:S(2)}) copy-start(bf16[32,16,256]{2,1,0:T(8,128)(2,1)} %copy-done.21) | copy-start | bytes 786436
  123.0 1.2 collective-permute-start.27
  124.2 3.7 %collective-permute-start.28 = (f32[2,16,16]{2,1,0:T(8,128)S(1)}, f32[2,16,16]{2,1,0:T(8,128)S(1)}, u32[]{:S(2)}, u32[]{:S(2)}) collective-permute-start(f32[2,16,16]{2,1,0:T(8,128)S(1)} %add.143), channel_id=1, source_target_pairs={{0,2},{2,0},{4,6},{6,4},{8,10},{10,8},{12,14},{14,12},{1,3},{3,1},... | collective-permute-start | bytes 6152 | tf_op jit(solution)/shard_map/ppermute | solution.py:468
  127.9 4.9 %collective-permute-start.29 = (f32[2,16,16]{2,1,0:T(8,128)S(1)}, f32[2,16,16]{2,1,0:T(8,128)S(1)}, u32[]{:S(2)}, u32[]{:S(2)}) collective-permute-start(f32[2,16,16]{2,1,0:T(8,128)S(1)} %add.144), channel_id=1, source_target_pairs={{0,4},{2,6},{4,0},{6,2},{8,12},{10,14},{12,8},{14,10},{1,5},{3,7},... | collective-permute-start | bytes 6152 | tf_op jit(solution)/shard_map/ppermute | solution.py:468
  132.8 4.7 %collective-permute-start.30 = (f32[2,16,16]{2,1,0:T(8,128)S(1)}, f32[2,16,16]{2,1,0:T(8,128)S(1)}, u32[]{:S(2)}, u32[]{:S(2)}) collective-permute-start(f32[2,16,16]{2,1,0:T(8,128)S(1)} %add.145), channel_id=1, source_target_pairs={{0,8},{2,10},{4,12},{6,14},{8,0},{10,2},{12,4},{14,6},{1,9},{3,11}... | collective-permute-start | bytes 6152 | tf_op jit(solution)/shard_map/ppermute | solution.py:468
  (29 other events, 381.7 us)

commit v2 on v1

v2 whole, which is shorter than its diff:
```python
import math

import jax
import jax.numpy as jnp
import numpy as np
from jax import lax
from jax.experimental import pallas as pl
from jax.experimental.pallas import tpu as pltpu
from jax.sharding import PartitionSpec as P

OBJ_STEP = 0.125
PROBE_STEP = 0.5
RB = 16
f32 = jnp.float32
bf16 = jnp.bfloat16
HI = lax.Precision.HIGHEST


def transform_tables(length):
    ids = np.arange(length)
    angles = (ids[:, None] * ids[None, :] % length) * (2.0 * math.pi / length)
    cos_tab = np.cos(angles) / math.sqrt(length)
    sin_tab = np.sin(angles) / math.sqrt(length)
    forward = np.block([[cos_tab, sin_tab], [-sin_tab, cos_tab]])
    inverse = np.block([[cos_tab, -sin_tab], [sin_tab, cos_tab]])
    return jnp.asarray(forward, dtype=bf16), jnp.asarray(inverse, dtype=bf16)


def iota(shape, dim):
    return lax.broadcasted_iota(jnp.int32, shape, dim)


def widen_kernel(tab_ref, out_ref):
    rows, cols = tab_ref.shape[1:]
    tall, wide = out_ref.shape[1:]
    up = (iota((tall, rows), 0) // RB == iota((tall, rows), 1)).astype(bf16)
    across = (iota((cols, wide), 1) // RB == iota((cols, wide), 0)).astype(bf16)
    same = iota((tall, wide), 0) % RB == iota((tall, wide), 1) % RB
    for at in range(tab_ref.shape[0]):
        left = jnp.dot(up, tab_ref[at], preferred_element_type=f32).astype(bf16)
        full = jnp.dot(left, across, preferred_element_type=f32)
        out_ref[at] = jnp.where(same, full, 0.0).astype(bf16)


def widen(tables):
    count, rows, cols = tables.shape
    return pl.pallas_call(
        widen_kernel,
        out_shape=jax.ShapeDtypeStruct((count, rows * RB, cols * RB), bf16),
        compiler_params=pltpu.CompilerParams(vmem_limit_bytes=8 << 20),
        cost_estimate=pl.CostEstimate(flops=1 << 28, bytes_accessed=1 << 20, transcendentals=0),
        name="widen",
    )(tables)


def cut_kernel(sel_ref, row_ref, col_ref, obj_ref, out_ref):
    spot = pl.program_id(0)
    length = out_ref.shape[2]
    height, width = obj_ref.shape[2:]
    row_at, col_at, sel = row_ref[spot], col_ref[spot], sel_ref[spot]
    rows = (iota((length, height), 1) == iota((length, height), 0) + row_at).astype(bf16)
    cols = (iota((width, length), 0) == iota((width, length), 1) + col_at).astype(bf16)
    for part in range(2):
        band = jnp.dot(rows, obj_ref[sel, part], preferred_element_type=f32).astype(bf16)
        out_ref[0, part] = jnp.dot(band, cols, preferred_element_type=f32).astype(bf16)


def cut_patches(obj_pair, sel, row_at, col_at, length):
    cap = sel.shape[0]
    grid_spec = pltpu.PrefetchScalarGridSpec(
        num_scalar_prefetch=3,
        grid=(cap,),
        in_specs=[pl.BlockSpec(obj_pair.shape, lambda i, *_: (0, 0, 0, 0))],
        out_specs=pl.BlockSpec((1, 2, length, length), lambda i, *_: (i, 0, 0, 0)),
    )
    return pl.pallas_call(
        cut_kernel,
        grid_spec=grid_spec,
        out_shape=jax.ShapeDtypeStruct((cap, 2, length, length), bf16),
        compiler_params=pltpu.CompilerParams(vmem_limit_bytes=12 << 20),
        cost_estimate=pl.CostEstimate(flops=4 << 30, bytes_accessed=4 << 20, transcendentals=0),
        name="cut_patches",
    )(sel, row_at, col_at, obj_pair)


STEPS = (0, 2, 3, 1)


def relax_kernel(tab_ref, live_ref, mix_ref, *refs):
    count = len(STEPS)
    blocks, refs = refs[:4 * count], refs[4 * count:]
    patch_ref, amp_ref, fwd_ref, inv_ref, keep0_ref, keep1_ref = refs[:6]
    cross0, cross1 = refs[6:6 + count], refs[6 + count:6 + 2 * count]
    grad_ref, stash_ref, probe_ref, new_ref = refs[6 + 2 * count:]
    group = pl.program_id(0)
    each = patch_ref.shape[0]
    length = patch_ref.shape[2]

    @pl.when(group == 0)
    def _():
        mix = mix_ref[0]
        for j, block_ref in enumerate(blocks):
            block = block_ref[...].reshape(block_ref.shape[0] * RB, length)
            mixed = jnp.dot(mix, block, preferred_element_type=f32)
            at = pl.multiple_of(tab_ref[j] * RB, RB)
            probe_ref[:, pl.ds(at, RB), :] = mixed.reshape(mixed.shape[0] // RB, RB, length)

    share = stash_ref.shape[0]
    for turn_at in range(len(blocks) // share):
        @pl.when(group == turn_at)
        def _(turn_at=turn_at):
            for i in range(share):
                stash_ref[i] = blocks[share * turn_at + i][...]

    def planes(q):
        spot = each * group + q
        return (probe_ref[2 * spot], probe_ref[2 * spot + 1],
                patch_ref[q, 0].astype(f32), patch_ref[q, 1].astype(f32))

    def leave(q):
        probe_r, probe_i, obj_r, obj_i = planes(q)
        exit_r = (probe_r * obj_r - probe_i * obj_i).astype(bf16)
        exit_i = (probe_r * obj_i + probe_i * obj_r).astype(bf16)
        return exit_r, exit_i

    def rows_pass(table, pairs):
        both = jnp.concatenate([jnp.concatenate(pair, axis=0) for pair in pairs], axis=1)
        out = jnp.dot(table[...], both, preferred_element_type=f32).astype(bf16)
        return jnp.concatenate([
            jnp.concatenate([out[:length, q * length:(q + 1) * length],
                             out[length:, q * length:(q + 1) * length]], axis=1)
            for q in range(each)], axis=0)

    def cols_pass(table, value):
        out = jnp.dot(value, table[...], preferred_element_type=f32)
        return [out[q * length:(q + 1) * length] for q in range(each)]

    def revise(q, far):
        far_r, far_i = far[:, :length], far[:, length:]
        scale = amp_ref[q].astype(f32) * lax.rsqrt(far_r * far_r + far_i * far_i + 1.0)
        return (far_r * scale).astype(bf16), (far_i * scale).astype(bf16)

    def update(q, exits, near):
        live = (each * group + q < live_ref[0]).astype(f32)
        probe_r, probe_i, obj_r, obj_i = planes(q)
        delta_r = near[:, :length] - exits[0].astype(f32)
        delta_i = near[:, length:] - exits[1].astype(f32)
        grad_ref[q, 0] = ((probe_r * delta_r + probe_i * delta_i) * live).astype(bf16)
        grad_ref[q, 1] = ((probe_r * delta_i - probe_i * delta_r) * live).astype(bf16)
        change_r = obj_r * delta_r + obj_i * delta_i
        change_i = obj_r * delta_i - obj_i * delta_r
        for part, value in ((0, probe_r + PROBE_STEP * change_r), (1, probe_i + PROBE_STEP * change_i)):
            new_ref[2 * q + part] = (value * live).astype(bf16).reshape(4 * count, RB, length)

    exits = [leave(q) for q in range(each)]
    far = cols_pass(inv_ref, rows_pass(fwd_ref, exits))
    revised = [revise(q, far[q]) for q in range(each)]
    near = cols_pass(fwd_ref, rows_pass(inv_ref, revised))
    for q in range(each):
        update(q, exits[q], near[q])
    for j in range(4 * count):
        at = tab_ref[j]
        side, far_side, place = j // (2 * count), j // count % 2, j % count
        for row in range(2 * each):
            if far_side:
                (cross1 if side else cross0)[place][row] = new_ref[row, at]
            else:
                (keep1_ref if side else keep0_ref)[place, row] = new_ref[row, at]


def whole(arr):
    return pl.BlockSpec(arr.shape, lambda *_: (0,) * arr.ndim)


def relax(tab, live, mix, blocks, patches, amplitude, forward, inverse):
    cap, _, length, _ = patches.shape
    count = len(STEPS)
    each = 4 if cap % 4 == 0 else 1
    share = len(blocks) * each // cap
    plane = pl.BlockSpec((each, 2, length, length), lambda i, *_: (i, 0, 0, 0))
    strips = pl.BlockSpec((count, 2 * each, RB, length), lambda i, *_: (0, i, 0, 0))
    strip = pl.BlockSpec((2 * each, RB, length), lambda i, *_: (i, 0, 0))
    grid_spec = pltpu.PrefetchScalarGridSpec(
        num_scalar_prefetch=2,
        grid=(cap // each,),
        in_specs=[
            whole(mix), *[whole(block) for block in blocks], plane,
            pl.BlockSpec((each, length, length), lambda i, *_: (i, 0, 0)),
            whole(forward), whole(inverse),
        ],
        out_specs=[strips, strips, *[strip] * (2 * count), plane,
                   pl.BlockSpec((share,) + blocks[0].shape, lambda i, *_: (i, 0, 0, 0))],
        scratch_shapes=[
            pltpu.VMEM((2 * cap, length, length), f32),
            pltpu.VMEM((2 * each, 4 * count, RB, length), bf16),
        ],
    )
    many = jax.ShapeDtypeStruct((count, 2 * cap, RB, length), bf16)
    single = jax.ShapeDtypeStruct((2 * cap, RB, length), bf16)
    outs = pl.pallas_call(
        relax_kernel,
        grid_spec=grid_spec,
        out_shape=[many, many, *[single] * (2 * count),
                   pltpu.HBM((cap, 2, length, length), bf16),
                   pltpu.HBM((len(blocks),) + blocks[0].shape, bf16)],
        compiler_params=pltpu.CompilerParams(vmem_limit_bytes=28 << 20),
        cost_estimate=pl.CostEstimate(flops=8 << 30, bytes_accessed=16 << 20, transcendentals=1 << 19),
        name="relax_positions",
    )(tab, live.reshape(1), mix, *blocks, patches, amplitude, forward, inverse)
    return (outs[0], outs[1], outs[2:2 + count], outs[2 + count:2 + 2 * count]), outs[-2], outs[-1]


def settle_kernel(sel_ref, row_ref, col_ref, grad_ref, mine_ref, other_ref, band_ref):
    cap, _, length, _ = grad_ref.shape
    height, width = mine_ref.shape[1:]
    places = []
    for spot in range(cap):
        row_at, col_at, sel = row_ref[spot], col_ref[spot], sel_ref[spot]
        cols = (iota((length, width), 1) == iota((length, width), 0) + col_at).astype(bf16)
        for part in range(2):
            band = jnp.dot(grad_ref[spot, part], cols, preferred_element_type=f32)
            band_ref[spot * length:(spot + 1) * length, part * width:(part + 1) * width] = band.astype(bf16)
        place = iota((2 * height, length), 1) + row_at + height * sel
        places.append((iota((2 * height, length), 0) == place).astype(bf16))
    places = jnp.concatenate(places, axis=1)
    for part in range(2):
        total = jnp.dot(places, band_ref[:, part * width:(part + 1) * width], preferred_element_type=f32)
        mine_ref[part] = total[:height]
        other_ref[part] = total[height:]


def settle(sel, row_at, col_at, grads, height, width):
    cap, _, length, _ = grads.shape
    tile = pl.BlockSpec((2, height, width), lambda *_: (0, 0, 0))
    grid_spec = pltpu.PrefetchScalarGridSpec(
        num_scalar_prefetch=3,
        grid=(1,),
        in_specs=[whole(grads)],
        out_specs=[tile, tile],
        scratch_shapes=[pltpu.VMEM((cap * length, 2 * width), bf16)],
    )
    shape = jax.ShapeDtypeStruct((2, height, width), f32)
    return pl.pallas_call(
        settle_kernel,
        grid_spec=grid_spec,
        out_shape=[shape, shape],
        compiler_params=pltpu.CompilerParams(vmem_limit_bytes=20 << 20),
        cost_estimate=pl.CostEstimate(flops=4 << 30, bytes_accessed=4 << 20, transcendentals=0),
        name="settle",
    )(sel, row_at, col_at, grads)


def weights_kernel(keep0_ref, keep1_ref, *refs):
    count = len(STEPS)
    cross, (block_ref, nw_ref) = refs[:2 * count], refs[2 * count:]
    lanes = keep0_ref.shape[3]
    tall = keep0_ref.shape[1] * RB
    wide = block_ref.shape[1] * RB
    table = jnp.zeros((tall, wide), f32)
    for j in range(4 * count):
        side, far_side, place = j // (2 * count), j // count % 2, j % count
        if far_side:
            mine = cross[count * side + place][...]
        else:
            mine = (keep1_ref if side else keep0_ref)[place]
        table += lax.dot_general(mine.reshape(tall, lanes), block_ref[j].reshape(wide, lanes),
                                 (((1,), (1,)), ((), ())), preferred_element_type=f32)
    same = (iota((tall, wide), 0) % RB) == (iota((tall, wide), 1) % RB)
    table = jnp.where(same, table, 0.0)
    slots, modes = tall // (2 * RB), wide // (2 * RB)

    def mul(left, right):
        return jnp.dot(left, right, precision=HI, preferred_element_type=f32)

    def gather_rows(which):
        pick = iota((slots, tall), 1) // RB == 2 * iota((slots, tall), 0) + which
        return mul(pick.astype(f32), table)

    def pick_cols(which):
        pick = iota((wide, modes), 0) // RB == which * modes + iota((wide, modes), 1)
        return pick.astype(f32)

    low, high = gather_rows(0), gather_rows(1)
    cols_r, cols_i = pick_cols(0), pick_cols(1)
    norm = 1.0 / (4 * count * RB * lanes)
    nw_ref[0] = (mul(low, cols_r) + mul(high, cols_i)) * norm
    nw_ref[1] = (mul(high, cols_r) - mul(low, cols_i)) * norm


def new_weights_of(updated, blocks):
    keep0, keep1, cross0, cross1 = updated
    args = [keep0, keep1, *cross0, *cross1, blocks]
    return pl.pallas_call(
        weights_kernel,
        out_shape=jax.ShapeDtypeStruct((2, keep0.shape[1] // 2, blocks.shape[1] // 2), f32),
        compiler_params=pltpu.CompilerParams(vmem_limit_bytes=16 << 20),
        cost_estimate=pl.CostEstimate(flops=2 << 30, bytes_accessed=6 << 20, transcendentals=0),
        name="new_weights",
    )(*args)


def sums_kernel(wide_ref, near_ref, twin_ref, far_ref, far_twin_ref, out_ref):
    lanes = near_ref.shape[-1]

    def flat(value):
        return value.reshape(-1, lanes)

    total = jnp.dot(wide_ref[0], flat(near_ref[0]), preferred_element_type=f32)
    total += jnp.dot(wide_ref[1], flat(twin_ref[0]), preferred_element_type=f32)
    total += jnp.dot(wide_ref[2], flat(far_ref[...]), preferred_element_type=f32)
    total += jnp.dot(wide_ref[3], flat(far_twin_ref[...]), preferred_element_type=f32)
    out_ref[...] = total.reshape(out_ref.shape).astype(out_ref.dtype)


def pair_sums(place, wide, near, twin, far, far_twin, kind):
    lanes = near.shape[-1]
    strip = pl.BlockSpec((1,) + near.shape[1:], lambda i: (place, 0, 0, 0))
    tall = wide.shape[1] // RB
    return pl.pallas_call(
        sums_kernel,
        grid=(1,),
        in_specs=[whole(wide), strip, strip, whole(far), whole(far_twin)],
        out_specs=pl.BlockSpec((tall, RB, lanes), lambda *_: (0, 0, 0)),
        out_shape=jax.ShapeDtypeStruct((tall, RB, lanes), kind),
        compiler_params=pltpu.CompilerParams(vmem_limit_bytes=8 << 20),
        cost_estimate=pl.CostEstimate(flops=1 << 29, bytes_accessed=2 << 20, transcendentals=0),
        name="mode_sums",
    )(wide, near, twin, far, far_twin)


def finish_kernel(*refs):
    own_ref, others = refs[0], refs[1:-3]
    sum_ref, gram_ref, acc_ref = refs[-3:]
    lanes = own_ref.shape[-1]
    total = own_ref[...]
    for other in others:
        total = total + other[...].astype(f32)
    acc_ref[...] = total
    for row in range(RB):
        sum_ref[:, row * lanes:(row + 1) * lanes] = acc_ref[:, row, :]
    modes = sum_ref.shape[0] // 2
    flat = sum_ref[...]
    full = lax.dot_general(flat, flat, (((1,), (1,)), ((), ())), precision=HI,
                           preferred_element_type=f32)
    gram_ref[0] = full[:modes, :modes] + full[modes:, modes:]
    gram_ref[1] = full[modes:, :modes] - full[:modes, modes:]


def finish_sums(own, others):
    tall, _, lanes = own.shape
    return pl.pallas_call(
        finish_kernel,
        out_shape=[
            jax.ShapeDtypeStruct((tall, RB * lanes), f32),
            jax.ShapeDtypeStruct((2, tall // 2, tall // 2), f32),
        ],
        scratch_shapes=[pltpu.VMEM((tall, RB, lanes), f32)],
        compiler_params=pltpu.CompilerParams(vmem_limit_bytes=8 << 20),
        cost_estimate=pl.CostEstimate(flops=1 << 28, bytes_accessed=2 << 20, transcendentals=0),
        name="finish_sums",
    )(own, *others)


def modes_kernel(norm, gram_ref, sum_ref, out_ref):
    count = gram_ref.shape[1]
    gram_r, gram_i = gram_ref[0], gram_ref[1]
    eye = (iota((count, count), 0) == iota((count, count), 1)).astype(f32)
    zero = jnp.zeros((count, count), f32)
    work = jnp.concatenate([gram_r, gram_i, eye, zero], axis=1)
    turned = jnp.concatenate([-gram_i, gram_r, zero, eye], axis=1)
    row_ids = iota((count, 1), 0)
    roots = jnp.zeros((count, 1), f32)
    for pivot in range(count):
        lead = work[pivot:pivot + 1, pivot:pivot + 1]
        roots = jnp.where(row_ids == pivot, lead, roots)
        if pivot + 1 < count:
            below = jnp.where(row_ids > pivot, 1.0 / lead, 0.0)
            coef_r = work[:, pivot:pivot + 1] * below
            coef_i = work[:, count + pivot:count + pivot + 1] * below
            row, row_t = work[pivot:pivot + 1], turned[pivot:pivot + 1]
            work = work - (coef_r * row + coef_i * row_t)
            turned = turned - (coef_r * row_t - coef_i * row)
    back = work[:, 2 * count:] * (norm * lax.rsqrt(roots))
    back_r, back_i = back[:, :count], back[:, count:]
    full = jnp.concatenate([
        jnp.concatenate([back_r, -back_i], axis=1),
        jnp.concatenate([back_i, back_r], axis=1)], axis=0)
    out_ref[...] = jnp.dot(full, sum_ref[...], precision=HI, preferred_element_type=f32)


def new_modes_of(gram, summed, norm):
    def kernel(gram_ref, sum_ref, out_ref):
        modes_kernel(norm, gram_ref, sum_ref, out_ref)

    return pl.pallas_call(
        kernel,
        out_shape=jax.ShapeDtypeStruct(summed.shape, f32),
        compiler_params=pltpu.CompilerParams(vmem_limit_bytes=8 << 20),
        cost_estimate=pl.CostEstimate(flops=1 << 27, bytes_accessed=1 << 20, transcendentals=256),
        name="orthonormal_modes",
    )(gram, summed)


def swap_tiles(value):
    count = lax.axis_size("tile")
    return lax.ppermute(value, "tile", [(i, (i + 1) % count) for i in range(count)])


def turn(value, step):
    count = lax.axis_size("scan")
    return lax.ppermute(value, "scan", [(i, (i + 2 * step) % count) for i in range(count)])


def across(value):
    count = lax.axis_size("scan")
    return lax.ppermute(value, "scan", [(i, i ^ 1) for i in range(count)])


def after(value, *others):
    return lax.optimization_barrier((value, *others))[0]


def places(z, y, tile):
    steps = jnp.array(STEPS, jnp.int32)
    strips = 2 * ((z + steps) % len(STEPS))
    strips = jnp.concatenate([strips + y, strips + 1 - y])
    return jnp.concatenate([2 * strips + tile, 2 * strips + 1 - tile]).astype(jnp.int32)


def gather_blocks(own, obj_b, cut, ready):
    come = {1: turn(own, 1), 3: turn(own, 3)}
    side = {0: across(own)}
    obj_pair = jnp.stack([obj_b, swap_tiles(obj_b)])
    patches = cut(obj_pair)
    patches, come[1], come[3], ready = lax.optimization_barrier((patches, come[1], come[3], ready))
    come[2] = turn(come[1], 1)
    for step in (1, 3, 2):
        side[step] = across(come[step])
    come[0] = own
    order = [-step % len(STEPS) for step in STEPS]
    mine = [come[step] for step in order] + [side[step] for step in order]
    return mine + [swap_tiles(value) for value in mine], patches, ready


def gather_any(own, obj_b, cut, ready):
    rows = own.shape[1]
    every = lax.all_gather(own, ("scan", "tile"))
    every = every.reshape((-1, RB // rows) + own.shape).transpose(0, 2, 1, 3, 4)
    every = every.reshape(-1, own.shape[0], RB, own.shape[2])
    blocks = [every[4 * step + 2 * y + tile] for tile in (0, 1) for y in (0, 1) for step in STEPS]
    return blocks, cut(jnp.stack([obj_b, swap_tiles(obj_b)])), ready


def gather_mixing(weights_b):
    wt_r, wt_i = jnp.swapaxes(weights_b[0], 0, 1), jnp.swapaxes(weights_b[1], 0, 1)
    real_rows = jnp.stack([wt_r, wt_i], axis=2)
    imag_rows = jnp.stack([-wt_i, wt_r], axis=2)
    count, cap = wt_r.shape
    return jnp.stack([real_rows, imag_rows], axis=0).reshape(2 * count, 2 * cap)


def scatter_sums(weights_b, updated, blocks):
    keep0, keep1, cross0, cross1 = updated
    pair = jnp.stack([weights_b, swap_tiles(weights_b)])
    pair = after(pair, blocks[-1])
    quad = jnp.concatenate([pair, across(pair)])
    wide = widen(jax.vmap(gather_mixing)(quad))
    order = (2, 3, 1, 0)
    at = {step: STEPS.index(step) for step in order}
    twin_cross = {step: swap_tiles(cross1[at[step]]) for step in order}
    twin = swap_tiles(keep1)
    far, far_twin, line = {}, {}, []
    for step in order:
        for value, dest in ((cross0[at[step]], far), (twin_cross[step], far_twin)):
            dest[step] = across(after(value, line[-3]) if len(line) >= 3 else value)
            line.append(dest[step])

    def part(step, kind):
        return pair_sums(at[step], wide, keep0, twin, far[step], far_twin[step], kind)

    through = turn(part(2, bf16), 1)
    third = turn(part(3, bf16), 3)
    first = turn((part(1, f32) + through.astype(f32)).astype(bf16), 1)
    return finish_sums(part(0, f32), [first, third])


def scatter_any(weights_b, updated, _):
    devices = lax.axis_size("scan") * lax.axis_size("tile")
    keep0, keep1, cross0, cross1 = updated
    count, slots, _, length = keep0.shape
    every = lax.all_gather(weights_b, ("scan", "tile"))
    rows = 4 * count * RB // devices
    parts = jnp.stack([keep0, keep1, jnp.stack(cross0), jnp.stack(cross1)], axis=1)
    parts = jnp.stack([parts[STEPS.index(step)] for step in range(count)])
    parts = parts.reshape(4 * count, slots, RB // rows, rows, length)
    parts = parts.transpose(0, 2, 1, 3, 4).reshape(devices, slots, rows, length)
    arrived = lax.all_to_all(parts, ("scan", "tile"), split_axis=0, concat_axis=0, tiled=True)
    flat = arrived.reshape(devices, slots // 2, 2, rows * length).astype(f32)
    wt_r, wt_i = every[:, 0].astype(f32), every[:, 1].astype(f32)
    up_r, up_i = flat[:, :, 0], flat[:, :, 1]

    def mul(left, right):
        return jnp.einsum("dpk,dpx->kx", left, right, precision=HI)

    sum_r = mul(wt_r, up_r) + mul(wt_i, up_i)
    sum_i = mul(wt_r, up_i) - mul(wt_i, up_r)

    def pair(left, right):
        return jnp.dot(left, right.T, precision=HI)

    gram = jnp.stack([pair(sum_r, sum_r) + pair(sum_i, sum_i),
                      pair(sum_i, sum_r) - pair(sum_r, sum_i)])
    return jnp.concatenate([sum_r, sum_i]), gram


def sum_everywhere(value, works):
    value = value + swap_tiles(value)
    count = lax.axis_size("scan")
    step, works = 1, list(works)
    results = []
    while step < count:
        come = lax.ppermute(value, "scan", [(i, i ^ step) for i in range(count)])
        step *= 2
        if works and step < count:
            results.append(works.pop(0)(value, results))
            value, come, results[-1] = lax.optimization_barrier((value, come, results[-1]))
        value = value + come
    return value, results


def local(
    object_field, probe_modes, weights, amplitude, slot_count, tile_owner, corner_row, corner_col
):
    n_tile = lax.axis_size("tile")
    devices = lax.axis_size("scan") * n_tile
    tile = lax.axis_index("tile")
    cap, length, _ = amplitude.shape
    count = probe_modes.shape[1]
    pixels = length * length
    rows = length // devices
    forward, inverse = transform_tables(length)

    def mine(value):
        return lax.dynamic_slice_in_dim(value, tile * cap, cap)

    owner, row_at, col_at = mine(tile_owner), mine(corner_row), mine(corner_col)
    sel = jnp.where(owner == tile, 0, 1).astype(jnp.int32)
    live_n = lax.dynamic_index_in_dim(slot_count, tile, 0, keepdims=False)

    own = probe_modes.astype(bf16).reshape(2 * count, rows, length)
    obj_b = object_field.astype(bf16)
    weights_b = weights.astype(bf16)
    planned = lax.axis_size("scan") == 8 and n_tile == 2 and rows == RB

    def cut(obj_pair):
        return cut_patches(obj_pair, sel, row_at, col_at, length)

    scan = lax.axis_index("scan")
    tab = places(scan // 2, scan % 2, tile) if planned else places(0, 0, 0)
    wt_r, wt_i = weights_b[0], weights_b[1]
    mix = jnp.stack([jnp.concatenate([wt_r, -wt_i], axis=1),
                     jnp.concatenate([wt_i, wt_r], axis=1)], axis=1)
    mix = widen(mix.reshape(1, 2 * cap, 2 * count))
    blocks, patches, (tab, mix, live_n, forward, inverse) = (gather_blocks if planned else gather_any)(
        own, obj_b, cut, (tab, mix, live_n, forward, inverse))
    updated, grads, stash = relax(tab, live_n, mix, blocks, patches, amplitude, forward, inverse)

    summed, gram = (scatter_sums if planned else scatter_any)(weights_b, updated, blocks)

    def put_back(token, _):
        mine_sum, other_sum = settle(sel, row_at, col_at, after(grads, token), *object_field.shape[1:])
        return mine_sum, other_sum

    def project(token, _):
        keep0, keep1, cross0, cross1 = updated
        return new_weights_of((after(keep0, token), keep1, cross0, cross1), stash)

    gram, (object_sums, new_weights) = sum_everywhere(gram, [put_back, project])
    new_object = object_field + OBJ_STEP * (object_sums[0] + swap_tiles(object_sums[1]))
    gram = after(gram, new_object)
    new_modes = new_modes_of(gram, summed, math.sqrt(pixels)).reshape(probe_modes.shape)
    return (new_object, new_modes, new_weights)


def solution(mesh):
    in_specs = (
        P(None, ("groups", "scan", "tile"), None),
        P(None, "groups", ("scan", "tile")),
        P(None, ("groups", "scan", "tile"), None),
        P(("groups", "scan", "tile"), None, None),
        P(("groups", "scan")),
        P(("groups", "scan")),
        P(("groups", "scan")),
        P(("groups", "scan")),
    )
    out_specs = (
        P(None, ("groups", "scan", "tile"), None),
        P(None, "groups", ("scan", "tile")),
        P(None, ("groups", "scan", "tile"), None),
    )
    return jax.shard_map(local, mesh=mesh, in_specs=in_specs, out_specs=out_specs, check_vma=False)
```

time: 142 us -> 105 us (0.74)
  Pallas kernels: 48.8 us -> 32.2 us
  waiting for transfers between devices: 44.9 us -> 37 us
  other arithmetic: 11.9 us -> 5.18 us
  local copies, waits for them, and re-layouts: 5.47 us -> 1.1 us
    pallas_call x6, Pallas kernels: 27.7 us -> 15.9 us  [the longest x1 11.2 us: relax(): pl.pallas_call(relax_kernel, grid_spec=grid_spec, out_shape=[many, many,...]
    ppermute x6, waiting for transfers between devices: 16.4 us -> 9.66 us  [turn(): lax.ppermute(value, 'scan', [(i, (i + 2 * step) % count) for i in range(c...]
    another operation x7 -> x2, other arithmetic: 6.73 us -> 1.2 us  [gather_blocks(): obj_pair = jnp.stack([obj_b, swap_tiles(obj_b)])]
    ppermute x9 -> x13, waiting for transfers between devices: 23.7 us -> 18.3 us  [across(): return lax.ppermute(value, 'scan', [(i, i ^ 1) for i in range(count)])]
    pallas_call x1, Pallas kernels: 8.3 us -> 4.57 us  [settle(): pl.pallas_call(settle_kernel, grid_spec=grid_spec, out_shape=[shape, shap...]
    ppermute x13 -> x17, waiting for transfers between devices: 2.25 us -> 5.48 us  [swap_tiles(): lax.ppermute(value, 'tile', [(i, (i + 1) % count) for i in range(count)])]
    unnamed x93 -> x28, local copies, waits for them, and re-layouts: 3.12 us -> 0.12 us
    ppermute x9 -> x13, starting transfers between devices: 11 us -> 13.5 us  [across(): return lax.ppermute(value, 'scan', [(i, i ^ 1) for i in range(count)])]
  transfers between devices with their start and end apart: 31 -> 39, of which waited for: 13 -> 19; matrix products, arithmetic and copies ran while one was open for 9% -> 4% of each run, Pallas kernels for 20% -> 16%
where the time goes in v2:
time: 105 us
  waiting for transfers between devices  37 us (35%)
  Pallas kernels  32.2 us (31%)
  starting transfers between devices  28.6 us (27%)
  other arithmetic  5.18 us (5%)
  local copies, waits for them, and re-layouts  1.1 us (1%)
  between operations  1.08 us (1%)
    ppermute x13, waiting for transfers between devices, across(): return lax.ppermute(value, 'scan', [(i, i ^ 1) for i in range(count)])  18.3 us
    ppermute x13, starting transfers between devices, across(): return lax.ppermute(value, 'scan', [(i, i ^ 1) for i in range(count)])  13.5 us
    pallas_call x1, Pallas kernels, relax(): pl.pallas_call(relax_kernel, grid_spec=grid_spec, out_shape=[many, many,...  11.2 us
    ppermute x6, starting transfers between devices, turn(): lax.ppermute(value, 'scan', [(i, (i + 2 * step) % count) for i in range(c...  10.5 us
    ppermute x6, waiting for transfers between devices, turn(): lax.ppermute(value, 'scan', [(i, (i + 2 * step) % count) for i in range(c...  9.66 us
    pallas_call x1, Pallas kernels, cut_patches(): pl.pallas_call(cut_kernel, grid_spec=grid_spec, out_shape=jax.ShapeDtypeS...  6.1 us
    ppermute x17, waiting for transfers between devices, swap_tiles(): lax.ppermute(value, 'tile', [(i, (i + 1) % count) for i in range(count)])  5.48 us
    pallas_call x1, Pallas kernels, settle(): pl.pallas_call(settle_kernel, grid_spec=grid_spec, out_shape=[shape, shap...  4.57 us
  transfers between devices with their start and end apart: 39, of which 19 were waited for; matrix products, arithmetic and copies ran while one was open for 4% of the time, Pallas kernels for 16%

profile of v2, /device:TPU:0, one launch (start us, length us, event | category | flops | bytes accessed | tf_op | source)
XLA Modules:
  0.0 105.2 jit_solution(9602447423112702151)
XLA Ops:
  0.7 1.1 %convert_element_type.17 = bf16[2,16,4096]{2,1,0:T(8,128)(2,1)S(1)} convert(f32[2,16,4096]{2,1,0:T(8,128)} %param.12) | non-fusion elementwise | flops 131072 | bytes 786432 | tf_op jit(solution)/shard_map/convert_element_type | solution.py:550
  1.9 3.1 %collective-permute-start.2 = (bf16[32,16,256]{2,1,0:T(8,128)(2,1)S(1)}, bf16[32,16,256]{2,1,0:T(8,128)(2,1)S(1)}, u32[]{:S(2)}, u32[]{:S(2)}) collective-permute-start(bf16[32,16,256]{2,1,0:T(8,128)(2,1)S(1)} %bitcast.50), channel_id=1, source_target_pairs={{0,4},{2,6},{4,8},{6,10},{8,12},{10,14},{12,0},{14,2},{1,5},{3,7},... | collective-permute-start | bytes 786440 | tf_op jit(solution)/shard_map/ppermute | solution.py:411
  5.0 2.1 %collective-permute-start.3 = (bf16[32,16,256]{2,1,0:T(8,128)(2,1)S(1)}, bf16[32,16,256]{2,1,0:T(8,128)(2,1)S(1)}, u32[]{:S(2)}, u32[]{:S(2)}) collective-permute-start(bf16[32,16,256]{2,1,0:T(8,128)(2,1)S(1)} %bitcast.51), channel_id=1, source_target_pairs={{0,12},{2,14},{4,0},{6,2},{8,4},{10,6},{12,8},{14,10},{1,13},{3,15... | collective-permute-start | bytes 786440 | tf_op jit(solution)/shard_map/ppermute | solution.py:411
  7.1 1.7 %collective-permute-start.8 = (bf16[32,16,256]{2,1,0:T(8,128)(2,1)S(1)}, bf16[32,16,256]{2,1,0:T(8,128)(2,1)S(1)}, u32[]{:S(2)}, u32[]{:S(2)}) collective-permute-start(bf16[32,16,256]{2,1,0:T(8,128)(2,1)S(1)} %bitcast.52), channel_id=1, source_target_pairs={{0,2},{2,0},{4,6},{6,4},{8,10},{10,8},{12,14},{14,12},{1,3},{3,1},... | collective-permute-start | bytes 786440 | tf_op jit(solution)/shard_map/ppermute | solution.py:416
  8.8 1.3 %convert_element_type.16 = bf16[2,320,384]{2,1,0:T(8,128)(2,1)S(1)} convert(f32[2,320,384]{2,1,0:T(8,128)} %param.11) | non-fusion elementwise | flops 245760 | bytes 1474560 | tf_op jit(solution)/shard_map/convert_element_type | solution.py:551
  10.9 0.6 dynamic_slice.16
  12.1 1.1 %pad_maximum_fusion.obj_ref = bf16[2,2,320,384]{3,2,1,0:T(8,128)(2,1)S(1)} fusion(bf16[1,2,320,384]{3,2,1,0:T(8,128)(2,1)} %bitcast.3, bf16[1,2,320,384]{3,2,1,0:T(8,128)(2,1)S(1)} %convert_bitcast_fusion), kind=kLoop, calls=%fused_computation | loop fusion | flops 491520 | bytes 1966080 | tf_op jit(solution)/shard_map/stack | solution.py:433
  13.3 6.1 %cut_patches.1.refs_16_ = bf16[8,2,256,256]{3,2,1,0:T(8,128)(2,1)S(1)} custom-call(s32[8]{0:T(128)S(1)} %compare_select_fusion.2.sel_ref, s32[8]{0:T(128)S(1)} %dynamic_slice.14.row_ref, s32[8]{0:T(128)S(1)} %dynamic_slice.15.col_ref, bf16[2,2,320,384]{3,2,1,0:T(8,128)(2,1)S(1)} %pad_maximum_fusion.obj_ref), custom_call_target="tpu_custom_call" | custom-call | flops 4294967296 | bytes 4194304 | tf_op jit(solution)/shard_map/cut_patches/pallas_call | solution.py:76
  19.5 1.5 %collective-permute-start.4 = (bf16[32,16,256]{2,1,0:T(8,128)(2,1)S(1)}, bf16[32,16,256]{2,1,0:T(8,128)(2,1)S(1)}, u32[]{:S(2)}, u32[]{:S(2)}) collective-permute-start(bf16[32,16,256]{2,1,0:T(8,128)(2,1)S(1)} %collective-permute-done.3.refs_3_), channel_id=1, source_target_pairs={{0,2},{2,0},{4,6},{6,4},{8,10},{10,8},{12,14},{14,12},{1,3},{3,1},... | collective-permute-start | bytes 786440 | tf_op jit(solution)/shard_map/ppermute | solution.py:416
  21.0 0.5 collective-permute-start.11
  21.5 0.6 collective-permute-done
  22.2 0.5 collective-permute-start.10
  22.7 6.9 %collective-permute-done.7.refs_1_ = bf16[32,16,256]{2,1,0:T(8,128)(2,1)S(1)} collective-permute-done((bf16[32,16,256]{2,1,0:T(8,128)(2,1)S(1)}, bf16[32,16,256]{2,1,0:T(8,128)(2,1)S(1)}, u32[]{:S(2)}, u32[]{:S(2)}) %collective-permute-start.7) | collective-permute-done | bytes 262176 | tf_op jit(solution)/shard_map/ppermute | solution.py:411
  30.0 1.5 %collective-permute-done.5.refs_15_ = bf16[32,16,256]{2,1,0:T(8,128)(2,1)S(1)} collective-permute-done((bf16[32,16,256]{2,1,0:T(8,128)(2,1)S(1)}, bf16[32,16,256]{2,1,0:T(8,128)(2,1)S(1)}, u32[]{:S(2)}, u32[]{:S(2)}) %collective-permute-start.5) | collective-permute-done | bytes 262176 | tf_op jit(solution)/shard_map/ppermute | solution.py:406
  31.5 1.7 %collective-permute-start.6 = (bf16[2,2,8,16]{3,2,1,0:T(8,128)(2,1)S(1)}, bf16[2,2,8,16]{3,2,1,0:T(8,128)(2,1)S(1)}, u32[]{:S(2)}, u32[]{:S(2)}) collective-permute-start(bf16[2,2,8,16]{3,2,1,0:T(8,128)(2,1)S(1)} %pad_maximum_fusion.1), channel_id=1, source_target_pairs={{0,2},{2,0},{4,6},{6,4},{8,10},{10,8},{12,14},{14,12},{1,3},{3,1},... | collective-permute-start | bytes 3080 | tf_op jit(solution)/shard_map/ppermute | solution.py:416
  33.2 0.5 collective-permute-start.14
  33.7 0.6 collective-permute-done.10.refs_6_
  34.3 4.9 %collective-permute-done.9.refs_5_ = bf16[32,16,256]{2,1,0:T(8,128)(2,1)S(1)} collective-permute-done((bf16[32,16,256]{2,1,0:T(8,128)(2,1)S(1)}, bf16[32,16,256]{2,1,0:T(8,128)(2,1)S(1)}, u32[]{:S(2)}, u32[]{:S(2)}) %collective-permute-start.9) | collective-permute-done | bytes 262176 | tf_op jit(solution)/shard_map/ppermute | solution.py:416
  39.7 1.0 collective-permute-done.17.refs_14_
  41.1 11.2 %relax_positions.1 = (bf16[4,16,16,256]{3,2,1,0:T(8,128)(2,1)S(1)}, bf16[4,16,16,256]{3,2,1,0:T(8,128)(2,1)S(1)}, bf16[16,16,256]{2,1,0:T(8,128)(2,1)S(1)}, bf16...) custom-call(s32[16]{0:T(128)S(1)} %pad_add_fusion.tab_ref, ...), custom_call_target="tpu_custom_call" | custom-call | flops 8589934592 | bytes 16777216 | tf_op jit(solution)/shard_map/relax_positions/pallas_call | solution.py:200
  52.8 1.1 %collective-permute-start.20 = (bf16[16,16,256]{2,1,0:T(8,128)(2,1)S(1)}, bf16[16,16,256]{2,1,0:T(8,128)(2,1)S(1)}, u32[]{:S(2)}, u32[]{:S(2)}) collective-permute-start(bf16[16,16,256]{2,1,0:T(8,128)(2,1)S(1)} %get-tuple-element.56.refs_1_), channel_id=1, source_target_pairs={{0,2},{2,0},{4,6},{6,4},{8,10},{10,8},{12,14},{14,12},{1,3},{3,1},... | collective-permute-start | bytes 393224 | tf_op jit(solution)/shard_map/ppermute | solution.py:416
  54.4 1.1 %collective-permute-start.25 = (bf16[16,16,256]{2,1,0:T(8,128)(2,1)S(1)}, bf16[16,16,256]{2,1,0:T(8,128)(2,1)S(1)}, u32[]{:S(2)}, u32[]{:S(2)}) collective-permute-start(bf16[16,16,256]{2,1,0:T(8,128)(2,1)S(1)} %collective-permute-done.24), channel_id=1, source_target_pairs={{0,2},{2,0},{4,6},{6,4},{8,10},{10,8},{12,14},{14,12},{1,3},{3,1},... | collective-permute-start | bytes 393224 | tf_op jit(solution)/shard_map/ppermute | solution.py:416
  55.8 1.0 collective-permute-start.29
  56.7 2.4 %collective-permute-done.20.far_ref = bf16[16,16,256]{2,1,0:T(8,128)(2,1)S(1)} collective-permute-done((bf16[16,16,256]{2,1,0:T(8,128)(2,1)S(1)}, bf16[16,16,256]{2,1,0:T(8,128)(2,1)S(1)}, u32[]{:S(2)}, u32[]{:S(2)}) %collective-permute-start.20) | collective-permute-done | bytes 131104 | tf_op jit(solution)/shard_map/ppermute | solution.py:416
  59.2 0.8 widen.3.wide_ref
  59.9 2.0 %collective-permute-done.25.far_twin_ref = bf16[16,16,256]{2,1,0:T(8,128)(2,1)S(1)} collective-permute-done((bf16[16,16,256]{2,1,0:T(8,128)(2,1)S(1)}, bf16[16,16,256]{2,1,0:T(8,128)(2,1)S(1)}, u32[]{:S(2)}, u32[]{:S(2)}) %collective-permute-start.25) | collective-permute-done | bytes 131104 | tf_op jit(solution)/shard_map/ppermute | solution.py:416
  62.4 1.1 collective-permute-start.31
  63.5 0.5 collective-permute-start.21
  64.0 1.5 %collective-permute-start.30 = (bf16[16,16,256]{2,1,0:T(8,128)(2,1)S(1)}, bf16[16,16,256]{2,1,0:T(8,128)(2,1)S(1)}, u32[]{:S(2)}, u32[]{:S(2)}) collective-permute-start(bf16[16,16,256]{2,1,0:T(8,128)(2,1)S(1)} %collective-permute-done.28), channel_id=1, source_target_pairs={{0,2},{2,0},{4,6},{6,4},{8,10},{10,8},{12,14},{14,12},{1,3},{3,1},... | collective-permute-start | bytes 393224 | tf_op jit(solution)/shard_map/ppermute | solution.py:416
  65.5 0.5 collective-permute-start.26
  66.0 3.8 %collective-permute-done.21.far_twin_ref = bf16[16,16,256]{2,1,0:T(8,128)(2,1)S(1)} collective-permute-done((bf16[16,16,256]{2,1,0:T(8,128)(2,1)S(1)}, bf16[16,16,256]{2,1,0:T(8,128)(2,1)S(1)}, u32[]{:S(2)}, u32[]{:S(2)}) %collective-permute-start.21) | collective-permute-done | bytes 131104 | tf_op jit(solution)/shard_map/ppermute | solution.py:416
  70.3 2.8 %collective-permute-start.33 = (bf16[32,16,256]{2,1,0:T(8,128)(2,1)S(1)}, bf16[32,16,256]{2,1,0:T(8,128)(2,1)S(1)}, u32[]{:S(2)}, u32[]{:S(2)}) collective-permute-start(bf16[32,16,256]{2,1,0:T(8,128)(2,1)S(1)} %mode_sums.7), channel_id=1, source_target_pairs={{0,12},{2,14},{4,0},{6,2},{8,4},{10,6},{12,8},{14,10},{1,13},{3,15... | collective-permute-start | bytes 786440 | tf_op jit(solution)/shard_map/ppermute | solution.py:411
  73.7 1.4 %collective-permute-start.32 = (bf16[32,16,256]{2,1,0:T(8,128)(2,1)S(1)}, bf16[32,16,256]{2,1,0:T(8,128)(2,1)S(1)}, u32[]{:S(2)}, u32[]{:S(2)}) collective-permute-start(bf16[32,16,256]{2,1,0:T(8,128)(2,1)S(1)} %add_convert_fusion), channel_id=1, source_target_pairs={{0,4},{2,6},{4,8},{6,10},{8,12},{10,14},{12,0},{14,2},{1,5},{3,7},... | collective-permute-start | bytes 786440 | tf_op jit(solution)/shard_map/ppermute | solution.py:411
  75.1 0.5 collective-permute-start.22
  75.6 1.5 %collective-permute-start.27 = (bf16[16,16,256]{2,1,0:T(8,128)(2,1)S(1)}, bf16[16,16,256]{2,1,0:T(8,128)(2,1)S(1)}, u32[]{:S(2)}, u32[]{:S(2)}) collective-permute-start(bf16[16,16,256]{2,1,0:T(8,128)(2,1)S(1)} %collective-permute-done.23), channel_id=1, source_target_pairs={{0,2},{2,0},{4,6},{6,4},{8,10},{10,8},{12,14},{14,12},{1,3},{3,1},... | collective-permute-start | bytes 393224 | tf_op jit(solution)/shard_map/ppermute | solution.py:416
  77.1 2.9 %collective-permute-done.22.far_ref = bf16[16,16,256]{2,1,0:T(8,128)(2,1)S(1)} collective-permute-done((bf16[16,16,256]{2,1,0:T(8,128)(2,1)S(1)}, bf16[16,16,256]{2,1,0:T(8,128)(2,1)S(1)}, u32[]{:S(2)}, u32[]{:S(2)}) %collective-permute-start.22) | collective-permute-done | bytes 131104 | tf_op jit(solution)/shard_map/ppermute | solution.py:416
  80.1 1.4 %collective-permute-done.27.far_twin_ref = bf16[16,16,256]{2,1,0:T(8,128)(2,1)S(1)} collective-permute-done((bf16[16,16,256]{2,1,0:T(8,128)(2,1)S(1)}, bf16[16,16,256]{2,1,0:T(8,128)(2,1)S(1)}, u32[]{:S(2)}, u32[]{:S(2)}) %collective-permute-start.27) | collective-permute-done | bytes 131104 | tf_op jit(solution)/shard_map/ppermute | solution.py:416
  81.5 0.4 mode_sums.4.refs_0_
  81.9 2.8 %collective-permute-done.32.refs_1_ = bf16[32,16,256]{2,1,0:T(8,128)(2,1)S(1)} collective-permute-done((bf16[32,16,256]{2,1,0:T(8,128)(2,1)S(1)}, bf16[32,16,256]{2,1,0:T(8,128)(2,1)S(1)}, u32[]{:S(2)}, u32[]{:S(2)}) %collective-permute-start.32) | collective-permute-done | bytes 262176 | tf_op jit(solution)/shard_map/ppermute | solution.py:411
  84.7 0.8 finish_sums.1
  85.5 1.2 %collective-permute-done.34 = f32[2,16,16]{2,1,0:T(8,128)S(1)} collective-permute-done((f32[2,16,16]{2,1,0:T(8,128)S(1)}, f32[2,16,16]{2,1,0:T(8,128)S(1)}, u32[]{:S(2)}, u32[]{:S(2)}) %collective-permute-start.34) | collective-permute-done | bytes 2080 | tf_op jit(solution)/shard_map/ppermute | solution.py:406
  87.1 4.6 %settle.1 = (f32[2,320,384]{2,1,0:T(8,128)S(1)}, f32[2,320,384]{2,1,0:T(8,128)S(1)}) custom-call(s32[8]{0:T(128)S(1)} %compare_select_fusion.2.sel_ref, s32[8]{0:T(128)S(1)} %dynamic_slice.14.row_ref, s32[8]{0:T(128)S(1)} %dynamic_slice.15.col_ref, bf16[8,2,256,256]{3,2,1,0:T(8,128)(2,1)S(1)} %copy-done.4), custom_call_target="tpu_custom_call" | custom-call | flops 4294967296 | bytes 4194304 | tf_op jit(solution)/shard_map/settle/pallas_call | solution.py:243
  92.0 2.9 %new_weights.1 = f32[2,8,16]{2,1,0:T(8,128)} custom-call(bf16[4,16,16,256]{3,2,1,0:T(8,128)(2,1)S(1)} %get-tuple-element.76.near_ref.keep0_ref, bf16[4,16,16,256]{3,2,1,0:T(8,128)(2,1)S(1)} %get-tuple-element.53.keep1_ref, bf16[16,16,256]{2,1,0:T(8,128)(2,1)S(1)} %get-tuple-element.58.refs_0_, bf16[16,16,256]{2,1,0:T(8,128)(2,1)S(1)} %get-tuple-element.56.refs_1_, ...), custom_call_target="tpu_custom_call" | custom-call | flops 2147483648 | bytes 6291456 | tf_op jit(solution)/shard_map/new_weights/pallas_call | solution.py:293
  94.9 0.6 collective-permute-done.37
  95.5 1.7 %collective-permute-start.38 = (f32[2,16,16]{2,1,0:T(8,128)S(1)}, f32[2,16,16]{2,1,0:T(8,128)S(1)}, u32[]{:S(2)}, u32[]{:S(2)}) collective-permute-start(f32[2,16,16]{2,1,0:T(8,128)S(1)} %add.79), channel_id=1, source_target_pairs={{0,8},{2,10},{4,12},{6,14},{8,0},{10,2},{12,4},{14,6},{1,9},{3,11}... | collective-permute-start | bytes 6152 | tf_op jit(solution)/shard_map/ppermute | solution.py:522
  97.3 2.9 %collective-permute-done.38 = f32[2,16,16]{2,1,0:T(8,128)S(1)} collective-permute-done((f32[2,16,16]{2,1,0:T(8,128)S(1)}, f32[2,16,16]{2,1,0:T(8,128)S(1)}, u32[]{:S(2)}, u32[]{:S(2)}) %collective-permute-start.38) | collective-permute-done | bytes 2080 | tf_op jit(solution)/shard_map/ppermute | solution.py:522
  100.3 1.1 %multiply_add_fusion = f32[2,320,384]{2,1,0:T(8,128)} fusion(f32[2,320,384]{2,1,0:T(8,128)S(1)} %copy-done.6, f32[2,320,384]{2,1,0:T(8,128)S(1)} %get-tuple-element.72, f32[2,320,384]{2,1,0:T(8,128)S(1)} %collective-permute-done.36), kind=kLoop, calls=%fused_computation.1 | loop fusion | flops 737280 | bytes 3932160 | tf_op jit(solution)/shard_map/add | solution.py:579
  101.3 3.8 %orthonormal_modes.1 = f32[32,4096]{1,0:T(8,128)} custom-call(f32[2,16,16]{2,1,0:T(8,128)S(1)} %add.80.gram_ref, f32[32,4096]{1,0:T(8,128)S(1)} %get-tuple-element.81.sum_ref), custom_call_target="tpu_custom_call" | custom-call | flops 134217728 | bytes 1048576 | tf_op jit(solution)/shard_map/orthonormal_modes/pallas_call | solution.py:395
  (104 shorter events, 6.2 us)
Async XLA Ops:
  0.6 11.0 %copy-start.5 = (f32[2,320,384]{2,1,0:T(8,128)S(1)}, f32[2,320,384]{2,1,0:T(8,128)}, u32[]{:S(2)}) copy-start(f32[2,320,384]{2,1,0:T(8,128)} %param.11) | copy-start | bytes 2949124
  0.7 9.7 %copy-start.9 = (s32[16]{0:T(128)S(1)}, s32[16]{0:T(128)}, u32[]{:S(2)}) copy-start(s32[16]{0:T(128)} %param.16) | copy-start | bytes 196
  0.7 10.1 %copy-start.10 = (s32[16]{0:T(128)S(1)}, s32[16]{0:T(128)}, u32[]{:S(2)}) copy-start(s32[16]{0:T(128)} %param.17) | copy-start | bytes 196
  0.7 10.1 %copy-start.11 = (s32[16]{0:T(128)S(1)}, s32[16]{0:T(128)}, u32[]{:S(2)}) copy-start(s32[16]{0:T(128)} %param.18) | copy-start | bytes 196
  0.7 10.2 %copy-start.12 = (s32[2]{0:T(128)S(1)}, s32[2]{0:T(128)}, u32[]{:S(2)}) copy-start(s32[2]{0:T(128)} %param.15) | copy-start | bytes 28
  1.9 17.5 %collective-permute-start.2 = (bf16[32,16,256]{2,1,0:T(8,128)(2,1)S(1)}, bf16[32,16,256]{2,1,0:T(8,128)(2,1)S(1)}, u32[]{:S(2)}, u32[]{:S(2)}) collective-permute-start(bf16[32,16,256]{2,1,0:T(8,128)(2,1)S(1)} %bitcast.50), channel_id=1, source_target_pairs={{0,4},{2,6},{4,8},{6,10},{8,12},{10,14},{12,0},{14,2},{1,5},{3,7},... | collective-permute-start | bytes 786440 | tf_op jit(solution)/shard_map/ppermute | solution.py:411
  5.0 14.4 %collective-permute-start.3 = (bf16[32,16,256]{2,1,0:T(8,128)(2,1)S(1)}, bf16[32,16,256]{2,1,0:T(8,128)(2,1)S(1)}, u32[]{:S(2)}, u32[]{:S(2)}) collective-permute-start(bf16[32,16,256]{2,1,0:T(8,128)(2,1)S(1)} %bitcast.51), channel_id=1, source_target_pairs={{0,12},{2,14},{4,0},{6,2},{8,4},{10,6},{12,8},{14,10},{1,13},{3,15... | collective-permute-start | bytes 786440 | tf_op jit(solution)/shard_map/ppermute | solution.py:411
  7.1 14.5 %collective-permute-start.8 = (bf16[32,16,256]{2,1,0:T(8,128)(2,1)S(1)}, bf16[32,16,256]{2,1,0:T(8,128)(2,1)S(1)}, u32[]{:S(2)}, u32[]{:S(2)}) collective-permute-start(bf16[32,16,256]{2,1,0:T(8,128)(2,1)S(1)} %bitcast.52), channel_id=1, source_target_pairs={{0,2},{2,0},{4,6},{6,4},{8,10},{10,8},{12,14},{14,12},{1,3},{3,1},... | collective-permute-start | bytes 786440 | tf_op jit(solution)/shard_map/ppermute | solution.py:416
  10.0 2.1 %collective-permute-start.1 = (bf16[2,320,384]{2,1,0:T(8,128)(2,1)S(1)}, bf16[2,320,384]{2,1,0:T(8,128)(2,1)}, u32[]{:S(2)}, u32[]{:S(2)}) collective-permute-start(bf16[2,320,384]{2,1,0:T(8,128)(2,1)S(1)} %convert_element_type.16), channel_id=1, source_target_pairs={{0,1},{1,0},{2,3},{3,2},{4,5},{5,4},{6,7},{7,6},{8,9},{9,8},{10,11... | collective-permute-start | bytes 1474568 | tf_op jit(solution)/shard_map/ppermute | solution.py:406
  13.2 27.9 %copy-start = (bf16[8,256,256]{2,1,0:T(8,128)(2,1)S(1)}, bf16[8,256,256]{2,1,0:T(8,128)(2,1)}, u32[]{:S(2)}) copy-start(bf16[8,256,256]{2,1,0:T(8,128)(2,1)} %refs_17_.1) | copy-start | bytes 3145732
  13.2 27.9 %copy-start.1 = (bf16[512,512]{1,0:T(8,128)(2,1)S(1)}, bf16[512,512]{1,0:T(8,128)(2,1)}, u32[]{:S(2)}) copy-start(bf16[512,512]{1,0:T(8,128)(2,1)} %constant.68.clone.refs_18_) | copy-start | bytes 1572868
  13.2 27.9 %copy-start.2 = (bf16[512,512]{1,0:T(8,128)(2,1)S(1)}, bf16[512,512]{1,0:T(8,128)(2,1)}, u32[]{:S(2)}) copy-start(bf16[512,512]{1,0:T(8,128)(2,1)} %constant.69.clone.refs_19_) | copy-start | bytes 1572868
  19.4 10.2 %collective-permute-start.7 = (bf16[32,16,256]{2,1,0:T(8,128)(2,1)S(1)}, bf16[32,16,256]{2,1,0:T(8,128)(2,1)S(1)}, u32[]{:S(2)}, u32[]{:S(2)}) collective-permute-start(bf16[32,16,256]{2,1,0:T(8,128)(2,1)S(1)} %collective-permute-done.2.refs_2_), channel_id=1, source_target_pairs={{0,4},{2,6},{4,8},{6,10},{8,12},{10,14},{12,0},{14,2},{1,5},{3,7},... | collective-permute-start | bytes 786440 | tf_op jit(solution)/shard_map/ppermute | solution.py:411
  19.5 10.4 %collective-permute-start.4 = (bf16[32,16,256]{2,1,0:T(8,128)(2,1)S(1)}, bf16[32,16,256]{2,1,0:T(8,128)(2,1)S(1)}, u32[]{:S(2)}, u32[]{:S(2)}) collective-permute-start(bf16[32,16,256]{2,1,0:T(8,128)(2,1)S(1)} %collective-permute-done.3.refs_3_), channel_id=1, source_target_pairs={{0,2},{2,0},{4,6},{6,4},{8,10},{10,8},{12,14},{14,12},{1,3},{3,1},... | collective-permute-start | bytes 786440 | tf_op jit(solution)/shard_map/ppermute | solution.py:416
  21.0 1.2 %collective-permute-start = (bf16[2,8,16]{2,1,0:T(8,128)(2,1)S(1)}, bf16[2,8,16]{2,1,0:T(8,128)(2,1)S(1)}, u32[]{:S(2)}, u32[]{:S(2)}) collective-permute-start(bf16[2,8,16]{2,1,0:T(8,128)(2,1)S(1)} %convert_element_type.15), channel_id=1, source_target_pairs={{0,1},{1,0},{2,3},{3,2},{4,5},{5,4},{6,7},{7,6},{8,9},{9,8},{10,11... | collective-permute-start | bytes 1544 | tf_op jit(solution)/shard_map/ppermute | solution.py:406
  21.0 12.1 %collective-permute-start.11 = (bf16[32,16,256]{2,1,0:T(8,128)(2,1)S(1)}, bf16[32,16,256]{2,1,0:T(8,128)(2,1)S(1)}, u32[]{:S(2)}, u32[]{:S(2)}) collective-permute-start(bf16[32,16,256]{2,1,0:T(8,128)(2,1)S(1)} %bitcast.53), channel_id=1, source_target_pairs={{0,1},{1,0},{2,3},{3,2},{4,5},{5,4},{6,7},{7,6},{8,9},{9,8},{10,11... | collective-permute-start | bytes 786440 | tf_op jit(solution)/shard_map/ppermute | solution.py:406
  21.5 11.6 %collective-permute-start.15 = (bf16[32,16,256]{2,1,0:T(8,128)(2,1)S(1)}, bf16[32,16,256]{2,1,0:T(8,128)(2,1)S(1)}, u32[]{:S(2)}, u32[]{:S(2)}) collective-permute-start(bf16[32,16,256]{2,1,0:T(8,128)(2,1)S(1)} %collective-permute-done.8.refs_4_), channel_id=1, source_target_pairs={{0,1},{1,0},{2,3},{3,2},{4,5},{5,4},{6,7},{7,6},{8,9},{9,8},{10,11... | collective-permute-start | bytes 786440 | tf_op jit(solution)/shard_map/ppermute | solution.py:406
  22.2 12.1 %collective-permute-start.10 = (bf16[32,16,256]{2,1,0:T(8,128)(2,1)S(1)}, bf16[32,16,256]{2,1,0:T(8,128)(2,1)S(1)}, u32[]{:S(2)}, u32[]{:S(2)}) collective-permute-start(bf16[32,16,256]{2,1,0:T(8,128)(2,1)S(1)} %collective-permute-done.2.refs_2_), channel_id=1, source_target_pairs={{0,2},{2,0},{4,6},{6,4},{8,10},{10,8},{12,14},{14,12},{1,3},{3,1},... | collective-permute-start | bytes 786440 | tf_op jit(solution)/shard_map/ppermute | solution.py:416
  29.6 9.6 %collective-permute-start.9 = (bf16[32,16,256]{2,1,0:T(8,128)(2,1)S(1)}, bf16[32,16,256]{2,1,0:T(8,128)(2,1)S(1)}, u32[]{:S(2)}, u32[]{:S(2)}) collective-permute-start(bf16[32,16,256]{2,1,0:T(8,128)(2,1)S(1)} %collective-permute-done.7.refs_1_), channel_id=1, source_target_pairs={{0,2},{2,0},{4,6},{6,4},{8,10},{10,8},{12,14},{14,12},{1,3},{3,1},... | collective-permute-start | bytes 786440 | tf_op jit(solution)/shard_map/ppermute | solution.py:416
  29.9 1.5 %collective-permute-start.5 = (bf16[32,16,256]{2,1,0:T(8,128)(2,1)S(1)}, bf16[32,16,256]{2,1,0:T(8,128)(2,1)S(1)}, u32[]{:S(2)}, u32[]{:S(2)}) collective-permute-start(bf16[32,16,256]{2,1,0:T(8,128)(2,1)S(1)} %collective-permute-done.4.refs_7_), channel_id=1, source_target_pairs={{0,1},{1,0},{2,3},{3,2},{4,5},{5,4},{6,7},{7,6},{8,9},{9,8},{10,11... | collective-permute-start | bytes 786440 | tf_op jit(solution)/shard_map/ppermute | solution.py:406
  31.5 7.8 %collective-permute-start.6 = (bf16[2,2,8,16]{3,2,1,0:T(8,128)(2,1)S(1)}, bf16[2,2,8,16]{3,2,1,0:T(8,128)(2,1)S(1)}, u32[]{:S(2)}, u32[]{:S(2)}) collective-permute-start(bf16[2,2,8,16]{3,2,1,0:T(8,128)(2,1)S(1)} %pad_maximum_fusion.1), channel_id=1, source_target_pairs={{0,2},{2,0},{4,6},{6,4},{8,10},{10,8},{12,14},{14,12},{1,3},{3,1},... | collective-permute-start | bytes 3080 | tf_op jit(solution)/shard_map/ppermute | solution.py:416
  33.2 6.6 %collective-permute-start.13 = (bf16[32,16,256]{2,1,0:T(8,128)(2,1)S(1)}, bf16[32,16,256]{2,1,0:T(8,128)(2,1)S(1)}, u32[]{:S(2)}, u32[]{:S(2)}) collective-permute-start(bf16[32,16,256]{2,1,0:T(8,128)(2,1)S(1)} %collective-permute-done.2.refs_2_), channel_id=1, source_target_pairs={{0,1},{1,0},{2,3},{3,2},{4,5},{5,4},{6,7},{7,6},{8,9},{9,8},{10,11... | collective-permute-start | bytes 786440 | tf_op jit(solution)/shard_map/ppermute | solution.py:406
  33.2 6.6 %collective-permute-start.14 = (bf16[32,16,256]{2,1,0:T(8,128)(2,1)S(1)}, bf16[32,16,256]{2,1,0:T(8,128)(2,1)S(1)}, u32[]{:S(2)}, u32[]{:S(2)}) collective-permute-start(bf16[32,16,256]{2,1,0:T(8,128)(2,1)S(1)} %collective-permute-done.3.refs_3_), channel_id=1, source_target_pairs={{0,1},{1,0},{2,3},{3,2},{4,5},{5,4},{6,7},{7,6},{8,9},{9,8},{10,11... | collective-permute-start | bytes 786440 | tf_op jit(solution)/shard_map/ppermute | solution.py:406
  34.3 5.4 %collective-permute-start.12 = (bf16[32,16,256]{2,1,0:T(8,128)(2,1)S(1)}, bf16[32,16,256]{2,1,0:T(8,128)(2,1)S(1)}, u32[]{:S(2)}, u32[]{:S(2)}) collective-permute-start(bf16[32,16,256]{2,1,0:T(8,128)(2,1)S(1)} %collective-permute-done.7.refs_1_), channel_id=1, source_target_pairs={{0,1},{1,0},{2,3},{3,2},{4,5},{5,4},{6,7},{7,6},{8,9},{9,8},{10,11... | collective-permute-start | bytes 786440 | tf_op jit(solution)/shard_map/ppermute | solution.py:406
  39.2 1.5 %collective-permute-start.17 = (bf16[32,16,256]{2,1,0:T(8,128)(2,1)S(1)}, bf16[32,16,256]{2,1,0:T(8,128)(2,1)S(1)}, u32[]{:S(2)}, u32[]{:S(2)}) collective-permute-start(bf16[32,16,256]{2,1,0:T(8,128)(2,1)S(1)} %collective-permute-done.10.refs_6_), channel_id=1, source_target_pairs={{0,1},{1,0},{2,3},{3,2},{4,5},{5,4},{6,7},{7,6},{8,9},{9,8},{10,11... | collective-permute-start | bytes 786440 | tf_op jit(solution)/shard_map/ppermute | solution.py:406
  39.3 1.8 %collective-permute-start.16 = (bf16[32,16,256]{2,1,0:T(8,128)(2,1)S(1)}, bf16[32,16,256]{2,1,0:T(8,128)(2,1)S(1)}, u32[]{:S(2)}, u32[]{:S(2)}) collective-permute-start(bf16[32,16,256]{2,1,0:T(8,128)(2,1)S(1)} %collective-permute-done.9.refs_5_), channel_id=1, source_target_pairs={{0,1},{1,0},{2,3},{3,2},{4,5},{5,4},{6,7},{7,6},{8,9},{9,8},{10,11... | collective-permute-start | bytes 786440 | tf_op jit(solution)/shard_map/ppermute | solution.py:406
  52.3 9.7 %collective-permute-start.18 = (bf16[4,16,16,256]{3,2,1,0:T(8,128)(2,1)S(1)}, bf16[4,16,16,256]{3,2,1,0:T(8,128)(2,1)S(1)}, u32[]{:S(2)}, u32[]{:S(2)}) collective-permute-start(bf16[4,16,16,256]{3,2,1,0:T(8,128)(2,1)S(1)} %get-tuple-element.53.keep1_ref), channel_id=1, source_target_pairs={{0,1},{1,0},{2,3},{3,2},{4,5},{5,4},{6,7},{7,6},{8,9},{9,8},{10,11... | collective-permute-start | bytes 1572872 | tf_op jit(solution)/shard_map/ppermute | solution.py:406
  52.4 2.0 %collective-permute-start.24 = (bf16[16,16,256]{2,1,0:T(8,128)(2,1)S(1)}, bf16[16,16,256]{2,1,0:T(8,128)(2,1)S(1)}, u32[]{:S(2)}, u32[]{:S(2)}) collective-permute-start(bf16[16,16,256]{2,1,0:T(8,128)(2,1)S(1)} %get-tuple-element.61.refs_5_), channel_id=1, source_target_pairs={{0,1},{1,0},{2,3},{3,2},{4,5},{5,4},{6,7},{7,6},{8,9},{9,8},{10,11... | collective-permute-start | bytes 393224 | tf_op jit(solution)/shard_map/ppermute | solution.py:406
  52.8 6.3 %collective-permute-start.20 = (bf16[16,16,256]{2,1,0:T(8,128)(2,1)S(1)}, bf16[16,16,256]{2,1,0:T(8,128)(2,1)S(1)}, u32[]{:S(2)}, u32[]{:S(2)}) collective-permute-start(bf16[16,16,256]{2,1,0:T(8,128)(2,1)S(1)} %get-tuple-element.56.refs_1_), channel_id=1, source_target_pairs={{0,2},{2,0},{4,6},{6,4},{8,10},{10,8},{12,14},{14,12},{1,3},{3,1},... | collective-permute-start | bytes 393224 | tf_op jit(solution)/shard_map/ppermute | solution.py:416
  53.9 9.5 %collective-permute-start.19 = (bf16[16,16,256]{2,1,0:T(8,128)(2,1)S(1)}, bf16[16,16,256]{2,1,0:T(8,128)(2,1)S(1)}, u32[]{:S(2)}, u32[]{:S(2)}) collective-permute-start(bf16[16,16,256]{2,1,0:T(8,128)(2,1)S(1)} %get-tuple-element.55.refs_6_), channel_id=1, source_target_pairs={{0,1},{1,0},{2,3},{3,2},{4,5},{5,4},{6,7},{7,6},{8,9},{9,8},{10,11... | collective-permute-start | bytes 393224 | tf_op jit(solution)/shard_map/ppermute | solution.py:406
  54.4 7.6 %collective-permute-start.25 = (bf16[16,16,256]{2,1,0:T(8,128)(2,1)S(1)}, bf16[16,16,256]{2,1,0:T(8,128)(2,1)S(1)}, u32[]{:S(2)}, u32[]{:S(2)}) collective-permute-start(bf16[16,16,256]{2,1,0:T(8,128)(2,1)S(1)} %collective-permute-done.24), channel_id=1, source_target_pairs={{0,2},{2,0},{4,6},{6,4},{8,10},{10,8},{12,14},{14,12},{1,3},{3,1},... | collective-permute-start | bytes 393224 | tf_op jit(solution)/shard_map/ppermute | solution.py:416
  55.8 8.2 %collective-permute-start.29 = (bf16[16,16,256]{2,1,0:T(8,128)(2,1)S(1)}, bf16[16,16,256]{2,1,0:T(8,128)(2,1)S(1)}, u32[]{:S(2)}, u32[]{:S(2)}) collective-permute-start(bf16[16,16,256]{2,1,0:T(8,128)(2,1)S(1)} %get-tuple-element.65.refs_2_), channel_id=1, source_target_pairs={{0,2},{2,0},{4,6},{6,4},{8,10},{10,8},{12,14},{14,12},{1,3},{3,1},... | collective-permute-start | bytes 393224 | tf_op jit(solution)/shard_map/ppermute | solution.py:416
  59.2 4.8 %collective-permute-start.28 = (bf16[16,16,256]{2,1,0:T(8,128)(2,1)S(1)}, bf16[16,16,256]{2,1,0:T(8,128)(2,1)S(1)}, u32[]{:S(2)}, u32[]{:S(2)}) collective-permute-start(bf16[16,16,256]{2,1,0:T(8,128)(2,1)S(1)} %get-tuple-element.64.refs_7_), channel_id=1, source_target_pairs={{0,1},{1,0},{2,3},{3,2},{4,5},{5,4},{6,7},{7,6},{8,9},{9,8},{10,11... | collective-permute-start | bytes 393224 | tf_op jit(solution)/shard_map/ppermute | solution.py:406
  62.4 11.1 %collective-permute-start.31 = (bf16[32,16,256]{2,1,0:T(8,128)(2,1)S(1)}, bf16[32,16,256]{2,1,0:T(8,128)(2,1)S(1)}, u32[]{:S(2)}, u32[]{:S(2)}) collective-permute-start(bf16[32,16,256]{2,1,0:T(8,128)(2,1)S(1)} %mode_sums.6), channel_id=1, source_target_pairs={{0,4},{2,6},{4,8},{6,10},{8,12},{10,14},{12,0},{14,2},{1,5},{3,7},... | collective-permute-start | bytes 786440 | tf_op jit(solution)/shard_map/ppermute | solution.py:411
  63.5 6.4 %collective-permute-start.21 = (bf16[16,16,256]{2,1,0:T(8,128)(2,1)S(1)}, bf16[16,16,256]{2,1,0:T(8,128)(2,1)S(1)}, u32[]{:S(2)}, u32[]{:S(2)}) collective-permute-start(bf16[16,16,256]{2,1,0:T(8,128)(2,1)S(1)} %collective-permute-done.19), channel_id=1, source_target_pairs={{0,2},{2,0},{4,6},{6,4},{8,10},{10,8},{12,14},{14,12},{1,3},{3,1},... | collective-permute-start | bytes 393224 | tf_op jit(solution)/shard_map/ppermute | solution.py:416
  64.0 9.1 %collective-permute-start.30 = (bf16[16,16,256]{2,1,0:T(8,128)(2,1)S(1)}, bf16[16,16,256]{2,1,0:T(8,128)(2,1)S(1)}, u32[]{:S(2)}, u32[]{:S(2)}) collective-permute-start(bf16[16,16,256]{2,1,0:T(8,128)(2,1)S(1)} %collective-permute-done.28), channel_id=1, source_target_pairs={{0,2},{2,0},{4,6},{6,4},{8,10},{10,8},{12,14},{14,12},{1,3},{3,1},... | collective-permute-start | bytes 393224 | tf_op jit(solution)/shard_map/ppermute | solution.py:416
  65.5 7.6 %collective-permute-start.26 = (bf16[16,16,256]{2,1,0:T(8,128)(2,1)S(1)}, bf16[16,16,256]{2,1,0:T(8,128)(2,1)S(1)}, u32[]{:S(2)}, u32[]{:S(2)}) collective-permute-start(bf16[16,16,256]{2,1,0:T(8,128)(2,1)S(1)} %get-tuple-element.62.refs_3_), channel_id=1, source_target_pairs={{0,2},{2,0},{4,6},{6,4},{8,10},{10,8},{12,14},{14,12},{1,3},{3,1},... | collective-permute-start | bytes 393224 | tf_op jit(solution)/shard_map/ppermute | solution.py:416
  66.0 9.6 %collective-permute-start.23 = (bf16[16,16,256]{2,1,0:T(8,128)(2,1)S(1)}, bf16[16,16,256]{2,1,0:T(8,128)(2,1)S(1)}, u32[]{:S(2)}, u32[]{:S(2)}) collective-permute-start(bf16[16,16,256]{2,1,0:T(8,128)(2,1)S(1)} %get-tuple-element.59.refs_4_), channel_id=1, source_target_pairs={{0,1},{1,0},{2,3},{3,2},{4,5},{5,4},{6,7},{7,6},{8,9},{9,8},{10,11... | collective-permute-start | bytes 393224 | tf_op jit(solution)/shard_map/ppermute | solution.py:406
  70.3 11.6 %collective-permute-start.33 = (bf16[32,16,256]{2,1,0:T(8,128)(2,1)S(1)}, bf16[32,16,256]{2,1,0:T(8,128)(2,1)S(1)}, u32[]{:S(2)}, u32[]{:S(2)}) collective-permute-start(bf16[32,16,256]{2,1,0:T(8,128)(2,1)S(1)} %mode_sums.7), channel_id=1, source_target_pairs={{0,12},{2,14},{4,0},{6,2},{8,4},{10,6},{12,8},{14,10},{1,13},{3,15... | collective-permute-start | bytes 786440 | tf_op jit(solution)/shard_map/ppermute | solution.py:411
  73.7 13.4 %copy-start.4 = (bf16[8,2,256,256]{3,2,1,0:T(8,128)(2,1)S(1)}, bf16[8,2,256,256]{3,2,1,0:T(8,128)(2,1)}, u32[]{:S(2)}) copy-start(bf16[8,2,256,256]{3,2,1,0:T(8,128)(2,1)} %get-tuple-element.69.grad_ref) | copy-start | bytes 6291460
  73.7 11.0 %collective-permute-start.32 = (bf16[32,16,256]{2,1,0:T(8,128)(2,1)S(1)}, bf16[32,16,256]{2,1,0:T(8,128)(2,1)S(1)}, u32[]{:S(2)}, u32[]{:S(2)}) collective-permute-start(bf16[32,16,256]{2,1,0:T(8,128)(2,1)S(1)} %add_convert_fusion), channel_id=1, source_target_pairs={{0,4},{2,6},{4,8},{6,10},{8,12},{10,14},{12,0},{14,2},{1,5},{3,7},... | collective-permute-start | bytes 786440 | tf_op jit(solution)/shard_map/ppermute | solution.py:411
  75.1 5.0 %collective-permute-start.22 = (bf16[16,16,256]{2,1,0:T(8,128)(2,1)S(1)}, bf16[16,16,256]{2,1,0:T(8,128)(2,1)S(1)}, u32[]{:S(2)}, u32[]{:S(2)}) collective-permute-start(bf16[16,16,256]{2,1,0:T(8,128)(2,1)S(1)} %get-tuple-element.58.refs_0_), channel_id=1, source_target_pairs={{0,2},{2,0},{4,6},{6,4},{8,10},{10,8},{12,14},{14,12},{1,3},{3,1},... | collective-permute-start | bytes 393224 | tf_op jit(solution)/shard_map/ppermute | solution.py:416
  75.6 5.9 %collective-permute-start.27 = (bf16[16,16,256]{2,1,0:T(8,128)(2,1)S(1)}, bf16[16,16,256]{2,1,0:T(8,128)(2,1)S(1)}, u32[]{:S(2)}, u32[]{:S(2)}) collective-permute-start(bf16[16,16,256]{2,1,0:T(8,128)(2,1)S(1)} %collective-permute-done.23), channel_id=1, source_target_pairs={{0,2},{2,0},{4,6},{6,4},{8,10},{10,8},{12,14},{14,12},{1,3},{3,1},... | collective-permute-start | bytes 393224 | tf_op jit(solution)/shard_map/ppermute | solution.py:416
  85.5 1.2 %collective-permute-start.34 = (f32[2,16,16]{2,1,0:T(8,128)S(1)}, f32[2,16,16]{2,1,0:T(8,128)S(1)}, u32[]{:S(2)}, u32[]{:S(2)}) collective-permute-start(f32[2,16,16]{2,1,0:T(8,128)S(1)} %get-tuple-element.67), channel_id=1, source_target_pairs={{0,1},{1,0},{2,3},{3,2},{4,5},{5,4},{6,7},{7,6},{8,9},{9,8},{10,11... | collective-permute-start | bytes 6152 | tf_op jit(solution)/shard_map/ppermute | solution.py:406
  86.7 4.9 %collective-permute-start.35 = (f32[2,16,16]{2,1,0:T(8,128)S(1)}, f32[2,16,16]{2,1,0:T(8,128)S(1)}, u32[]{:S(2)}, u32[]{:S(2)}) collective-permute-start(f32[2,16,16]{2,1,0:T(8,128)S(1)} %add.75), channel_id=1, source_target_pairs={{0,2},{2,0},{4,6},{6,4},{8,10},{10,8},{12,14},{14,12},{1,3},{3,1},... | collective-permute-start | bytes 6152 | tf_op jit(solution)/shard_map/ppermute | solution.py:522
  91.6 8.6 %collective-permute-start.36 = (f32[2,320,384]{2,1,0:T(8,128)S(1)}, f32[2,320,384]{2,1,0:T(8,128)S(1)}, u32[]{:S(2)}, u32[]{:S(2)}) collective-permute-start(f32[2,320,384]{2,1,0:T(8,128)S(1)} %get-tuple-element.73), channel_id=1, source_target_pairs={{0,1},{1,0},{2,3},{3,2},{4,5},{5,4},{6,7},{7,6},{8,9},{9,8},{10,11... | collective-permute-start | bytes 2949128 | tf_op jit(solution)/shard_map/ppermute | solution.py:406
  91.7 3.8 %collective-permute-start.37 = (f32[2,16,16]{2,1,0:T(8,128)S(1)}, f32[2,16,16]{2,1,0:T(8,128)S(1)}, u32[]{:S(2)}, u32[]{:S(2)}) collective-permute-start(f32[2,16,16]{2,1,0:T(8,128)S(1)} %add.78), channel_id=1, source_target_pairs={{0,4},{2,6},{4,0},{6,2},{8,12},{10,14},{12,8},{14,10},{1,5},{3,7},... | collective-permute-start | bytes 6152 | tf_op jit(solution)/shard_map/ppermute | solution.py:522
  95.5 4.7 %collective-permute-start.38 = (f32[2,16,16]{2,1,0:T(8,128)S(1)}, f32[2,16,16]{2,1,0:T(8,128)S(1)}, u32[]{:S(2)}, u32[]{:S(2)}) collective-permute-start(f32[2,16,16]{2,1,0:T(8,128)S(1)} %add.79), channel_id=1, source_target_pairs={{0,8},{2,10},{4,12},{6,14},{8,0},{10,2},{12,4},{14,6},{1,9},{3,11}... | collective-permute-start | bytes 6152 | tf_op jit(solution)/shard_map/ppermute | solution.py:522
  (4 other events, 32.2 us)

commit v3 on v2

--- a/solution.py
+++ b/solution.py
@@ -11,6 +11,7 @@
 OBJ_STEP = 0.125
 PROBE_STEP = 0.5
 RB = 16
+DEPTH = 3
 f32 = jnp.float32
 bf16 = jnp.bfloat16
 HI = lax.Precision.HIGHEST
@@ -53,11 +54,12 @@
     )(tables)
 
 
-def cut_kernel(sel_ref, row_ref, col_ref, obj_ref, out_ref):
-    spot = pl.program_id(0)
+def cut_kernel(meta_ref, owner_ref, row_ref, col_ref, obj_ref, out_ref):
+    spot = pl.program_id(0) + meta_ref[0] * pl.num_programs(0)
     length = out_ref.shape[2]
     height, width = obj_ref.shape[2:]
-    row_at, col_at, sel = row_ref[spot], col_ref[spot], sel_ref[spot]
+    row_at, col_at = row_ref[spot], col_ref[spot]
+    sel = (owner_ref[spot] != meta_ref[0]).astype(jnp.int32)
     rows = (iota((length, height), 1) == iota((length, height), 0) + row_at).astype(bf16)
     cols = (iota((width, length), 0) == iota((width, length), 1) + col_at).astype(bf16)
     for part in range(2):
@@ -65,10 +67,9 @@
         out_ref[0, part] = jnp.dot(band, cols, preferred_element_type=f32).astype(bf16)
 
 
-def cut_patches(obj_pair, sel, row_at, col_at, length):
-    cap = sel.shape[0]
+def cut_patches(obj_pair, scalars, cap, length):
     grid_spec = pltpu.PrefetchScalarGridSpec(
-        num_scalar_prefetch=3,
+        num_scalar_prefetch=4,
         grid=(cap,),
         in_specs=[pl.BlockSpec(obj_pair.shape, lambda i, *_: (0, 0, 0, 0))],
         out_specs=pl.BlockSpec((1, 2, length, length), lambda i, *_: (i, 0, 0, 0)),
@@ -80,18 +81,27 @@
         compiler_params=pltpu.CompilerParams(vmem_limit_bytes=12 << 20),
         cost_estimate=pl.CostEstimate(flops=4 << 30, bytes_accessed=4 << 20, transcendentals=0),
         name="cut_patches",
-    )(sel, row_at, col_at, obj_pair)
+    )(*scalars, obj_pair)
 
 
 STEPS = (0, 2, 3, 1)
 
 
-def relax_kernel(tab_ref, live_ref, mix_ref, *refs):
+def place_of(meta_ref, j):
     count = len(STEPS)
+    side, far_side, place = j // (2 * count), j // count % 2, j % count
+    z, y, first = meta_ref[1], meta_ref[2], meta_ref[3]
+    strip = 2 * ((z + STEPS[place]) % count) + (1 - y if far_side else y)
+    return 2 * strip + (1 - first if side else first)
+
+
+def relax_kernel(meta_ref, live_ref, mix_ref, *refs):
+    count = len(STEPS)
+    tab = [place_of(meta_ref, j) for j in range(4 * count)]
     blocks, refs = refs[:4 * count], refs[4 * count:]
     patch_ref, amp_ref, fwd_ref, inv_ref, keep0_ref, keep1_ref = refs[:6]
     cross0, cross1 = refs[6:6 + count], refs[6 + count:6 + 2 * count]
-    grad_ref, stash_ref, probe_ref, new_ref = refs[6 + 2 * count:]
+    grad_r_ref, grad_i_ref, stash_ref, probe_ref, new_ref, stash_sem = refs[6 + 2 * count:]
     group = pl.program_id(0)
     each = patch_ref.shape[0]
     length = patch_ref.shape[2]
@@ -102,15 +112,16 @@
         for j, block_ref in enumerate(blocks):
             block = block_ref[...].reshape(block_ref.shape[0] * RB, length)
             mixed = jnp.dot(mix, block, preferred_element_type=f32)
-            at = pl.multiple_of(tab_ref[j] * RB, RB)
+            at = pl.multiple_of(tab[j] * RB, RB)
             probe_ref[:, pl.ds(at, RB), :] = mixed.reshape(mixed.shape[0] // RB, RB, length)
 
-    share = stash_ref.shape[0]
-    for turn_at in range(len(blocks) // share):
-        @pl.when(group == turn_at)
-        def _(turn_at=turn_at):
-            for i in range(share):
-                stash_ref[i] = blocks[share * turn_at + i][...]
+    def stashing(j):
+        return pltpu.make_async_copy(blocks[j], stash_ref.at[j], stash_sem.at[j])
+
+    @pl.when(group == 0)
+    def _():
+        for j in range(len(blocks)):
+            stashing(j).start()
 
     def planes(q):
         spot = each * group + q
@@ -141,12 +152,12 @@
         return (far_r * scale).astype(bf16), (far_i * scale).astype(bf16)
 
     def update(q, exits, near):
-        live = (each * group + q < live_ref[0]).astype(f32)
+        live = (each * group + q < live_ref[meta_ref[0]]).astype(f32)
         probe_r, probe_i, obj_r, obj_i = planes(q)
         delta_r = near[:, :length] - exits[0].astype(f32)
         delta_i = near[:, length:] - exits[1].astype(f32)
-        grad_ref[q, 0] = ((probe_r * delta_r + probe_i * delta_i) * live).astype(bf16)
-        grad_ref[q, 1] = ((probe_r * delta_i - probe_i * delta_r) * live).astype(bf16)
+        grad_r_ref[q] = ((probe_r * delta_r + probe_i * delta_i) * live).astype(bf16)
+        grad_i_ref[q] = ((probe_r * delta_i - probe_i * delta_r) * live).astype(bf16)
         change_r = obj_r * delta_r + obj_i * delta_i
         change_i = obj_r * delta_i - obj_i * delta_r
         for part, value in ((0, probe_r + PROBE_STEP * change_r), (1, probe_i + PROBE_STEP * change_i)):
@@ -158,8 +169,13 @@
     near = cols_pass(fwd_ref, rows_pass(inv_ref, revised))
     for q in range(each):
         update(q, exits[q], near[q])
+    @pl.when(group == pl.num_programs(0) - 1)
+    def _():
+        for j in range(len(blocks)):
+            stashing(j).wait()
+
     for j in range(4 * count):
-        at = tab_ref[j]
+        at = tab[j]
         side, far_side, place = j // (2 * count), j // count % 2, j % count
         for row in range(2 * each):
             if far_side:
@@ -172,27 +188,28 @@
     return pl.BlockSpec(arr.shape, lambda *_: (0,) * arr.ndim)
 
 
-def relax(tab, live, mix, blocks, patches, amplitude, forward, inverse):
+def relax(meta, live, mix, blocks, patches, amplitude, forward, inverse):
     cap, _, length, _ = patches.shape
     count = len(STEPS)
     each = 4 if cap % 4 == 0 else 1
-    share = len(blocks) * each // cap
     plane = pl.BlockSpec((each, 2, length, length), lambda i, *_: (i, 0, 0, 0))
     strips = pl.BlockSpec((count, 2 * each, RB, length), lambda i, *_: (0, i, 0, 0))
     strip = pl.BlockSpec((2 * each, RB, length), lambda i, *_: (i, 0, 0))
+    flat = pl.BlockSpec((each, length, length), lambda i, *_: (i, 0, 0))
     grid_spec = pltpu.PrefetchScalarGridSpec(
         num_scalar_prefetch=2,
         grid=(cap // each,),
         in_specs=[
             whole(mix), *[whole(block) for block in blocks], plane,
-            pl.BlockSpec((each, length, length), lambda i, *_: (i, 0, 0)),
+            flat,
             whole(forward), whole(inverse),
         ],
-        out_specs=[strips, strips, *[strip] * (2 * count), plane,
-                   pl.BlockSpec((share,) + blocks[0].shape, lambda i, *_: (i, 0, 0, 0))],
+        out_specs=[strips, strips, *[strip] * (2 * count), flat, flat,
+                   pl.BlockSpec(memory_space=pl.ANY)],
         scratch_shapes=[
             pltpu.VMEM((2 * cap, length, length), f32),
             pltpu.VMEM((2 * each, 4 * count, RB, length), bf16),
+            pltpu.SemaphoreType.DMA((len(blocks),)),
         ],
     )
     many = jax.ShapeDtypeStruct((count, 2 * cap, RB, length), bf16)
@@ -201,53 +218,54 @@
         relax_kernel,
         grid_spec=grid_spec,
         out_shape=[many, many, *[single] * (2 * count),
-                   pltpu.HBM((cap, 2, length, length), bf16),
+                   pltpu.HBM((cap, length, length), bf16),
+                   pltpu.HBM((cap, length, length), bf16),
                    pltpu.HBM((len(blocks),) + blocks[0].shape, bf16)],
         compiler_params=pltpu.CompilerParams(vmem_limit_bytes=28 << 20),
         cost_estimate=pl.CostEstimate(flops=8 << 30, bytes_accessed=16 << 20, transcendentals=1 << 19),
         name="relax_positions",
-    )(tab, live.reshape(1), mix, *blocks, patches, amplitude, forward, inverse)
-    return (outs[0], outs[1], outs[2:2 + count], outs[2 + count:2 + 2 * count]), outs[-2], outs[-1]
-
-
-def settle_kernel(sel_ref, row_ref, col_ref, grad_ref, mine_ref, other_ref, band_ref):
-    cap, _, length, _ = grad_ref.shape
-    height, width = mine_ref.shape[1:]
+    )(meta, live, mix, *blocks, patches, amplitude, forward, inverse)
+    return (outs[0], outs[1], outs[2:2 + count], outs[2 + count:2 + 2 * count]), outs[-3:-1], outs[-1]
+
+
+def settle_kernel(meta_ref, owner_ref, row_ref, col_ref, grad_ref, mine_ref, other_ref, band_ref):
+    cap, length, _ = grad_ref.shape
+    height, width = mine_ref.shape
     places = []
     for spot in range(cap):
-        row_at, col_at, sel = row_ref[spot], col_ref[spot], sel_ref[spot]
+        at = spot + meta_ref[0] * cap
+        row_at, col_at = row_ref[at], col_ref[at]
+        sel = (owner_ref[at] != meta_ref[0]).astype(jnp.int32)
         cols = (iota((length, width), 1) == iota((length, width), 0) + col_at).astype(bf16)
-        for part in range(2):
-            band = jnp.dot(grad_ref[spot, part], cols, preferred_element_type=f32)
-            band_ref[spot * length:(spot + 1) * length, part * width:(part + 1) * width] = band.astype(bf16)
+        band = jnp.dot(grad_ref[spot], cols, preferred_element_type=f32)
+        band_ref[spot * length:(spot + 1) * length] = band.astype(bf16)
         place = iota((2 * height, length), 1) + row_at + height * sel
         places.append((iota((2 * height, length), 0) == place).astype(bf16))
     places = jnp.concatenate(places, axis=1)
-    for part in range(2):
-        total = jnp.dot(places, band_ref[:, part * width:(part + 1) * width], preferred_element_type=f32)
-        mine_ref[part] = total[:height]
-        other_ref[part] = total[height:]
-
-
-def settle(sel, row_at, col_at, grads, height, width):
-    cap, _, length, _ = grads.shape
-    tile = pl.BlockSpec((2, height, width), lambda *_: (0, 0, 0))
+    total = jnp.dot(places, band_ref[...], preferred_element_type=f32)
+    mine_ref[...] = total[:height]
+    other_ref[...] = total[height:]
+
+
+def settle(scalars, grads, height, width):
+    cap, length, _ = grads.shape
+    tile = pl.BlockSpec((height, width), lambda *_: (0, 0))
     grid_spec = pltpu.PrefetchScalarGridSpec(
-        num_scalar_prefetch=3,
+        num_scalar_prefetch=4,
         grid=(1,),
         in_specs=[whole(grads)],
         out_specs=[tile, tile],
-        scratch_shapes=[pltpu.VMEM((cap * length, 2 * width), bf16)],
+        scratch_shapes=[pltpu.VMEM((cap * length, width), bf16)],
     )
-    shape = jax.ShapeDtypeStruct((2, height, width), f32)
+    shape = jax.ShapeDtypeStruct((height, width), f32)
     return pl.pallas_call(
         settle_kernel,
         grid_spec=grid_spec,
         out_shape=[shape, shape],
         compiler_params=pltpu.CompilerParams(vmem_limit_bytes=20 << 20),
-        cost_estimate=pl.CostEstimate(flops=4 << 30, bytes_accessed=4 << 20, transcendentals=0),
+        cost_estimate=pl.CostEstimate(flops=2 << 30, bytes_accessed=4 << 20, transcendentals=0),
         name="settle",
-    )(sel, row_at, col_at, grads)
+    )(*scalars, grads)
 
 
 def weights_kernel(keep0_ref, keep1_ref, *refs):
@@ -385,7 +403,14 @@
     full = jnp.concatenate([
         jnp.concatenate([back_r, -back_i], axis=1),
         jnp.concatenate([back_i, back_r], axis=1)], axis=0)
-    out_ref[...] = jnp.dot(full, sum_ref[...], precision=HI, preferred_element_type=f32)
+    full_top = full.astype(bf16)
+    full_rest = (full - full_top.astype(f32)).astype(bf16)
+    flat = sum_ref[...]
+    flat_top = flat.astype(bf16)
+    flat_rest = (flat - flat_top.astype(f32)).astype(bf16)
+    left = jnp.concatenate([full_top, full_top, full_rest], axis=1)
+    right = jnp.concatenate([flat_top, flat_rest, flat_top], axis=0)
+    out_ref[...] = jnp.dot(left, right, preferred_element_type=f32)
 
 
 def new_modes_of(gram, summed, norm):
@@ -418,13 +443,6 @@
 
 def after(value, *others):
     return lax.optimization_barrier((value, *others))[0]
-
-
-def places(z, y, tile):
-    steps = jnp.array(STEPS, jnp.int32)
-    strips = 2 * ((z + steps) % len(STEPS))
-    strips = jnp.concatenate([strips + y, strips + 1 - y])
-    return jnp.concatenate([2 * strips + tile, 2 * strips + 1 - tile]).astype(jnp.int32)
 
 
 def gather_blocks(own, obj_b, cut, ready):
@@ -472,9 +490,8 @@
     far, far_twin, line = {}, {}, []
     for step in order:
         for value, dest in ((cross0[at[step]], far), (twin_cross[step], far_twin)):
-            dest[step] = across(after(value, line[-3]) if len(line) >= 3 else value)
+            dest[step] = across(after(value, line[-DEPTH]) if len(line) >= DEPTH else value)
             line.append(dest[step])
-
     def part(step, kind):
         return pair_sums(at[step], wide, keep0, twin, far[step], far_twin[step], kind)
 
@@ -521,9 +538,9 @@
     while step < count:
         come = lax.ppermute(value, "scan", [(i, i ^ step) for i in range(count)])
         step *= 2
-        if works and step < count:
-            results.append(works.pop(0)(value, results))
-            value, come, results[-1] = lax.optimization_barrier((value, come, results[-1]))
+        if works:
+            value, come, result = lax.optimization_barrier((value, come, works.pop(0)(value)))
+            results.append(result)
         value = value + come
     return value, results
 
@@ -540,44 +557,40 @@
     rows = length // devices
     forward, inverse = transform_tables(length)
 
-    def mine(value):
-        return lax.dynamic_slice_in_dim(value, tile * cap, cap)
-
-    owner, row_at, col_at = mine(tile_owner), mine(corner_row), mine(corner_col)
-    sel = jnp.where(owner == tile, 0, 1).astype(jnp.int32)
-    live_n = lax.dynamic_index_in_dim(slot_count, tile, 0, keepdims=False)
-
     own = probe_modes.astype(bf16).reshape(2 * count, rows, length)
     obj_b = object_field.astype(bf16)
     weights_b = weights.astype(bf16)
     planned = lax.axis_size("scan") == 8 and n_tile == 2 and rows == RB
 
+    scan = lax.axis_index("scan")
+    zero = jnp.zeros_like(scan)
+    meta = jnp.stack([tile, scan // 2, scan % 2, tile] if planned else [tile, zero, zero, zero])
+    meta = meta.astype(jnp.int32)
+    scalars = (meta, tile_owner, corner_row, corner_col)
+
     def cut(obj_pair):
-        return cut_patches(obj_pair, sel, row_at, col_at, length)
-
-    scan = lax.axis_index("scan")
-    tab = places(scan // 2, scan % 2, tile) if planned else places(0, 0, 0)
+        return cut_patches(obj_pair, scalars, cap, length)
+
     wt_r, wt_i = weights_b[0], weights_b[1]
     mix = jnp.stack([jnp.concatenate([wt_r, -wt_i], axis=1),
                      jnp.concatenate([wt_i, wt_r], axis=1)], axis=1)
     mix = widen(mix.reshape(1, 2 * cap, 2 * count))
-    blocks, patches, (tab, mix, live_n, forward, inverse) = (gather_blocks if planned else gather_any)(
-        own, obj_b, cut, (tab, mix, live_n, forward, inverse))
-    updated, grads, stash = relax(tab, live_n, mix, blocks, patches, amplitude, forward, inverse)
+    blocks, patches, (mix, forward, inverse) = (gather_blocks if planned else gather_any)(
+        own, obj_b, cut, (mix, forward, inverse))
+    updated, grads, stash = relax(meta, slot_count, mix, blocks, patches, amplitude, forward, inverse)
+
+    def put_back(part):
+        return lambda token: settle(scalars, after(grads[part], token), *object_field.shape[1:])
 
     summed, gram = (scatter_sums if planned else scatter_any)(weights_b, updated, blocks)
 
-    def put_back(token, _):
-        mine_sum, other_sum = settle(sel, row_at, col_at, after(grads, token), *object_field.shape[1:])
-        return mine_sum, other_sum
-
-    def project(token, _):
+    def project(token):
         keep0, keep1, cross0, cross1 = updated
         return new_weights_of((after(keep0, token), keep1, cross0, cross1), stash)
 
-    gram, (object_sums, new_weights) = sum_everywhere(gram, [put_back, project])
-    new_object = object_field + OBJ_STEP * (object_sums[0] + swap_tiles(object_sums[1]))
-    gram = after(gram, new_object)
+    gram, (real, imag, new_weights) = sum_everywhere(gram, [put_back(0), put_back(1), project])
+    steps = [mine_sum + swap_tiles(other_sum) for mine_sum, other_sum in (real, imag)]
+    new_object = object_field + OBJ_STEP * jnp.stack(steps)
     new_modes = new_modes_of(gram, summed, math.sqrt(pixels)).reshape(probe_modes.shape)
     return (new_object, new_modes, new_weights)
 

time: 105 us -> 103 us (0.981)
    ppermute x3, waiting for transfers between devices: 3.59 us -> 2.31 us  [sum_everywhere(): come = lax.ppermute(value, 'scan', [(i, i ^ step) for i in range(count)])]
    pallas_call x1, Pallas kernels: 11.2 us -> 10 us  [relax(): pl.pallas_call(relax_kernel, grid_spec=grid_spec, out_shape=[many, many,...]
    pallas_call x1 -> x2, Pallas kernels: 4.57 us -> 5.24 us  [settle(): pl.pallas_call(settle_kernel, grid_spec=grid_spec, out_shape=[shape, shap...]
    ppermute x17 -> x18, waiting for transfers between devices: 5.48 us -> 5.9 us  [swap_tiles(): lax.ppermute(value, 'tile', [(i, (i + 1) % count) for i in range(count)])]
    ppermute x17 -> x18, starting transfers between devices: 2.21 us -> 2.24 us  [swap_tiles(): lax.ppermute(value, 'tile', [(i, (i + 1) % count) for i in range(count)])]
  transfers between devices with their start and end apart: 39 -> 40, of which waited for: 19 -> 20; matrix products, arithmetic and copies ran while one was open for 4% -> 4% of each run, Pallas kernels for 16% -> 20%
where the time goes in v3:
time: 103 us
  waiting for transfers between devices  36.1 us (35%)
  Pallas kernels  31.5 us (31%)
  starting transfers between devices  28 us (27%)
  other arithmetic  5.77 us (6%)
  between operations  1.08 us (1%)
    ppermute x13, waiting for transfers between devices, across(): return lax.ppermute(value, 'scan', [(i, i ^ 1) for i in range(count)])  18.3 us
    ppermute x13, starting transfers between devices, across(): return lax.ppermute(value, 'scan', [(i, i ^ 1) for i in range(count)])  13.4 us
    ppermute x6, starting transfers between devices, turn(): lax.ppermute(value, 'scan', [(i, (i + 2 * step) % count) for i in range(c...  10.5 us
    pallas_call x1, Pallas kernels, relax(): pl.pallas_call(relax_kernel, grid_spec=grid_spec, out_shape=[many, many,...  10 us
    ppermute x6, waiting for transfers between devices, turn(): lax.ppermute(value, 'scan', [(i, (i + 2 * step) % count) for i in range(c...  9.67 us
    pallas_call x1, Pallas kernels, cut_patches(): pl.pallas_call(cut_kernel, grid_spec=grid_spec, out_shape=jax.ShapeDtypeS...  6.17 us
    ppermute x18, waiting for transfers between devices, swap_tiles(): lax.ppermute(value, 'tile', [(i, (i + 1) % count) for i in range(count)])  5.9 us
    pallas_call x2, Pallas kernels, settle(): pl.pallas_call(settle_kernel, grid_spec=grid_spec, out_shape=[shape, shap...  5.24 us
  transfers between devices with their start and end apart: 40, of which 20 were waited for; matrix products, arithmetic and copies ran while one was open for 4% of the time, Pallas kernels for 20%

profile of v3, /device:TPU:0, one launch (start us, length us, event | category | flops | bytes accessed | tf_op | source)
XLA Modules:
  0.0 102.8 jit_solution(2939768602157961904)
XLA Ops:
  0.7 1.1 %convert_element_type.17 = bf16[2,16,4096]{2,1,0:T(8,128)(2,1)S(1)} convert(f32[2,16,4096]{2,1,0:T(8,128)} %param.11) | non-fusion elementwise | flops 131072 | bytes 786432 | tf_op jit(solution)/shard_map/convert_element_type | solution.py:560
  1.9 3.1 %collective-permute-start.2 = (bf16[32,16,256]{2,1,0:T(8,128)(2,1)S(1)}, bf16[32,16,256]{2,1,0:T(8,128)(2,1)S(1)}, u32[]{:S(2)}, u32[]{:S(2)}) collective-permute-start(bf16[32,16,256]{2,1,0:T(8,128)(2,1)S(1)} %bitcast.55), channel_id=1, source_target_pairs={{0,4},{2,6},{4,8},{6,10},{8,12},{10,14},{12,0},{14,2},{1,5},{3,7},... | collective-permute-start | bytes 786440 | tf_op jit(solution)/shard_map/ppermute | solution.py:436
  5.0 2.1 %collective-permute-start.3 = (bf16[32,16,256]{2,1,0:T(8,128)(2,1)S(1)}, bf16[32,16,256]{2,1,0:T(8,128)(2,1)S(1)}, u32[]{:S(2)}, u32[]{:S(2)}) collective-permute-start(bf16[32,16,256]{2,1,0:T(8,128)(2,1)S(1)} %bitcast.56), channel_id=1, source_target_pairs={{0,12},{2,14},{4,0},{6,2},{8,4},{10,6},{12,8},{14,10},{1,13},{3,15... | collective-permute-start | bytes 786440 | tf_op jit(solution)/shard_map/ppermute | solution.py:436
  7.0 1.7 %collective-permute-start.8 = (bf16[32,16,256]{2,1,0:T(8,128)(2,1)S(1)}, bf16[32,16,256]{2,1,0:T(8,128)(2,1)S(1)}, u32[]{:S(2)}, u32[]{:S(2)}) collective-permute-start(bf16[32,16,256]{2,1,0:T(8,128)(2,1)S(1)} %bitcast.57), channel_id=1, source_target_pairs={{0,2},{2,0},{4,6},{6,4},{8,10},{10,8},{12,14},{14,12},{1,3},{3,1},... | collective-permute-start | bytes 786440 | tf_op jit(solution)/shard_map/ppermute | solution.py:441
  8.7 1.3 %convert_element_type.16 = bf16[2,320,384]{2,1,0:T(8,128)(2,1)S(1)} convert(f32[2,320,384]{2,1,0:T(8,128)} %param.10) | non-fusion elementwise | flops 245760 | bytes 1474560 | tf_op jit(solution)/shard_map/convert_element_type | solution.py:561
  10.1 0.7 convert_element_type.15
  11.4 0.7 collective-permute-done.1
  12.0 1.1 %pad_maximum_fusion.obj_ref = bf16[2,2,320,384]{3,2,1,0:T(8,128)(2,1)S(1)} fusion(bf16[1,2,320,384]{3,2,1,0:T(8,128)(2,1)} %bitcast.6, bf16[1,2,320,384]{3,2,1,0:T(8,128)(2,1)S(1)} %convert_bitcast_fusion), kind=kLoop, calls=%fused_computation | loop fusion | flops 491520 | bytes 1966080 | tf_op jit(solution)/shard_map/stack | solution.py:451
  13.3 6.2 %cut_patches.1.refs_16_ = bf16[8,2,256,256]{3,2,1,0:T(8,128)(2,1)S(1)} custom-call(s32[4]{0:T(128)S(1)} %pad_add_fusion.meta_ref, s32[16]{0:T(128)S(1)} %copy-done.2, s32[16]{0:T(128)S(1)} %copy-done.3, s32[16]{0:T(128)S(1)} %copy-done.4, bf16[2,2,320,384]{3,2,1,0:T(8,128)(2,1)S(1)} %pad_maximum_fusion.obj_ref), custom_call_target="tpu_custom_call" | custom-call | flops 4294967296 | bytes 4194304 | tf_op jit(solution)/shard_map/cut_patches/pallas_call | solution.py:77
  19.6 1.4 %collective-permute-start.4 = (bf16[32,16,256]{2,1,0:T(8,128)(2,1)S(1)}, bf16[32,16,256]{2,1,0:T(8,128)(2,1)S(1)}, u32[]{:S(2)}, u32[]{:S(2)}) collective-permute-start(bf16[32,16,256]{2,1,0:T(8,128)(2,1)S(1)} %collective-permute-done.3.refs_3_), channel_id=1, source_target_pairs={{0,2},{2,0},{4,6},{6,4},{8,10},{10,8},{12,14},{14,12},{1,3},{3,1},... | collective-permute-start | bytes 786440 | tf_op jit(solution)/shard_map/ppermute | solution.py:441
  21.0 0.5 collective-permute-start.11
  21.5 0.6 collective-permute-done
  22.2 0.7 collective-permute-start.10
  22.8 6.9 %collective-permute-done.7.refs_1_ = bf16[32,16,256]{2,1,0:T(8,128)(2,1)S(1)} collective-permute-done((bf16[32,16,256]{2,1,0:T(8,128)(2,1)S(1)}, bf16[32,16,256]{2,1,0:T(8,128)(2,1)S(1)}, u32[]{:S(2)}, u32[]{:S(2)}) %collective-permute-start.7) | collective-permute-done | bytes 262176 | tf_op jit(solution)/shard_map/ppermute | solution.py:436
  30.1 1.5 %collective-permute-done.5.refs_15_ = bf16[32,16,256]{2,1,0:T(8,128)(2,1)S(1)} collective-permute-done((bf16[32,16,256]{2,1,0:T(8,128)(2,1)S(1)}, bf16[32,16,256]{2,1,0:T(8,128)(2,1)S(1)}, u32[]{:S(2)}, u32[]{:S(2)}) %collective-permute-start.5) | collective-permute-done | bytes 262176 | tf_op jit(solution)/shard_map/ppermute | solution.py:431
  31.6 1.7 %collective-permute-start.6 = (bf16[2,2,8,16]{3,2,1,0:T(8,128)(2,1)S(1)}, bf16[2,2,8,16]{3,2,1,0:T(8,128)(2,1)S(1)}, u32[]{:S(2)}, u32[]{:S(2)}) collective-permute-start(bf16[2,2,8,16]{3,2,1,0:T(8,128)(2,1)S(1)} %pad_maximum_fusion.1), channel_id=1, source_target_pairs={{0,2},{2,0},{4,6},{6,4},{8,10},{10,8},{12,14},{14,12},{1,3},{3,1},... | collective-permute-start | bytes 3080 | tf_op jit(solution)/shard_map/ppermute | solution.py:441
  33.8 0.6 collective-permute-done.10.refs_6_
  34.4 4.9 %collective-permute-done.9.refs_5_ = bf16[32,16,256]{2,1,0:T(8,128)(2,1)S(1)} collective-permute-done((bf16[32,16,256]{2,1,0:T(8,128)(2,1)S(1)}, bf16[32,16,256]{2,1,0:T(8,128)(2,1)S(1)}, u32[]{:S(2)}, u32[]{:S(2)}) %collective-permute-start.9) | collective-permute-done | bytes 262176 | tf_op jit(solution)/shard_map/ppermute | solution.py:441
  39.8 1.0 collective-permute-done.17.refs_14_
  41.2 10.0 %relax_positions.1 = (bf16[4,16,16,256]{3,2,1,0:T(8,128)(2,1)S(1)}, bf16[4,16,16,256]{3,2,1,0:T(8,128)(2,1)S(1)}, bf16[16,16,256]{2,1,0:T(8,128)(2,1)S(1)}, bf16...) custom-call(s32[4]{0:T(128)S(1)} %pad_add_fusion.meta_ref, ...), custom_call_target="tpu_custom_call" | custom-call | flops 8589934592 | bytes 16777216 | tf_op jit(solution)/shard_map/relax_positions/pallas_call | solution.py:217
  51.8 1.0 collective-permute-start.20
  52.9 0.5 collective-permute-done.24
  53.4 1.0 collective-permute-start.25
  54.6 1.1 %collective-permute-start.29 = (bf16[16,16,256]{2,1,0:T(8,128)(2,1)S(1)}, bf16[16,16,256]{2,1,0:T(8,128)(2,1)S(1)}, u32[]{:S(2)}, u32[]{:S(2)}) collective-permute-start(bf16[16,16,256]{2,1,0:T(8,128)(2,1)S(1)} %get-tuple-element.68.refs_2_), channel_id=1, source_target_pairs={{0,2},{2,0},{4,6},{6,4},{8,10},{10,8},{12,14},{14,12},{1,3},{3,1},... | collective-permute-start | bytes 393224 | tf_op jit(solution)/shard_map/ppermute | solution.py:441
  55.7 2.4 %collective-permute-done.20.far_ref = bf16[16,16,256]{2,1,0:T(8,128)(2,1)S(1)} collective-permute-done((bf16[16,16,256]{2,1,0:T(8,128)(2,1)S(1)}, bf16[16,16,256]{2,1,0:T(8,128)(2,1)S(1)}, u32[]{:S(2)}, u32[]{:S(2)}) %collective-permute-start.20) | collective-permute-done | bytes 131104 | tf_op jit(solution)/shard_map/ppermute | solution.py:441
  58.2 0.8 widen.3.wide_ref
  59.0 2.0 %collective-permute-done.25.far_twin_ref = bf16[16,16,256]{2,1,0:T(8,128)(2,1)S(1)} collective-permute-done((bf16[16,16,256]{2,1,0:T(8,128)(2,1)S(1)}, bf16[16,16,256]{2,1,0:T(8,128)(2,1)S(1)}, u32[]{:S(2)}, u32[]{:S(2)}) %collective-permute-start.25) | collective-permute-done | bytes 131104 | tf_op jit(solution)/shard_map/ppermute | solution.py:441
  61.4 1.0 %collective-permute-start.31 = (bf16[32,16,256]{2,1,0:T(8,128)(2,1)S(1)}, bf16[32,16,256]{2,1,0:T(8,128)(2,1)S(1)}, u32[]{:S(2)}, u32[]{:S(2)}) collective-permute-start(bf16[32,16,256]{2,1,0:T(8,128)(2,1)S(1)} %mode_sums.6), channel_id=1, source_target_pairs={{0,4},{2,6},{4,8},{6,10},{8,12},{10,14},{12,0},{14,2},{1,5},{3,7},... | collective-permute-start | bytes 786440 | tf_op jit(solution)/shard_map/ppermute | solution.py:436
  62.5 0.5 collective-permute-start.21
  63.0 1.5 %collective-permute-start.30 = (bf16[16,16,256]{2,1,0:T(8,128)(2,1)S(1)}, bf16[16,16,256]{2,1,0:T(8,128)(2,1)S(1)}, u32[]{:S(2)}, u32[]{:S(2)}) collective-permute-start(bf16[16,16,256]{2,1,0:T(8,128)(2,1)S(1)} %collective-permute-done.28), channel_id=1, source_target_pairs={{0,2},{2,0},{4,6},{6,4},{8,10},{10,8},{12,14},{14,12},{1,3},{3,1},... | collective-permute-start | bytes 393224 | tf_op jit(solution)/shard_map/ppermute | solution.py:441
  64.5 0.5 collective-permute-start.26
  65.0 3.8 %collective-permute-done.21.far_twin_ref = bf16[16,16,256]{2,1,0:T(8,128)(2,1)S(1)} collective-permute-done((bf16[16,16,256]{2,1,0:T(8,128)(2,1)S(1)}, bf16[16,16,256]{2,1,0:T(8,128)(2,1)S(1)}, u32[]{:S(2)}, u32[]{:S(2)}) %collective-permute-start.21) | collective-permute-done | bytes 131104 | tf_op jit(solution)/shard_map/ppermute | solution.py:441
  69.3 2.8 %collective-permute-start.33 = (bf16[32,16,256]{2,1,0:T(8,128)(2,1)S(1)}, bf16[32,16,256]{2,1,0:T(8,128)(2,1)S(1)}, u32[]{:S(2)}, u32[]{:S(2)}) collective-permute-start(bf16[32,16,256]{2,1,0:T(8,128)(2,1)S(1)} %mode_sums.7), channel_id=1, source_target_pairs={{0,12},{2,14},{4,0},{6,2},{8,4},{10,6},{12,8},{14,10},{1,13},{3,15... | collective-permute-start | bytes 786440 | tf_op jit(solution)/shard_map/ppermute | solution.py:436
  72.7 1.4 %collective-permute-start.32 = (bf16[32,16,256]{2,1,0:T(8,128)(2,1)S(1)}, bf16[32,16,256]{2,1,0:T(8,128)(2,1)S(1)}, u32[]{:S(2)}, u32[]{:S(2)}) collective-permute-start(bf16[32,16,256]{2,1,0:T(8,128)(2,1)S(1)} %add_convert_fusion), channel_id=1, source_target_pairs={{0,4},{2,6},{4,8},{6,10},{8,12},{10,14},{12,0},{14,2},{1,5},{3,7},... | collective-permute-start | bytes 786440 | tf_op jit(solution)/shard_map/ppermute | solution.py:436
  74.6 1.5 %collective-permute-start.27 = (bf16[16,16,256]{2,1,0:T(8,128)(2,1)S(1)}, bf16[16,16,256]{2,1,0:T(8,128)(2,1)S(1)}, u32[]{:S(2)}, u32[]{:S(2)}) collective-permute-start(bf16[16,16,256]{2,1,0:T(8,128)(2,1)S(1)} %collective-permute-done.23), channel_id=1, source_target_pairs={{0,2},{2,0},{4,6},{6,4},{8,10},{10,8},{12,14},{14,12},{1,3},{3,1},... | collective-permute-start | bytes 393224 | tf_op jit(solution)/shard_map/ppermute | solution.py:441
  76.1 2.9 %collective-permute-done.22.far_ref = bf16[16,16,256]{2,1,0:T(8,128)(2,1)S(1)} collective-permute-done((bf16[16,16,256]{2,1,0:T(8,128)(2,1)S(1)}, bf16[16,16,256]{2,1,0:T(8,128)(2,1)S(1)}, u32[]{:S(2)}, u32[]{:S(2)}) %collective-permute-start.22) | collective-permute-done | bytes 131104 | tf_op jit(solution)/shard_map/ppermute | solution.py:441
  79.1 1.4 %collective-permute-done.27.far_twin_ref = bf16[16,16,256]{2,1,0:T(8,128)(2,1)S(1)} collective-permute-done((bf16[16,16,256]{2,1,0:T(8,128)(2,1)S(1)}, bf16[16,16,256]{2,1,0:T(8,128)(2,1)S(1)}, u32[]{:S(2)}, u32[]{:S(2)}) %collective-permute-start.27) | collective-permute-done | bytes 131104 | tf_op jit(solution)/shard_map/ppermute | solution.py:441
  80.9 2.8 %collective-permute-done.32.refs_1_ = bf16[32,16,256]{2,1,0:T(8,128)(2,1)S(1)} collective-permute-done((bf16[32,16,256]{2,1,0:T(8,128)(2,1)S(1)}, bf16[32,16,256]{2,1,0:T(8,128)(2,1)S(1)}, u32[]{:S(2)}, u32[]{:S(2)}) %collective-permute-start.32) | collective-permute-done | bytes 262176 | tf_op jit(solution)/shard_map/ppermute | solution.py:436
  83.7 0.8 finish_sums.1
  84.6 1.2 %collective-permute-done.34 = f32[2,16,16]{2,1,0:T(8,128)S(1)} collective-permute-done((f32[2,16,16]{2,1,0:T(8,128)S(1)}, f32[2,16,16]{2,1,0:T(8,128)S(1)}, u32[]{:S(2)}, u32[]{:S(2)}) %collective-permute-start.34) | collective-permute-done | bytes 2080 | tf_op jit(solution)/shard_map/ppermute | solution.py:431
  86.1 2.6 %settle.2 = (f32[320,384]{1,0:T(8,128)S(1)}, f32[320,384]{1,0:T(8,128)S(1)}) custom-call(s32[4]{0:T(128)S(1)} %pad_add_fusion.meta_ref, s32[16]{0:T(128)S(1)} %copy-done.2, s32[16]{0:T(128)S(1)} %copy-done.3, s32[16]{0:T(128)S(1)} %copy-done.4, bf16[8,256,256]{2,1,0:T(8,128)(2,1)S(1)} %copy-done.9), custom_call_target="tpu_custom_call" | custom-call | flops 2147483648 | bytes 4194304 | tf_op jit(solution)/shard_map/settle/pallas_call | solution.py:261
  88.7 0.8 collective-permute-done.35
  89.6 2.6 %settle.3 = (f32[320,384]{1,0:T(8,128)S(1)}, f32[320,384]{1,0:T(8,128)S(1)}) custom-call(s32[4]{0:T(128)S(1)} %pad_add_fusion.meta_ref, s32[16]{0:T(128)S(1)} %copy-done.2, s32[16]{0:T(128)S(1)} %copy-done.3, s32[16]{0:T(128)S(1)} %copy-done.4, bf16[8,256,256]{2,1,0:T(8,128)(2,1)S(1)} %copy-done.8), custom_call_target="tpu_custom_call" | custom-call | flops 2147483648 | bytes 4194304 | tf_op jit(solution)/shard_map/settle/pallas_call | solution.py:261
  92.2 1.1 %collective-permute-done.37 = f32[2,16,16]{2,1,0:T(8,128)S(1)} collective-permute-done((f32[2,16,16]{2,1,0:T(8,128)S(1)}, f32[2,16,16]{2,1,0:T(8,128)S(1)}, u32[]{:S(2)}, u32[]{:S(2)}) %collective-permute-start.37) | collective-permute-done | bytes 2080 | tf_op jit(solution)/shard_map/ppermute | solution.py:539
  93.3 1.4 %collective-permute-start.39 = (f32[2,16,16]{2,1,0:T(8,128)S(1)}, f32[2,16,16]{2,1,0:T(8,128)S(1)}, u32[]{:S(2)}, u32[]{:S(2)}) collective-permute-start(f32[2,16,16]{2,1,0:T(8,128)S(1)} %add.36), channel_id=1, source_target_pairs={{0,8},{2,10},{4,12},{6,14},{8,0},{10,2},{12,4},{14,6},{1,9},{3,11}... | collective-permute-start | bytes 6152 | tf_op jit(solution)/shard_map/ppermute | solution.py:539
  94.7 2.9 %new_weights.1 = f32[2,8,16]{2,1,0:T(8,128)} custom-call(bf16[4,16,16,256]{3,2,1,0:T(8,128)(2,1)S(1)} %get-tuple-element.87.near_ref.keep0_ref, bf16[4,16,16,256]{3,2,1,0:T(8,128)(2,1)S(1)} %get-tuple-element.56.keep1_ref, bf16[16,16,256]{2,1,0:T(8,128)(2,1)S(1)} %get-tuple-element.61.refs_0_, bf16[16,16,256]{2,1,0:T(8,128)(2,1)S(1)} %get-tuple-element.59.refs_1_, ...), custom_call_target="tpu_custom_call" | custom-call | flops 2147483648 | bytes 6291456 | tf_op jit(solution)/shard_map/new_weights/pallas_call | solution.py:311
  98.1 3.6 %orthonormal_modes.1 = f32[32,4096]{1,0:T(8,128)} custom-call(f32[2,16,16]{2,1,0:T(8,128)S(1)} %add.37.gram_ref, f32[32,4096]{1,0:T(8,128)S(1)} %get-tuple-element.91.sum_ref), custom_call_target="tpu_custom_call" | custom-call | flops 134217728 | bytes 1048576 | tf_op jit(solution)/shard_map/orthonormal_modes/pallas_call | solution.py:420
  101.8 1.0 %fusion = f32[2,320,384]{2,1,0:T(8,128)} fusion(f32[2,320,384]{2,1,0:T(8,128)S(1)} %copy-done.11, f32[1,320,384]{2,1,0:T(8,128)S(1)} %add_bitcast_fusion, f32[1,320,384]{2,1,0:T(8,128)S(1)} %add_bitcast_fusion.1), kind=kLoop, calls=%fused_computation.2 | loop fusion | flops 737280 | bytes 2949120 | tf_op jit(solution)/shard_map/add | solution.py:593
  (102 shorter events, 7.0 us)
Async XLA Ops:
  0.6 12.5 %copy-start.2 = (s32[16]{0:T(128)S(1)}, s32[16]{0:T(128)}, u32[]{:S(2)}) copy-start(s32[16]{0:T(128)} %owner_ref.5) | copy-start | bytes 196
  0.7 12.5 %copy-start.3 = (s32[16]{0:T(128)S(1)}, s32[16]{0:T(128)}, u32[]{:S(2)}) copy-start(s32[16]{0:T(128)} %row_ref.5) | copy-start | bytes 196
  1.9 17.6 %collective-permute-start.2 = (bf16[32,16,256]{2,1,0:T(8,128)(2,1)S(1)}, bf16[32,16,256]{2,1,0:T(8,128)(2,1)S(1)}, u32[]{:S(2)}, u32[]{:S(2)}) collective-permute-start(bf16[32,16,256]{2,1,0:T(8,128)(2,1)S(1)} %bitcast.55), channel_id=1, source_target_pairs={{0,4},{2,6},{4,8},{6,10},{8,12},{10,14},{12,0},{14,2},{1,5},{3,7},... | collective-permute-start | bytes 786440 | tf_op jit(solution)/shard_map/ppermute | solution.py:436
  5.0 14.5 %collective-permute-start.3 = (bf16[32,16,256]{2,1,0:T(8,128)(2,1)S(1)}, bf16[32,16,256]{2,1,0:T(8,128)(2,1)S(1)}, u32[]{:S(2)}, u32[]{:S(2)}) collective-permute-start(bf16[32,16,256]{2,1,0:T(8,128)(2,1)S(1)} %bitcast.56), channel_id=1, source_target_pairs={{0,12},{2,14},{4,0},{6,2},{8,4},{10,6},{12,8},{14,10},{1,13},{3,15... | collective-permute-start | bytes 786440 | tf_op jit(solution)/shard_map/ppermute | solution.py:436
  7.0 14.5 %collective-permute-start.8 = (bf16[32,16,256]{2,1,0:T(8,128)(2,1)S(1)}, bf16[32,16,256]{2,1,0:T(8,128)(2,1)S(1)}, u32[]{:S(2)}, u32[]{:S(2)}) collective-permute-start(bf16[32,16,256]{2,1,0:T(8,128)(2,1)S(1)} %bitcast.57), channel_id=1, source_target_pairs={{0,2},{2,0},{4,6},{6,4},{8,10},{10,8},{12,14},{14,12},{1,3},{3,1},... | collective-permute-start | bytes 786440 | tf_op jit(solution)/shard_map/ppermute | solution.py:441
  10.0 2.1 %collective-permute-start.1 = (bf16[2,320,384]{2,1,0:T(8,128)(2,1)S(1)}, bf16[2,320,384]{2,1,0:T(8,128)(2,1)}, u32[]{:S(2)}, u32[]{:S(2)}) collective-permute-start(bf16[2,320,384]{2,1,0:T(8,128)(2,1)S(1)} %convert_element_type.16), channel_id=1, source_target_pairs={{0,1},{1,0},{2,3},{3,2},{4,5},{5,4},{6,7},{7,6},{8,9},{9,8},{10,11... | collective-permute-start | bytes 1474568 | tf_op jit(solution)/shard_map/ppermute | solution.py:431
  13.2 16.8 %copy-start.12 = (f32[2,8,16]{2,1,0:T(8,128)S(1)}, f32[2,8,16]{2,1,0:T(8,128)}, u32[]{:S(2)}) copy-start(f32[2,8,16]{2,1,0:T(8,128)} %param.12) | copy-start | bytes 3076
  13.2 28.0 %copy-start = (bf16[8,256,256]{2,1,0:T(8,128)(2,1)S(1)}, bf16[8,256,256]{2,1,0:T(8,128)(2,1)}, u32[]{:S(2)}) copy-start(bf16[8,256,256]{2,1,0:T(8,128)(2,1)} %refs_17_.1) | copy-start | bytes 3145732
  13.2 28.0 %copy-start.1 = (s32[2]{0:T(128)S(1)}, s32[2]{0:T(128)}, u32[]{:S(2)}) copy-start(s32[2]{0:T(128)} %live_ref.1) | copy-start | bytes 28
  13.3 27.9 %copy-start.5 = (bf16[512,512]{1,0:T(8,128)(2,1)S(1)}, bf16[512,512]{1,0:T(8,128)(2,1)}, u32[]{:S(2)}) copy-start(bf16[512,512]{1,0:T(8,128)(2,1)} %constant.38.clone.refs_18_) | copy-start | bytes 1572868
  13.3 27.9 %copy-start.6 = (bf16[512,512]{1,0:T(8,128)(2,1)S(1)}, bf16[512,512]{1,0:T(8,128)(2,1)}, u32[]{:S(2)}) copy-start(bf16[512,512]{1,0:T(8,128)(2,1)} %constant.39.clone.refs_19_) | copy-start | bytes 1572868
  19.5 10.2 %collective-permute-start.7 = (bf16[32,16,256]{2,1,0:T(8,128)(2,1)S(1)}, bf16[32,16,256]{2,1,0:T(8,128)(2,1)S(1)}, u32[]{:S(2)}, u32[]{:S(2)}) collective-permute-start(bf16[32,16,256]{2,1,0:T(8,128)(2,1)S(1)} %collective-permute-done.2.refs_2_), channel_id=1, source_target_pairs={{0,4},{2,6},{4,8},{6,10},{8,12},{10,14},{12,0},{14,2},{1,5},{3,7},... | collective-permute-start | bytes 786440 | tf_op jit(solution)/shard_map/ppermute | solution.py:436
  19.6 10.5 %collective-permute-start.4 = (bf16[32,16,256]{2,1,0:T(8,128)(2,1)S(1)}, bf16[32,16,256]{2,1,0:T(8,128)(2,1)S(1)}, u32[]{:S(2)}, u32[]{:S(2)}) collective-permute-start(bf16[32,16,256]{2,1,0:T(8,128)(2,1)S(1)} %collective-permute-done.3.refs_3_), channel_id=1, source_target_pairs={{0,2},{2,0},{4,6},{6,4},{8,10},{10,8},{12,14},{14,12},{1,3},{3,1},... | collective-permute-start | bytes 786440 | tf_op jit(solution)/shard_map/ppermute | solution.py:441
  21.0 1.2 %collective-permute-start = (bf16[2,8,16]{2,1,0:T(8,128)(2,1)S(1)}, bf16[2,8,16]{2,1,0:T(8,128)(2,1)S(1)}, u32[]{:S(2)}, u32[]{:S(2)}) collective-permute-start(bf16[2,8,16]{2,1,0:T(8,128)(2,1)S(1)} %convert_element_type.15), channel_id=1, source_target_pairs={{0,1},{1,0},{2,3},{3,2},{4,5},{5,4},{6,7},{7,6},{8,9},{9,8},{10,11... | collective-permute-start | bytes 1544 | tf_op jit(solution)/shard_map/ppermute | solution.py:431
  21.0 12.3 %collective-permute-start.11 = (bf16[32,16,256]{2,1,0:T(8,128)(2,1)S(1)}, bf16[32,16,256]{2,1,0:T(8,128)(2,1)S(1)}, u32[]{:S(2)}, u32[]{:S(2)}) collective-permute-start(bf16[32,16,256]{2,1,0:T(8,128)(2,1)S(1)} %bitcast.58), channel_id=1, source_target_pairs={{0,1},{1,0},{2,3},{3,2},{4,5},{5,4},{6,7},{7,6},{8,9},{9,8},{10,11... | collective-permute-start | bytes 786440 | tf_op jit(solution)/shard_map/ppermute | solution.py:431
  21.5 11.8 %collective-permute-start.15 = (bf16[32,16,256]{2,1,0:T(8,128)(2,1)S(1)}, bf16[32,16,256]{2,1,0:T(8,128)(2,1)S(1)}, u32[]{:S(2)}, u32[]{:S(2)}) collective-permute-start(bf16[32,16,256]{2,1,0:T(8,128)(2,1)S(1)} %collective-permute-done.8.refs_4_), channel_id=1, source_target_pairs={{0,1},{1,0},{2,3},{3,2},{4,5},{5,4},{6,7},{7,6},{8,9},{9,8},{10,11... | collective-permute-start | bytes 786440 | tf_op jit(solution)/shard_map/ppermute | solution.py:431
  22.2 12.2 %collective-permute-start.10 = (bf16[32,16,256]{2,1,0:T(8,128)(2,1)S(1)}, bf16[32,16,256]{2,1,0:T(8,128)(2,1)S(1)}, u32[]{:S(2)}, u32[]{:S(2)}) collective-permute-start(bf16[32,16,256]{2,1,0:T(8,128)(2,1)S(1)} %collective-permute-done.2.refs_2_), channel_id=1, source_target_pairs={{0,2},{2,0},{4,6},{6,4},{8,10},{10,8},{12,14},{14,12},{1,3},{3,1},... | collective-permute-start | bytes 786440 | tf_op jit(solution)/shard_map/ppermute | solution.py:441
  29.7 9.6 %collective-permute-start.9 = (bf16[32,16,256]{2,1,0:T(8,128)(2,1)S(1)}, bf16[32,16,256]{2,1,0:T(8,128)(2,1)S(1)}, u32[]{:S(2)}, u32[]{:S(2)}) collective-permute-start(bf16[32,16,256]{2,1,0:T(8,128)(2,1)S(1)} %collective-permute-done.7.refs_1_), channel_id=1, source_target_pairs={{0,2},{2,0},{4,6},{6,4},{8,10},{10,8},{12,14},{14,12},{1,3},{3,1},... | collective-permute-start | bytes 786440 | tf_op jit(solution)/shard_map/ppermute | solution.py:441
  30.0 1.5 %collective-permute-start.5 = (bf16[32,16,256]{2,1,0:T(8,128)(2,1)S(1)}, bf16[32,16,256]{2,1,0:T(8,128)(2,1)S(1)}, u32[]{:S(2)}, u32[]{:S(2)}) collective-permute-start(bf16[32,16,256]{2,1,0:T(8,128)(2,1)S(1)} %collective-permute-done.4.refs_7_), channel_id=1, source_target_pairs={{0,1},{1,0},{2,3},{3,2},{4,5},{5,4},{6,7},{7,6},{8,9},{9,8},{10,11... | collective-permute-start | bytes 786440 | tf_op jit(solution)/shard_map/ppermute | solution.py:431
  31.6 7.8 %collective-permute-start.6 = (bf16[2,2,8,16]{3,2,1,0:T(8,128)(2,1)S(1)}, bf16[2,2,8,16]{3,2,1,0:T(8,128)(2,1)S(1)}, u32[]{:S(2)}, u32[]{:S(2)}) collective-permute-start(bf16[2,2,8,16]{3,2,1,0:T(8,128)(2,1)S(1)} %pad_maximum_fusion.1), channel_id=1, source_target_pairs={{0,2},{2,0},{4,6},{6,4},{8,10},{10,8},{12,14},{14,12},{1,3},{3,1},... | collective-permute-start | bytes 3080 | tf_op jit(solution)/shard_map/ppermute | solution.py:441
  33.3 6.6 %collective-permute-start.13 = (bf16[32,16,256]{2,1,0:T(8,128)(2,1)S(1)}, bf16[32,16,256]{2,1,0:T(8,128)(2,1)S(1)}, u32[]{:S(2)}, u32[]{:S(2)}) collective-permute-start(bf16[32,16,256]{2,1,0:T(8,128)(2,1)S(1)} %collective-permute-done.2.refs_2_), channel_id=1, source_target_pairs={{0,1},{1,0},{2,3},{3,2},{4,5},{5,4},{6,7},{7,6},{8,9},{9,8},{10,11... | collective-permute-start | bytes 786440 | tf_op jit(solution)/shard_map/ppermute | solution.py:431
  33.3 6.6 %collective-permute-start.14 = (bf16[32,16,256]{2,1,0:T(8,128)(2,1)S(1)}, bf16[32,16,256]{2,1,0:T(8,128)(2,1)S(1)}, u32[]{:S(2)}, u32[]{:S(2)}) collective-permute-start(bf16[32,16,256]{2,1,0:T(8,128)(2,1)S(1)} %collective-permute-done.3.refs_3_), channel_id=1, source_target_pairs={{0,1},{1,0},{2,3},{3,2},{4,5},{5,4},{6,7},{7,6},{8,9},{9,8},{10,11... | collective-permute-start | bytes 786440 | tf_op jit(solution)/shard_map/ppermute | solution.py:431
  34.4 5.4 %collective-permute-start.12 = (bf16[32,16,256]{2,1,0:T(8,128)(2,1)S(1)}, bf16[32,16,256]{2,1,0:T(8,128)(2,1)S(1)}, u32[]{:S(2)}, u32[]{:S(2)}) collective-permute-start(bf16[32,16,256]{2,1,0:T(8,128)(2,1)S(1)} %collective-permute-done.7.refs_1_), channel_id=1, source_target_pairs={{0,1},{1,0},{2,3},{3,2},{4,5},{5,4},{6,7},{7,6},{8,9},{9,8},{10,11... | collective-permute-start | bytes 786440 | tf_op jit(solution)/shard_map/ppermute | solution.py:431
  39.3 1.5 %collective-permute-start.17 = (bf16[32,16,256]{2,1,0:T(8,128)(2,1)S(1)}, bf16[32,16,256]{2,1,0:T(8,128)(2,1)S(1)}, u32[]{:S(2)}, u32[]{:S(2)}) collective-permute-start(bf16[32,16,256]{2,1,0:T(8,128)(2,1)S(1)} %collective-permute-done.10.refs_6_), channel_id=1, source_target_pairs={{0,1},{1,0},{2,3},{3,2},{4,5},{5,4},{6,7},{7,6},{8,9},{9,8},{10,11... | collective-permute-start | bytes 786440 | tf_op jit(solution)/shard_map/ppermute | solution.py:431
  39.4 1.8 %collective-permute-start.16 = (bf16[32,16,256]{2,1,0:T(8,128)(2,1)S(1)}, bf16[32,16,256]{2,1,0:T(8,128)(2,1)S(1)}, u32[]{:S(2)}, u32[]{:S(2)}) collective-permute-start(bf16[32,16,256]{2,1,0:T(8,128)(2,1)S(1)} %collective-permute-done.9.refs_5_), channel_id=1, source_target_pairs={{0,1},{1,0},{2,3},{3,2},{4,5},{5,4},{6,7},{7,6},{8,9},{9,8},{10,11... | collective-permute-start | bytes 786440 | tf_op jit(solution)/shard_map/ppermute | solution.py:431
  51.2 9.7 %collective-permute-start.18 = (bf16[4,16,16,256]{3,2,1,0:T(8,128)(2,1)S(1)}, bf16[4,16,16,256]{3,2,1,0:T(8,128)(2,1)S(1)}, u32[]{:S(2)}, u32[]{:S(2)}) collective-permute-start(bf16[4,16,16,256]{3,2,1,0:T(8,128)(2,1)S(1)} %get-tuple-element.56.keep1_ref), channel_id=1, source_target_pairs={{0,1},{1,0},{2,3},{3,2},{4,5},{5,4},{6,7},{7,6},{8,9},{9,8},{10,11... | collective-permute-start | bytes 1572872 | tf_op jit(solution)/shard_map/ppermute | solution.py:431
  51.5 2.0 %collective-permute-start.24 = (bf16[16,16,256]{2,1,0:T(8,128)(2,1)S(1)}, bf16[16,16,256]{2,1,0:T(8,128)(2,1)S(1)}, u32[]{:S(2)}, u32[]{:S(2)}) collective-permute-start(bf16[16,16,256]{2,1,0:T(8,128)(2,1)S(1)} %get-tuple-element.64.refs_5_), channel_id=1, source_target_pairs={{0,1},{1,0},{2,3},{3,2},{4,5},{5,4},{6,7},{7,6},{8,9},{9,8},{10,11... | collective-permute-start | bytes 393224 | tf_op jit(solution)/shard_map/ppermute | solution.py:431
  51.8 6.3 %collective-permute-start.20 = (bf16[16,16,256]{2,1,0:T(8,128)(2,1)S(1)}, bf16[16,16,256]{2,1,0:T(8,128)(2,1)S(1)}, u32[]{:S(2)}, u32[]{:S(2)}) collective-permute-start(bf16[16,16,256]{2,1,0:T(8,128)(2,1)S(1)} %get-tuple-element.59.refs_1_), channel_id=1, source_target_pairs={{0,2},{2,0},{4,6},{6,4},{8,10},{10,8},{12,14},{14,12},{1,3},{3,1},... | collective-permute-start | bytes 393224 | tf_op jit(solution)/shard_map/ppermute | solution.py:441
  52.8 9.7 %collective-permute-start.19 = (bf16[16,16,256]{2,1,0:T(8,128)(2,1)S(1)}, bf16[16,16,256]{2,1,0:T(8,128)(2,1)S(1)}, u32[]{:S(2)}, u32[]{:S(2)}) collective-permute-start(bf16[16,16,256]{2,1,0:T(8,128)(2,1)S(1)} %get-tuple-element.58.refs_6_), channel_id=1, source_target_pairs={{0,1},{1,0},{2,3},{3,2},{4,5},{5,4},{6,7},{7,6},{8,9},{9,8},{10,11... | collective-permute-start | bytes 393224 | tf_op jit(solution)/shard_map/ppermute | solution.py:431
  53.4 7.6 %collective-permute-start.25 = (bf16[16,16,256]{2,1,0:T(8,128)(2,1)S(1)}, bf16[16,16,256]{2,1,0:T(8,128)(2,1)S(1)}, u32[]{:S(2)}, u32[]{:S(2)}) collective-permute-start(bf16[16,16,256]{2,1,0:T(8,128)(2,1)S(1)} %collective-permute-done.24), channel_id=1, source_target_pairs={{0,2},{2,0},{4,6},{6,4},{8,10},{10,8},{12,14},{14,12},{1,3},{3,1},... | collective-permute-start | bytes 393224 | tf_op jit(solution)/shard_map/ppermute | solution.py:441
  54.6 8.4 %collective-permute-start.29 = (bf16[16,16,256]{2,1,0:T(8,128)(2,1)S(1)}, bf16[16,16,256]{2,1,0:T(8,128)(2,1)S(1)}, u32[]{:S(2)}, u32[]{:S(2)}) collective-permute-start(bf16[16,16,256]{2,1,0:T(8,128)(2,1)S(1)} %get-tuple-element.68.refs_2_), channel_id=1, source_target_pairs={{0,2},{2,0},{4,6},{6,4},{8,10},{10,8},{12,14},{14,12},{1,3},{3,1},... | collective-permute-start | bytes 393224 | tf_op jit(solution)/shard_map/ppermute | solution.py:441
  58.2 4.8 %collective-permute-start.28 = (bf16[16,16,256]{2,1,0:T(8,128)(2,1)S(1)}, bf16[16,16,256]{2,1,0:T(8,128)(2,1)S(1)}, u32[]{:S(2)}, u32[]{:S(2)}) collective-permute-start(bf16[16,16,256]{2,1,0:T(8,128)(2,1)S(1)} %get-tuple-element.67.refs_7_), channel_id=1, source_target_pairs={{0,1},{1,0},{2,3},{3,2},{4,5},{5,4},{6,7},{7,6},{8,9},{9,8},{10,11... | collective-permute-start | bytes 393224 | tf_op jit(solution)/shard_map/ppermute | solution.py:431
  61.4 11.2 %collective-permute-start.31 = (bf16[32,16,256]{2,1,0:T(8,128)(2,1)S(1)}, bf16[32,16,256]{2,1,0:T(8,128)(2,1)S(1)}, u32[]{:S(2)}, u32[]{:S(2)}) collective-permute-start(bf16[32,16,256]{2,1,0:T(8,128)(2,1)S(1)} %mode_sums.6), channel_id=1, source_target_pairs={{0,4},{2,6},{4,8},{6,10},{8,12},{10,14},{12,0},{14,2},{1,5},{3,7},... | collective-permute-start | bytes 786440 | tf_op jit(solution)/shard_map/ppermute | solution.py:436
  62.5 6.4 %collective-permute-start.21 = (bf16[16,16,256]{2,1,0:T(8,128)(2,1)S(1)}, bf16[16,16,256]{2,1,0:T(8,128)(2,1)S(1)}, u32[]{:S(2)}, u32[]{:S(2)}) collective-permute-start(bf16[16,16,256]{2,1,0:T(8,128)(2,1)S(1)} %collective-permute-done.19), channel_id=1, source_target_pairs={{0,2},{2,0},{4,6},{6,4},{8,10},{10,8},{12,14},{14,12},{1,3},{3,1},... | collective-permute-start | bytes 393224 | tf_op jit(solution)/shard_map/ppermute | solution.py:441
  63.0 9.1 %collective-permute-start.30 = (bf16[16,16,256]{2,1,0:T(8,128)(2,1)S(1)}, bf16[16,16,256]{2,1,0:T(8,128)(2,1)S(1)}, u32[]{:S(2)}, u32[]{:S(2)}) collective-permute-start(bf16[16,16,256]{2,1,0:T(8,128)(2,1)S(1)} %collective-permute-done.28), channel_id=1, source_target_pairs={{0,2},{2,0},{4,6},{6,4},{8,10},{10,8},{12,14},{14,12},{1,3},{3,1},... | collective-permute-start | bytes 393224 | tf_op jit(solution)/shard_map/ppermute | solution.py:441
  64.5 7.6 %collective-permute-start.26 = (bf16[16,16,256]{2,1,0:T(8,128)(2,1)S(1)}, bf16[16,16,256]{2,1,0:T(8,128)(2,1)S(1)}, u32[]{:S(2)}, u32[]{:S(2)}) collective-permute-start(bf16[16,16,256]{2,1,0:T(8,128)(2,1)S(1)} %get-tuple-element.65.refs_3_), channel_id=1, source_target_pairs={{0,2},{2,0},{4,6},{6,4},{8,10},{10,8},{12,14},{14,12},{1,3},{3,1},... | collective-permute-start | bytes 393224 | tf_op jit(solution)/shard_map/ppermute | solution.py:441
  65.0 9.6 %collective-permute-start.23 = (bf16[16,16,256]{2,1,0:T(8,128)(2,1)S(1)}, bf16[16,16,256]{2,1,0:T(8,128)(2,1)S(1)}, u32[]{:S(2)}, u32[]{:S(2)}) collective-permute-start(bf16[16,16,256]{2,1,0:T(8,128)(2,1)S(1)} %get-tuple-element.62.refs_4_), channel_id=1, source_target_pairs={{0,1},{1,0},{2,3},{3,2},{4,5},{5,4},{6,7},{7,6},{8,9},{9,8},{10,11... | collective-permute-start | bytes 393224 | tf_op jit(solution)/shard_map/ppermute | solution.py:431
  69.3 16.8 %copy-start.9 = (bf16[8,256,256]{2,1,0:T(8,128)(2,1)S(1)}, bf16[8,256,256]{2,1,0:T(8,128)(2,1)}, u32[]{:S(2)}) copy-start(bf16[8,256,256]{2,1,0:T(8,128)(2,1)} %get-tuple-element.72.grad_ref) | copy-start | bytes 3145732
  69.3 11.6 %collective-permute-start.33 = (bf16[32,16,256]{2,1,0:T(8,128)(2,1)S(1)}, bf16[32,16,256]{2,1,0:T(8,128)(2,1)S(1)}, u32[]{:S(2)}, u32[]{:S(2)}) collective-permute-start(bf16[32,16,256]{2,1,0:T(8,128)(2,1)S(1)} %mode_sums.7), channel_id=1, source_target_pairs={{0,12},{2,14},{4,0},{6,2},{8,4},{10,6},{12,8},{14,10},{1,13},{3,15... | collective-permute-start | bytes 786440 | tf_op jit(solution)/shard_map/ppermute | solution.py:436
  72.7 11.0 %collective-permute-start.32 = (bf16[32,16,256]{2,1,0:T(8,128)(2,1)S(1)}, bf16[32,16,256]{2,1,0:T(8,128)(2,1)S(1)}, u32[]{:S(2)}, u32[]{:S(2)}) collective-permute-start(bf16[32,16,256]{2,1,0:T(8,128)(2,1)S(1)} %add_convert_fusion), channel_id=1, source_target_pairs={{0,4},{2,6},{4,8},{6,10},{8,12},{10,14},{12,0},{14,2},{1,5},{3,7},... | collective-permute-start | bytes 786440 | tf_op jit(solution)/shard_map/ppermute | solution.py:436
  74.1 5.0 %collective-permute-start.22 = (bf16[16,16,256]{2,1,0:T(8,128)(2,1)S(1)}, bf16[16,16,256]{2,1,0:T(8,128)(2,1)S(1)}, u32[]{:S(2)}, u32[]{:S(2)}) collective-permute-start(bf16[16,16,256]{2,1,0:T(8,128)(2,1)S(1)} %get-tuple-element.61.refs_0_), channel_id=1, source_target_pairs={{0,2},{2,0},{4,6},{6,4},{8,10},{10,8},{12,14},{14,12},{1,3},{3,1},... | collective-permute-start | bytes 393224 | tf_op jit(solution)/shard_map/ppermute | solution.py:441
  74.6 5.9 %collective-permute-start.27 = (bf16[16,16,256]{2,1,0:T(8,128)(2,1)S(1)}, bf16[16,16,256]{2,1,0:T(8,128)(2,1)S(1)}, u32[]{:S(2)}, u32[]{:S(2)}) collective-permute-start(bf16[16,16,256]{2,1,0:T(8,128)(2,1)S(1)} %collective-permute-done.23), channel_id=1, source_target_pairs={{0,2},{2,0},{4,6},{6,4},{8,10},{10,8},{12,14},{14,12},{1,3},{3,1},... | collective-permute-start | bytes 393224 | tf_op jit(solution)/shard_map/ppermute | solution.py:441
  84.5 1.2 %collective-permute-start.34 = (f32[2,16,16]{2,1,0:T(8,128)S(1)}, f32[2,16,16]{2,1,0:T(8,128)S(1)}, u32[]{:S(2)}, u32[]{:S(2)}) collective-permute-start(f32[2,16,16]{2,1,0:T(8,128)S(1)} %get-tuple-element.70), channel_id=1, source_target_pairs={{0,1},{1,0},{2,3},{3,2},{4,5},{5,4},{6,7},{7,6},{8,9},{9,8},{10,11... | collective-permute-start | bytes 6152 | tf_op jit(solution)/shard_map/ppermute | solution.py:431
  85.8 3.7 %collective-permute-start.35 = (f32[2,16,16]{2,1,0:T(8,128)S(1)}, f32[2,16,16]{2,1,0:T(8,128)S(1)}, u32[]{:S(2)}, u32[]{:S(2)}) collective-permute-start(f32[2,16,16]{2,1,0:T(8,128)S(1)} %add.31), channel_id=1, source_target_pairs={{0,2},{2,0},{4,6},{6,4},{8,10},{10,8},{12,14},{14,12},{1,3},{3,1},... | collective-permute-start | bytes 6152 | tf_op jit(solution)/shard_map/ppermute | solution.py:539
  89.5 12.2 %collective-permute-start.36 = (f32[320,384]{1,0:T(8,128)S(1)}, f32[320,384]{1,0:T(8,128)S(1)}, u32[]{:S(2)}, u32[]{:S(2)}) collective-permute-start(f32[320,384]{1,0:T(8,128)S(1)} %get-tuple-element.76), channel_id=1, source_target_pairs={{0,1},{1,0},{2,3},{3,2},{4,5},{5,4},{6,7},{7,6},{8,9},{9,8},{10,11... | collective-permute-start | bytes 1474568 | tf_op jit(solution)/shard_map/ppermute | solution.py:431
  89.5 3.8 %collective-permute-start.37 = (f32[2,16,16]{2,1,0:T(8,128)S(1)}, f32[2,16,16]{2,1,0:T(8,128)S(1)}, u32[]{:S(2)}, u32[]{:S(2)}) collective-permute-start(f32[2,16,16]{2,1,0:T(8,128)S(1)} %add.33), channel_id=1, source_target_pairs={{0,4},{2,6},{4,0},{6,2},{8,12},{10,14},{12,8},{14,10},{1,5},{3,7},... | collective-permute-start | bytes 6152 | tf_op jit(solution)/shard_map/ppermute | solution.py:539
  93.3 8.4 %collective-permute-start.38 = (f32[320,384]{1,0:T(8,128)S(1)}, f32[320,384]{1,0:T(8,128)S(1)}, u32[]{:S(2)}, u32[]{:S(2)}) collective-permute-start(f32[320,384]{1,0:T(8,128)S(1)} %get-tuple-element.84), channel_id=1, source_target_pairs={{0,1},{1,0},{2,3},{3,2},{4,5},{5,4},{6,7},{7,6},{8,9},{9,8},{10,11... | collective-permute-start | bytes 1474568 | tf_op jit(solution)/shard_map/ppermute | solution.py:431
  93.3 4.8 %collective-permute-start.39 = (f32[2,16,16]{2,1,0:T(8,128)S(1)}, f32[2,16,16]{2,1,0:T(8,128)S(1)}, u32[]{:S(2)}, u32[]{:S(2)}) collective-permute-start(f32[2,16,16]{2,1,0:T(8,128)S(1)} %add.36), channel_id=1, source_target_pairs={{0,8},{2,10},{4,12},{6,14},{8,0},{10,2},{12,4},{14,6},{1,9},{3,11}... | collective-permute-start | bytes 6152 | tf_op jit(solution)/shard_map/ppermute | solution.py:539
  (5 other events, 41.4 us)

commit v4 on v3

--- a/solution.py
+++ b/solution.py
@@ -237,14 +237,15 @@
         row_at, col_at = row_ref[at], col_ref[at]
         sel = (owner_ref[at] != meta_ref[0]).astype(jnp.int32)
         cols = (iota((length, width), 1) == iota((length, width), 0) + col_at).astype(bf16)
-        band = jnp.dot(grad_ref[spot], cols, preferred_element_type=f32)
-        band_ref[spot * length:(spot + 1) * length] = band.astype(bf16)
-        place = iota((2 * height, length), 1) + row_at + height * sel
-        places.append((iota((2 * height, length), 0) == place).astype(bf16))
+        band = jnp.dot(grad_ref[spot], cols, preferred_element_type=f32).astype(bf16)
+        for which in range(2):
+            flag = (sel == which).astype(f32).astype(bf16)
+            band_ref[spot * length:(spot + 1) * length, which * width:(which + 1) * width] = band * flag
+        places.append((iota((height, length), 0) == iota((height, length), 1) + row_at).astype(bf16))
     places = jnp.concatenate(places, axis=1)
     total = jnp.dot(places, band_ref[...], preferred_element_type=f32)
-    mine_ref[...] = total[:height]
-    other_ref[...] = total[height:]
+    mine_ref[...] = total[:, :width]
+    other_ref[...] = total[:, width:]
 
 
 def settle(scalars, grads, height, width):
@@ -255,7 +256,7 @@
         grid=(1,),
         in_specs=[whole(grads)],
         out_specs=[tile, tile],
-        scratch_shapes=[pltpu.VMEM((cap * length, width), bf16)],
+        scratch_shapes=[pltpu.VMEM((cap * length, 2 * width), bf16)],
     )
     shape = jax.ShapeDtypeStruct((height, width), f32)
     return pl.pallas_call(
@@ -290,19 +291,17 @@
     def mul(left, right):
         return jnp.dot(left, right, precision=HI, preferred_element_type=f32)
 
-    def gather_rows(which):
-        pick = iota((slots, tall), 1) // RB == 2 * iota((slots, tall), 0) + which
-        return mul(pick.astype(f32), table)
-
-    def pick_cols(which):
-        pick = iota((wide, modes), 0) // RB == which * modes + iota((wide, modes), 1)
-        return pick.astype(f32)
-
-    low, high = gather_rows(0), gather_rows(1)
-    cols_r, cols_i = pick_cols(0), pick_cols(1)
+    rows = jnp.sum(table.reshape(2 * slots, RB, wide), axis=1)
+    pick = (iota((wide, 2 * modes), 0) // RB == iota((wide, 2 * modes), 1)).astype(f32)
+    small = mul(rows, pick)
+
+    def every_other(which):
+        return mul((iota((slots, 2 * slots), 1) == 2 * iota((slots, 2 * slots), 0) + which).astype(f32), small)
+
+    low, high = every_other(0), every_other(1)
     norm = 1.0 / (4 * count * RB * lanes)
-    nw_ref[0] = (mul(low, cols_r) + mul(high, cols_i)) * norm
-    nw_ref[1] = (mul(high, cols_r) - mul(low, cols_i)) * norm
+    nw_ref[0] = (low[:, :modes] + high[:, modes:]) * norm
+    nw_ref[1] = (high[:, :modes] - low[:, modes:]) * norm
 
 
 def new_weights_of(updated, blocks):
@@ -452,7 +451,7 @@
     patches = cut(obj_pair)
     patches, come[1], come[3], ready = lax.optimization_barrier((patches, come[1], come[3], ready))
     come[2] = turn(come[1], 1)
-    for step in (1, 3, 2):
+    for step in (3, 1, 2):
         side[step] = across(come[step])
     come[0] = own
     order = [-step % len(STEPS) for step in STEPS]

time: 103 us -> 103 us (level)
  waiting for transfers between devices: 36.1 us -> 37.2 us
    ppermute x3, waiting for transfers between devices: 2.31 us -> 3.39 us  [sum_everywhere(): come = lax.ppermute(value, 'scan', [(i, i ^ step) for i in range(count)])]
  transfers between devices with their start and end apart: 40 -> 40, of which waited for: 20 -> 20; matrix products, arithmetic and copies ran while one was open for 4% -> 4% of each run, Pallas kernels for 20% -> 19%
where the time goes in v4:
time: 103 us
  waiting for transfers between devices  37.2 us (36%)
  Pallas kernels  30.6 us (30%)
  starting transfers between devices  27.8 us (27%)
  other arithmetic  5.77 us (6%)
  between operations  1.08 us (1%)
    ppermute x13, waiting for transfers between devices, across(): return lax.ppermute(value, 'scan', [(i, i ^ 1) for i in range(count)])  18.3 us
    ppermute x13, starting transfers between devices, across(): return lax.ppermute(value, 'scan', [(i, i ^ 1) for i in range(count)])  13.4 us
    ppermute x6, starting transfers between devices, turn(): lax.ppermute(value, 'scan', [(i, (i + 2 * step) % count) for i in range(c...  10.5 us
    pallas_call x1, Pallas kernels, relax(): pl.pallas_call(relax_kernel, grid_spec=grid_spec, out_shape=[many, many,...  10 us
    ppermute x6, waiting for transfers between devices, turn(): lax.ppermute(value, 'scan', [(i, (i + 2 * step) % count) for i in range(c...  9.67 us
    pallas_call x1, Pallas kernels, cut_patches(): pl.pallas_call(cut_kernel, grid_spec=grid_spec, out_shape=jax.ShapeDtypeS...  6.17 us
    ppermute x18, waiting for transfers between devices, swap_tiles(): lax.ppermute(value, 'tile', [(i, (i + 1) % count) for i in range(count)])  5.9 us
    pallas_call x2, Pallas kernels, settle(): pl.pallas_call(settle_kernel, grid_spec=grid_spec, out_shape=[shape, shap...  4.83 us
  transfers between devices with their start and end apart: 40, of which 20 were waited for; matrix products, arithmetic and copies ran while one was open for 4% of the time, Pallas kernels for 19%

profile of v4, /device:TPU:0, one launch (start us, length us, event | category | flops | bytes accessed | tf_op | source)
XLA Modules:
  0.0 102.8 jit_solution(13764494547456413504)
XLA Ops:
  0.7 1.1 %convert_element_type.17 = bf16[2,16,4096]{2,1,0:T(8,128)(2,1)S(1)} convert(f32[2,16,4096]{2,1,0:T(8,128)} %param.11) | non-fusion elementwise | flops 131072 | bytes 786432 | tf_op jit(solution)/shard_map/convert_element_type | solution.py:559
  1.9 3.1 %collective-permute-start.2 = (bf16[32,16,256]{2,1,0:T(8,128)(2,1)S(1)}, bf16[32,16,256]{2,1,0:T(8,128)(2,1)S(1)}, u32[]{:S(2)}, u32[]{:S(2)}) collective-permute-start(bf16[32,16,256]{2,1,0:T(8,128)(2,1)S(1)} %bitcast.55), channel_id=1, source_target_pairs={{0,4},{2,6},{4,8},{6,10},{8,12},{10,14},{12,0},{14,2},{1,5},{3,7},... | collective-permute-start | bytes 786440 | tf_op jit(solution)/shard_map/ppermute | solution.py:435
  5.0 2.1 %collective-permute-start.3 = (bf16[32,16,256]{2,1,0:T(8,128)(2,1)S(1)}, bf16[32,16,256]{2,1,0:T(8,128)(2,1)S(1)}, u32[]{:S(2)}, u32[]{:S(2)}) collective-permute-start(bf16[32,16,256]{2,1,0:T(8,128)(2,1)S(1)} %bitcast.56), channel_id=1, source_target_pairs={{0,12},{2,14},{4,0},{6,2},{8,4},{10,6},{12,8},{14,10},{1,13},{3,15... | collective-permute-start | bytes 786440 | tf_op jit(solution)/shard_map/ppermute | solution.py:435
  7.0 1.7 %collective-permute-start.8 = (bf16[32,16,256]{2,1,0:T(8,128)(2,1)S(1)}, bf16[32,16,256]{2,1,0:T(8,128)(2,1)S(1)}, u32[]{:S(2)}, u32[]{:S(2)}) collective-permute-start(bf16[32,16,256]{2,1,0:T(8,128)(2,1)S(1)} %bitcast.57), channel_id=1, source_target_pairs={{0,2},{2,0},{4,6},{6,4},{8,10},{10,8},{12,14},{14,12},{1,3},{3,1},... | collective-permute-start | bytes 786440 | tf_op jit(solution)/shard_map/ppermute | solution.py:440
  8.7 1.3 %convert_element_type.16 = bf16[2,320,384]{2,1,0:T(8,128)(2,1)S(1)} convert(f32[2,320,384]{2,1,0:T(8,128)} %param.10) | non-fusion elementwise | flops 245760 | bytes 1474560 | tf_op jit(solution)/shard_map/convert_element_type | solution.py:560
  10.1 0.7 convert_element_type.15
  11.4 0.7 collective-permute-done.1
  12.0 1.1 %pad_maximum_fusion.obj_ref = bf16[2,2,320,384]{3,2,1,0:T(8,128)(2,1)S(1)} fusion(bf16[1,2,320,384]{3,2,1,0:T(8,128)(2,1)} %bitcast.6, bf16[1,2,320,384]{3,2,1,0:T(8,128)(2,1)S(1)} %convert_bitcast_fusion), kind=kLoop, calls=%fused_computation | loop fusion | flops 491520 | bytes 1966080 | tf_op jit(solution)/shard_map/stack | solution.py:450
  13.3 6.2 %cut_patches.1.refs_16_ = bf16[8,2,256,256]{3,2,1,0:T(8,128)(2,1)S(1)} custom-call(s32[4]{0:T(128)S(1)} %pad_add_fusion.meta_ref, s32[16]{0:T(128)S(1)} %copy-done.2, s32[16]{0:T(128)S(1)} %copy-done.3, s32[16]{0:T(128)S(1)} %copy-done.4, bf16[2,2,320,384]{3,2,1,0:T(8,128)(2,1)S(1)} %pad_maximum_fusion.obj_ref), custom_call_target="tpu_custom_call" | custom-call | flops 4294967296 | bytes 4194304 | tf_op jit(solution)/shard_map/cut_patches/pallas_call | solution.py:77
  19.6 1.4 %collective-permute-start.4 = (bf16[32,16,256]{2,1,0:T(8,128)(2,1)S(1)}, bf16[32,16,256]{2,1,0:T(8,128)(2,1)S(1)}, u32[]{:S(2)}, u32[]{:S(2)}) collective-permute-start(bf16[32,16,256]{2,1,0:T(8,128)(2,1)S(1)} %collective-permute-done.3.refs_3_), channel_id=1, source_target_pairs={{0,2},{2,0},{4,6},{6,4},{8,10},{10,8},{12,14},{14,12},{1,3},{3,1},... | collective-permute-start | bytes 786440 | tf_op jit(solution)/shard_map/ppermute | solution.py:440
  21.0 0.5 collective-permute-start.11
  21.5 0.6 collective-permute-done
  22.2 0.7 collective-permute-start.10
  22.8 6.9 %collective-permute-done.7.refs_1_ = bf16[32,16,256]{2,1,0:T(8,128)(2,1)S(1)} collective-permute-done((bf16[32,16,256]{2,1,0:T(8,128)(2,1)S(1)}, bf16[32,16,256]{2,1,0:T(8,128)(2,1)S(1)}, u32[]{:S(2)}, u32[]{:S(2)}) %collective-permute-start.7) | collective-permute-done | bytes 262176 | tf_op jit(solution)/shard_map/ppermute | solution.py:435
  30.1 1.5 %collective-permute-done.5.refs_15_ = bf16[32,16,256]{2,1,0:T(8,128)(2,1)S(1)} collective-permute-done((bf16[32,16,256]{2,1,0:T(8,128)(2,1)S(1)}, bf16[32,16,256]{2,1,0:T(8,128)(2,1)S(1)}, u32[]{:S(2)}, u32[]{:S(2)}) %collective-permute-start.5) | collective-permute-done | bytes 262176 | tf_op jit(solution)/shard_map/ppermute | solution.py:430
  31.6 1.7 %collective-permute-start.6 = (bf16[2,2,8,16]{3,2,1,0:T(8,128)(2,1)S(1)}, bf16[2,2,8,16]{3,2,1,0:T(8,128)(2,1)S(1)}, u32[]{:S(2)}, u32[]{:S(2)}) collective-permute-start(bf16[2,2,8,16]{3,2,1,0:T(8,128)(2,1)S(1)} %pad_maximum_fusion.1), channel_id=1, source_target_pairs={{0,2},{2,0},{4,6},{6,4},{8,10},{10,8},{12,14},{14,12},{1,3},{3,1},... | collective-permute-start | bytes 3080 | tf_op jit(solution)/shard_map/ppermute | solution.py:440
  33.8 0.6 collective-permute-done.10.refs_6_
  34.4 4.9 %collective-permute-done.9.refs_5_ = bf16[32,16,256]{2,1,0:T(8,128)(2,1)S(1)} collective-permute-done((bf16[32,16,256]{2,1,0:T(8,128)(2,1)S(1)}, bf16[32,16,256]{2,1,0:T(8,128)(2,1)S(1)}, u32[]{:S(2)}, u32[]{:S(2)}) %collective-permute-start.9) | collective-permute-done | bytes 262176 | tf_op jit(solution)/shard_map/ppermute | solution.py:440
  39.8 1.0 collective-permute-done.17.refs_14_
  41.2 10.0 %relax_positions.1 = (bf16[4,16,16,256]{3,2,1,0:T(8,128)(2,1)S(1)}, bf16[4,16,16,256]{3,2,1,0:T(8,128)(2,1)S(1)}, bf16[16,16,256]{2,1,0:T(8,128)(2,1)S(1)}, bf16...) custom-call(s32[4]{0:T(128)S(1)} %pad_add_fusion.meta_ref, ...), custom_call_target="tpu_custom_call" | custom-call | flops 8589934592 | bytes 16777216 | tf_op jit(solution)/shard_map/relax_positions/pallas_call | solution.py:217
  51.8 1.0 collective-permute-start.20
  53.4 1.0 collective-permute-start.25
  54.6 1.1 %collective-permute-start.29 = (bf16[16,16,256]{2,1,0:T(8,128)(2,1)S(1)}, bf16[16,16,256]{2,1,0:T(8,128)(2,1)S(1)}, u32[]{:S(2)}, u32[]{:S(2)}) collective-permute-start(bf16[16,16,256]{2,1,0:T(8,128)(2,1)S(1)} %get-tuple-element.68.refs_2_), channel_id=1, source_target_pairs={{0,2},{2,0},{4,6},{6,4},{8,10},{10,8},{12,14},{14,12},{1,3},{3,1},... | collective-permute-start | bytes 393224 | tf_op jit(solution)/shard_map/ppermute | solution.py:440
  55.7 2.4 %collective-permute-done.20.far_ref = bf16[16,16,256]{2,1,0:T(8,128)(2,1)S(1)} collective-permute-done((bf16[16,16,256]{2,1,0:T(8,128)(2,1)S(1)}, bf16[16,16,256]{2,1,0:T(8,128)(2,1)S(1)}, u32[]{:S(2)}, u32[]{:S(2)}) %collective-permute-start.20) | collective-permute-done | bytes 131104 | tf_op jit(solution)/shard_map/ppermute | solution.py:440
  58.2 0.8 widen.3.wide_ref
  59.0 2.0 %collective-permute-done.25.far_twin_ref = bf16[16,16,256]{2,1,0:T(8,128)(2,1)S(1)} collective-permute-done((bf16[16,16,256]{2,1,0:T(8,128)(2,1)S(1)}, bf16[16,16,256]{2,1,0:T(8,128)(2,1)S(1)}, u32[]{:S(2)}, u32[]{:S(2)}) %collective-permute-start.25) | collective-permute-done | bytes 131104 | tf_op jit(solution)/shard_map/ppermute | solution.py:440
  61.4 1.0 %collective-permute-start.31 = (bf16[32,16,256]{2,1,0:T(8,128)(2,1)S(1)}, bf16[32,16,256]{2,1,0:T(8,128)(2,1)S(1)}, u32[]{:S(2)}, u32[]{:S(2)}) collective-permute-start(bf16[32,16,256]{2,1,0:T(8,128)(2,1)S(1)} %mode_sums.6), channel_id=1, source_target_pairs={{0,4},{2,6},{4,8},{6,10},{8,12},{10,14},{12,0},{14,2},{1,5},{3,7},... | collective-permute-start | bytes 786440 | tf_op jit(solution)/shard_map/ppermute | solution.py:435
  62.5 0.5 collective-permute-start.21
  63.0 1.5 %collective-permute-start.30 = (bf16[16,16,256]{2,1,0:T(8,128)(2,1)S(1)}, bf16[16,16,256]{2,1,0:T(8,128)(2,1)S(1)}, u32[]{:S(2)}, u32[]{:S(2)}) collective-permute-start(bf16[16,16,256]{2,1,0:T(8,128)(2,1)S(1)} %collective-permute-done.28), channel_id=1, source_target_pairs={{0,2},{2,0},{4,6},{6,4},{8,10},{10,8},{12,14},{14,12},{1,3},{3,1},... | collective-permute-start | bytes 393224 | tf_op jit(solution)/shard_map/ppermute | solution.py:440
  64.5 0.5 collective-permute-start.26
  65.0 3.8 %collective-permute-done.21.far_twin_ref = bf16[16,16,256]{2,1,0:T(8,128)(2,1)S(1)} collective-permute-done((bf16[16,16,256]{2,1,0:T(8,128)(2,1)S(1)}, bf16[16,16,256]{2,1,0:T(8,128)(2,1)S(1)}, u32[]{:S(2)}, u32[]{:S(2)}) %collective-permute-start.21) | collective-permute-done | bytes 131104 | tf_op jit(solution)/shard_map/ppermute | solution.py:440
  69.3 2.8 %collective-permute-start.33 = (bf16[32,16,256]{2,1,0:T(8,128)(2,1)S(1)}, bf16[32,16,256]{2,1,0:T(8,128)(2,1)S(1)}, u32[]{:S(2)}, u32[]{:S(2)}) collective-permute-start(bf16[32,16,256]{2,1,0:T(8,128)(2,1)S(1)} %mode_sums.7), channel_id=1, source_target_pairs={{0,12},{2,14},{4,0},{6,2},{8,4},{10,6},{12,8},{14,10},{1,13},{3,15... | collective-permute-start | bytes 786440 | tf_op jit(solution)/shard_map/ppermute | solution.py:435
  72.7 1.4 %collective-permute-start.32 = (bf16[32,16,256]{2,1,0:T(8,128)(2,1)S(1)}, bf16[32,16,256]{2,1,0:T(8,128)(2,1)S(1)}, u32[]{:S(2)}, u32[]{:S(2)}) collective-permute-start(bf16[32,16,256]{2,1,0:T(8,128)(2,1)S(1)} %add_convert_fusion), channel_id=1, source_target_pairs={{0,4},{2,6},{4,8},{6,10},{8,12},{10,14},{12,0},{14,2},{1,5},{3,7},... | collective-permute-start | bytes 786440 | tf_op jit(solution)/shard_map/ppermute | solution.py:435
  74.6 1.5 %collective-permute-start.27 = (bf16[16,16,256]{2,1,0:T(8,128)(2,1)S(1)}, bf16[16,16,256]{2,1,0:T(8,128)(2,1)S(1)}, u32[]{:S(2)}, u32[]{:S(2)}) collective-permute-start(bf16[16,16,256]{2,1,0:T(8,128)(2,1)S(1)} %collective-permute-done.23), channel_id=1, source_target_pairs={{0,2},{2,0},{4,6},{6,4},{8,10},{10,8},{12,14},{14,12},{1,3},{3,1},... | collective-permute-start | bytes 393224 | tf_op jit(solution)/shard_map/ppermute | solution.py:440
  76.1 2.9 %collective-permute-done.22.far_ref = bf16[16,16,256]{2,1,0:T(8,128)(2,1)S(1)} collective-permute-done((bf16[16,16,256]{2,1,0:T(8,128)(2,1)S(1)}, bf16[16,16,256]{2,1,0:T(8,128)(2,1)S(1)}, u32[]{:S(2)}, u32[]{:S(2)}) %collective-permute-start.22) | collective-permute-done | bytes 131104 | tf_op jit(solution)/shard_map/ppermute | solution.py:440
  79.1 1.4 %collective-permute-done.27.far_twin_ref = bf16[16,16,256]{2,1,0:T(8,128)(2,1)S(1)} collective-permute-done((bf16[16,16,256]{2,1,0:T(8,128)(2,1)S(1)}, bf16[16,16,256]{2,1,0:T(8,128)(2,1)S(1)}, u32[]{:S(2)}, u32[]{:S(2)}) %collective-permute-start.27) | collective-permute-done | bytes 131104 | tf_op jit(solution)/shard_map/ppermute | solution.py:440
  80.9 2.8 %collective-permute-done.32.refs_1_ = bf16[32,16,256]{2,1,0:T(8,128)(2,1)S(1)} collective-permute-done((bf16[32,16,256]{2,1,0:T(8,128)(2,1)S(1)}, bf16[32,16,256]{2,1,0:T(8,128)(2,1)S(1)}, u32[]{:S(2)}, u32[]{:S(2)}) %collective-permute-start.32) | collective-permute-done | bytes 262176 | tf_op jit(solution)/shard_map/ppermute | solution.py:435
  83.7 0.8 finish_sums.1
  84.6 1.2 %collective-permute-done.34 = f32[2,16,16]{2,1,0:T(8,128)S(1)} collective-permute-done((f32[2,16,16]{2,1,0:T(8,128)S(1)}, f32[2,16,16]{2,1,0:T(8,128)S(1)}, u32[]{:S(2)}, u32[]{:S(2)}) %collective-permute-start.34) | collective-permute-done | bytes 2080 | tf_op jit(solution)/shard_map/ppermute | solution.py:430
  86.1 2.4 %settle.2 = (f32[320,384]{1,0:T(8,128)S(1)}, f32[320,384]{1,0:T(8,128)S(1)}) custom-call(s32[4]{0:T(128)S(1)} %pad_add_fusion.meta_ref, s32[16]{0:T(128)S(1)} %copy-done.2, s32[16]{0:T(128)S(1)} %copy-done.3, s32[16]{0:T(128)S(1)} %copy-done.4, bf16[8,256,256]{2,1,0:T(8,128)(2,1)S(1)} %copy-done.9), custom_call_target="tpu_custom_call" | custom-call | flops 2147483648 | bytes 4194304 | tf_op jit(solution)/shard_map/settle/pallas_call | solution.py:262
  88.5 1.0 collective-permute-done.35
  89.6 2.4 %settle.3 = (f32[320,384]{1,0:T(8,128)S(1)}, f32[320,384]{1,0:T(8,128)S(1)}) custom-call(s32[4]{0:T(128)S(1)} %pad_add_fusion.meta_ref, s32[16]{0:T(128)S(1)} %copy-done.2, s32[16]{0:T(128)S(1)} %copy-done.3, s32[16]{0:T(128)S(1)} %copy-done.4, bf16[8,256,256]{2,1,0:T(8,128)(2,1)S(1)} %copy-done.8), custom_call_target="tpu_custom_call" | custom-call | flops 2147483648 | bytes 4194304 | tf_op jit(solution)/shard_map/settle/pallas_call | solution.py:262
  92.0 1.3 %collective-permute-done.37 = f32[2,16,16]{2,1,0:T(8,128)S(1)} collective-permute-done((f32[2,16,16]{2,1,0:T(8,128)S(1)}, f32[2,16,16]{2,1,0:T(8,128)S(1)}, u32[]{:S(2)}, u32[]{:S(2)}) %collective-permute-start.37) | collective-permute-done | bytes 2080 | tf_op jit(solution)/shard_map/ppermute | solution.py:538
  93.3 1.2 %collective-permute-start.39 = (f32[2,16,16]{2,1,0:T(8,128)S(1)}, f32[2,16,16]{2,1,0:T(8,128)S(1)}, u32[]{:S(2)}, u32[]{:S(2)}) collective-permute-start(f32[2,16,16]{2,1,0:T(8,128)S(1)} %add.36), channel_id=1, source_target_pairs={{0,8},{2,10},{4,12},{6,14},{8,0},{10,2},{12,4},{14,6},{1,9},{3,11}... | collective-permute-start | bytes 6152 | tf_op jit(solution)/shard_map/ppermute | solution.py:538
  94.5 2.4 %new_weights.1 = f32[2,8,16]{2,1,0:T(8,128)} custom-call(bf16[4,16,16,256]{3,2,1,0:T(8,128)(2,1)S(1)} %get-tuple-element.87.near_ref.keep0_ref, bf16[4,16,16,256]{3,2,1,0:T(8,128)(2,1)S(1)} %get-tuple-element.56.keep1_ref, bf16[16,16,256]{2,1,0:T(8,128)(2,1)S(1)} %get-tuple-element.61.refs_0_, bf16[16,16,256]{2,1,0:T(8,128)(2,1)S(1)} %get-tuple-element.59.refs_1_, ...), custom_call_target="tpu_custom_call" | custom-call | flops 2147483648 | bytes 6291456 | tf_op jit(solution)/shard_map/new_weights/pallas_call | solution.py:310
  96.9 1.1 %collective-permute-done.39 = f32[2,16,16]{2,1,0:T(8,128)S(1)} collective-permute-done((f32[2,16,16]{2,1,0:T(8,128)S(1)}, f32[2,16,16]{2,1,0:T(8,128)S(1)}, u32[]{:S(2)}, u32[]{:S(2)}) %collective-permute-start.39) | collective-permute-done | bytes 2080 | tf_op jit(solution)/shard_map/ppermute | solution.py:538
  98.0 3.6 %orthonormal_modes.1 = f32[32,4096]{1,0:T(8,128)} custom-call(f32[2,16,16]{2,1,0:T(8,128)S(1)} %add.37.gram_ref, f32[32,4096]{1,0:T(8,128)S(1)} %get-tuple-element.91.sum_ref), custom_call_target="tpu_custom_call" | custom-call | flops 134217728 | bytes 1048576 | tf_op jit(solution)/shard_map/orthonormal_modes/pallas_call | solution.py:419
  101.7 1.0 %fusion = f32[2,320,384]{2,1,0:T(8,128)} fusion(f32[2,320,384]{2,1,0:T(8,128)S(1)} %copy-done.11, f32[1,320,384]{2,1,0:T(8,128)S(1)} %add_bitcast_fusion, f32[1,320,384]{2,1,0:T(8,128)S(1)} %add_bitcast_fusion.1), kind=kLoop, calls=%fused_computation.2 | loop fusion | flops 737280 | bytes 2949120 | tf_op jit(solution)/shard_map/add | solution.py:592
  (102 shorter events, 7.0 us)
Async XLA Ops:
  0.6 12.5 %copy-start.2 = (s32[16]{0:T(128)S(1)}, s32[16]{0:T(128)}, u32[]{:S(2)}) copy-start(s32[16]{0:T(128)} %owner_ref.5) | copy-start | bytes 196
  0.7 12.5 %copy-start.3 = (s32[16]{0:T(128)S(1)}, s32[16]{0:T(128)}, u32[]{:S(2)}) copy-start(s32[16]{0:T(128)} %row_ref.5) | copy-start | bytes 196
  1.9 17.6 %collective-permute-start.2 = (bf16[32,16,256]{2,1,0:T(8,128)(2,1)S(1)}, bf16[32,16,256]{2,1,0:T(8,128)(2,1)S(1)}, u32[]{:S(2)}, u32[]{:S(2)}) collective-permute-start(bf16[32,16,256]{2,1,0:T(8,128)(2,1)S(1)} %bitcast.55), channel_id=1, source_target_pairs={{0,4},{2,6},{4,8},{6,10},{8,12},{10,14},{12,0},{14,2},{1,5},{3,7},... | collective-permute-start | bytes 786440 | tf_op jit(solution)/shard_map/ppermute | solution.py:435
  5.0 14.5 %collective-permute-start.3 = (bf16[32,16,256]{2,1,0:T(8,128)(2,1)S(1)}, bf16[32,16,256]{2,1,0:T(8,128)(2,1)S(1)}, u32[]{:S(2)}, u32[]{:S(2)}) collective-permute-start(bf16[32,16,256]{2,1,0:T(8,128)(2,1)S(1)} %bitcast.56), channel_id=1, source_target_pairs={{0,12},{2,14},{4,0},{6,2},{8,4},{10,6},{12,8},{14,10},{1,13},{3,15... | collective-permute-start | bytes 786440 | tf_op jit(solution)/shard_map/ppermute | solution.py:435
  7.0 14.5 %collective-permute-start.8 = (bf16[32,16,256]{2,1,0:T(8,128)(2,1)S(1)}, bf16[32,16,256]{2,1,0:T(8,128)(2,1)S(1)}, u32[]{:S(2)}, u32[]{:S(2)}) collective-permute-start(bf16[32,16,256]{2,1,0:T(8,128)(2,1)S(1)} %bitcast.57), channel_id=1, source_target_pairs={{0,2},{2,0},{4,6},{6,4},{8,10},{10,8},{12,14},{14,12},{1,3},{3,1},... | collective-permute-start | bytes 786440 | tf_op jit(solution)/shard_map/ppermute | solution.py:440
  10.0 2.1 %collective-permute-start.1 = (bf16[2,320,384]{2,1,0:T(8,128)(2,1)S(1)}, bf16[2,320,384]{2,1,0:T(8,128)(2,1)}, u32[]{:S(2)}, u32[]{:S(2)}) collective-permute-start(bf16[2,320,384]{2,1,0:T(8,128)(2,1)S(1)} %convert_element_type.16), channel_id=1, source_target_pairs={{0,1},{1,0},{2,3},{3,2},{4,5},{5,4},{6,7},{7,6},{8,9},{9,8},{10,11... | collective-permute-start | bytes 1474568 | tf_op jit(solution)/shard_map/ppermute | solution.py:430
  13.2 16.8 %copy-start.12 = (f32[2,8,16]{2,1,0:T(8,128)S(1)}, f32[2,8,16]{2,1,0:T(8,128)}, u32[]{:S(2)}) copy-start(f32[2,8,16]{2,1,0:T(8,128)} %param.12) | copy-start | bytes 3076
  13.2 28.0 %copy-start = (bf16[8,256,256]{2,1,0:T(8,128)(2,1)S(1)}, bf16[8,256,256]{2,1,0:T(8,128)(2,1)}, u32[]{:S(2)}) copy-start(bf16[8,256,256]{2,1,0:T(8,128)(2,1)} %refs_17_.1) | copy-start | bytes 3145732
  13.2 28.0 %copy-start.1 = (s32[2]{0:T(128)S(1)}, s32[2]{0:T(128)}, u32[]{:S(2)}) copy-start(s32[2]{0:T(128)} %live_ref.1) | copy-start | bytes 28
  13.3 27.9 %copy-start.5 = (bf16[512,512]{1,0:T(8,128)(2,1)S(1)}, bf16[512,512]{1,0:T(8,128)(2,1)}, u32[]{:S(2)}) copy-start(bf16[512,512]{1,0:T(8,128)(2,1)} %constant.38.clone.refs_18_) | copy-start | bytes 1572868
  13.3 27.9 %copy-start.6 = (bf16[512,512]{1,0:T(8,128)(2,1)S(1)}, bf16[512,512]{1,0:T(8,128)(2,1)}, u32[]{:S(2)}) copy-start(bf16[512,512]{1,0:T(8,128)(2,1)} %constant.39.clone.refs_19_) | copy-start | bytes 1572868
  19.5 10.2 %collective-permute-start.7 = (bf16[32,16,256]{2,1,0:T(8,128)(2,1)S(1)}, bf16[32,16,256]{2,1,0:T(8,128)(2,1)S(1)}, u32[]{:S(2)}, u32[]{:S(2)}) collective-permute-start(bf16[32,16,256]{2,1,0:T(8,128)(2,1)S(1)} %collective-permute-done.2.refs_2_), channel_id=1, source_target_pairs={{0,4},{2,6},{4,8},{6,10},{8,12},{10,14},{12,0},{14,2},{1,5},{3,7},... | collective-permute-start | bytes 786440 | tf_op jit(solution)/shard_map/ppermute | solution.py:435
  19.6 10.5 %collective-permute-start.4 = (bf16[32,16,256]{2,1,0:T(8,128)(2,1)S(1)}, bf16[32,16,256]{2,1,0:T(8,128)(2,1)S(1)}, u32[]{:S(2)}, u32[]{:S(2)}) collective-permute-start(bf16[32,16,256]{2,1,0:T(8,128)(2,1)S(1)} %collective-permute-done.3.refs_3_), channel_id=1, source_target_pairs={{0,2},{2,0},{4,6},{6,4},{8,10},{10,8},{12,14},{14,12},{1,3},{3,1},... | collective-permute-start | bytes 786440 | tf_op jit(solution)/shard_map/ppermute | solution.py:440
  21.0 1.2 %collective-permute-start = (bf16[2,8,16]{2,1,0:T(8,128)(2,1)S(1)}, bf16[2,8,16]{2,1,0:T(8,128)(2,1)S(1)}, u32[]{:S(2)}, u32[]{:S(2)}) collective-permute-start(bf16[2,8,16]{2,1,0:T(8,128)(2,1)S(1)} %convert_element_type.15), channel_id=1, source_target_pairs={{0,1},{1,0},{2,3},{3,2},{4,5},{5,4},{6,7},{7,6},{8,9},{9,8},{10,11... | collective-permute-start | bytes 1544 | tf_op jit(solution)/shard_map/ppermute | solution.py:430
  21.0 12.3 %collective-permute-start.11 = (bf16[32,16,256]{2,1,0:T(8,128)(2,1)S(1)}, bf16[32,16,256]{2,1,0:T(8,128)(2,1)S(1)}, u32[]{:S(2)}, u32[]{:S(2)}) collective-permute-start(bf16[32,16,256]{2,1,0:T(8,128)(2,1)S(1)} %bitcast.58), channel_id=1, source_target_pairs={{0,1},{1,0},{2,3},{3,2},{4,5},{5,4},{6,7},{7,6},{8,9},{9,8},{10,11... | collective-permute-start | bytes 786440 | tf_op jit(solution)/shard_map/ppermute | solution.py:430
  21.5 11.8 %collective-permute-start.15 = (bf16[32,16,256]{2,1,0:T(8,128)(2,1)S(1)}, bf16[32,16,256]{2,1,0:T(8,128)(2,1)S(1)}, u32[]{:S(2)}, u32[]{:S(2)}) collective-permute-start(bf16[32,16,256]{2,1,0:T(8,128)(2,1)S(1)} %collective-permute-done.8.refs_4_), channel_id=1, source_target_pairs={{0,1},{1,0},{2,3},{3,2},{4,5},{5,4},{6,7},{7,6},{8,9},{9,8},{10,11... | collective-permute-start | bytes 786440 | tf_op jit(solution)/shard_map/ppermute | solution.py:430
  22.2 12.2 %collective-permute-start.10 = (bf16[32,16,256]{2,1,0:T(8,128)(2,1)S(1)}, bf16[32,16,256]{2,1,0:T(8,128)(2,1)S(1)}, u32[]{:S(2)}, u32[]{:S(2)}) collective-permute-start(bf16[32,16,256]{2,1,0:T(8,128)(2,1)S(1)} %collective-permute-done.2.refs_2_), channel_id=1, source_target_pairs={{0,2},{2,0},{4,6},{6,4},{8,10},{10,8},{12,14},{14,12},{1,3},{3,1},... | collective-permute-start | bytes 786440 | tf_op jit(solution)/shard_map/ppermute | solution.py:440
  29.7 9.6 %collective-permute-start.9 = (bf16[32,16,256]{2,1,0:T(8,128)(2,1)S(1)}, bf16[32,16,256]{2,1,0:T(8,128)(2,1)S(1)}, u32[]{:S(2)}, u32[]{:S(2)}) collective-permute-start(bf16[32,16,256]{2,1,0:T(8,128)(2,1)S(1)} %collective-permute-done.7.refs_1_), channel_id=1, source_target_pairs={{0,2},{2,0},{4,6},{6,4},{8,10},{10,8},{12,14},{14,12},{1,3},{3,1},... | collective-permute-start | bytes 786440 | tf_op jit(solution)/shard_map/ppermute | solution.py:440
  30.0 1.5 %collective-permute-start.5 = (bf16[32,16,256]{2,1,0:T(8,128)(2,1)S(1)}, bf16[32,16,256]{2,1,0:T(8,128)(2,1)S(1)}, u32[]{:S(2)}, u32[]{:S(2)}) collective-permute-start(bf16[32,16,256]{2,1,0:T(8,128)(2,1)S(1)} %collective-permute-done.4.refs_7_), channel_id=1, source_target_pairs={{0,1},{1,0},{2,3},{3,2},{4,5},{5,4},{6,7},{7,6},{8,9},{9,8},{10,11... | collective-permute-start | bytes 786440 | tf_op jit(solution)/shard_map/ppermute | solution.py:430
  31.6 7.8 %collective-permute-start.6 = (bf16[2,2,8,16]{3,2,1,0:T(8,128)(2,1)S(1)}, bf16[2,2,8,16]{3,2,1,0:T(8,128)(2,1)S(1)}, u32[]{:S(2)}, u32[]{:S(2)}) collective-permute-start(bf16[2,2,8,16]{3,2,1,0:T(8,128)(2,1)S(1)} %pad_maximum_fusion.1), channel_id=1, source_target_pairs={{0,2},{2,0},{4,6},{6,4},{8,10},{10,8},{12,14},{14,12},{1,3},{3,1},... | collective-permute-start | bytes 3080 | tf_op jit(solution)/shard_map/ppermute | solution.py:440
  33.3 6.6 %collective-permute-start.13 = (bf16[32,16,256]{2,1,0:T(8,128)(2,1)S(1)}, bf16[32,16,256]{2,1,0:T(8,128)(2,1)S(1)}, u32[]{:S(2)}, u32[]{:S(2)}) collective-permute-start(bf16[32,16,256]{2,1,0:T(8,128)(2,1)S(1)} %collective-permute-done.2.refs_2_), channel_id=1, source_target_pairs={{0,1},{1,0},{2,3},{3,2},{4,5},{5,4},{6,7},{7,6},{8,9},{9,8},{10,11... | collective-permute-start | bytes 786440 | tf_op jit(solution)/shard_map/ppermute | solution.py:430
  33.3 6.6 %collective-permute-start.14 = (bf16[32,16,256]{2,1,0:T(8,128)(2,1)S(1)}, bf16[32,16,256]{2,1,0:T(8,128)(2,1)S(1)}, u32[]{:S(2)}, u32[]{:S(2)}) collective-permute-start(bf16[32,16,256]{2,1,0:T(8,128)(2,1)S(1)} %collective-permute-done.3.refs_3_), channel_id=1, source_target_pairs={{0,1},{1,0},{2,3},{3,2},{4,5},{5,4},{6,7},{7,6},{8,9},{9,8},{10,11... | collective-permute-start | bytes 786440 | tf_op jit(solution)/shard_map/ppermute | solution.py:430
  34.4 5.4 %collective-permute-start.12 = (bf16[32,16,256]{2,1,0:T(8,128)(2,1)S(1)}, bf16[32,16,256]{2,1,0:T(8,128)(2,1)S(1)}, u32[]{:S(2)}, u32[]{:S(2)}) collective-permute-start(bf16[32,16,256]{2,1,0:T(8,128)(2,1)S(1)} %collective-permute-done.7.refs_1_), channel_id=1, source_target_pairs={{0,1},{1,0},{2,3},{3,2},{4,5},{5,4},{6,7},{7,6},{8,9},{9,8},{10,11... | collective-permute-start | bytes 786440 | tf_op jit(solution)/shard_map/ppermute | solution.py:430
  39.3 1.5 %collective-permute-start.17 = (bf16[32,16,256]{2,1,0:T(8,128)(2,1)S(1)}, bf16[32,16,256]{2,1,0:T(8,128)(2,1)S(1)}, u32[]{:S(2)}, u32[]{:S(2)}) collective-permute-start(bf16[32,16,256]{2,1,0:T(8,128)(2,1)S(1)} %collective-permute-done.10.refs_6_), channel_id=1, source_target_pairs={{0,1},{1,0},{2,3},{3,2},{4,5},{5,4},{6,7},{7,6},{8,9},{9,8},{10,11... | collective-permute-start | bytes 786440 | tf_op jit(solution)/shard_map/ppermute | solution.py:430
  39.4 1.8 %collective-permute-start.16 = (bf16[32,16,256]{2,1,0:T(8,128)(2,1)S(1)}, bf16[32,16,256]{2,1,0:T(8,128)(2,1)S(1)}, u32[]{:S(2)}, u32[]{:S(2)}) collective-permute-start(bf16[32,16,256]{2,1,0:T(8,128)(2,1)S(1)} %collective-permute-done.9.refs_5_), channel_id=1, source_target_pairs={{0,1},{1,0},{2,3},{3,2},{4,5},{5,4},{6,7},{7,6},{8,9},{9,8},{10,11... | collective-permute-start | bytes 786440 | tf_op jit(solution)/shard_map/ppermute | solution.py:430
  51.2 9.7 %collective-permute-start.18 = (bf16[4,16,16,256]{3,2,1,0:T(8,128)(2,1)S(1)}, bf16[4,16,16,256]{3,2,1,0:T(8,128)(2,1)S(1)}, u32[]{:S(2)}, u32[]{:S(2)}) collective-permute-start(bf16[4,16,16,256]{3,2,1,0:T(8,128)(2,1)S(1)} %get-tuple-element.56.keep1_ref), channel_id=1, source_target_pairs={{0,1},{1,0},{2,3},{3,2},{4,5},{5,4},{6,7},{7,6},{8,9},{9,8},{10,11... | collective-permute-start | bytes 1572872 | tf_op jit(solution)/shard_map/ppermute | solution.py:430
  51.5 2.0 %collective-permute-start.24 = (bf16[16,16,256]{2,1,0:T(8,128)(2,1)S(1)}, bf16[16,16,256]{2,1,0:T(8,128)(2,1)S(1)}, u32[]{:S(2)}, u32[]{:S(2)}) collective-permute-start(bf16[16,16,256]{2,1,0:T(8,128)(2,1)S(1)} %get-tuple-element.64.refs_5_), channel_id=1, source_target_pairs={{0,1},{1,0},{2,3},{3,2},{4,5},{5,4},{6,7},{7,6},{8,9},{9,8},{10,11... | collective-permute-start | bytes 393224 | tf_op jit(solution)/shard_map/ppermute | solution.py:430
  51.8 6.3 %collective-permute-start.20 = (bf16[16,16,256]{2,1,0:T(8,128)(2,1)S(1)}, bf16[16,16,256]{2,1,0:T(8,128)(2,1)S(1)}, u32[]{:S(2)}, u32[]{:S(2)}) collective-permute-start(bf16[16,16,256]{2,1,0:T(8,128)(2,1)S(1)} %get-tuple-element.59.refs_1_), channel_id=1, source_target_pairs={{0,2},{2,0},{4,6},{6,4},{8,10},{10,8},{12,14},{14,12},{1,3},{3,1},... | collective-permute-start | bytes 393224 | tf_op jit(solution)/shard_map/ppermute | solution.py:440
  52.8 9.7 %collective-permute-start.19 = (bf16[16,16,256]{2,1,0:T(8,128)(2,1)S(1)}, bf16[16,16,256]{2,1,0:T(8,128)(2,1)S(1)}, u32[]{:S(2)}, u32[]{:S(2)}) collective-permute-start(bf16[16,16,256]{2,1,0:T(8,128)(2,1)S(1)} %get-tuple-element.58.refs_6_), channel_id=1, source_target_pairs={{0,1},{1,0},{2,3},{3,2},{4,5},{5,4},{6,7},{7,6},{8,9},{9,8},{10,11... | collective-permute-start | bytes 393224 | tf_op jit(solution)/shard_map/ppermute | solution.py:430
  53.4 7.6 %collective-permute-start.25 = (bf16[16,16,256]{2,1,0:T(8,128)(2,1)S(1)}, bf16[16,16,256]{2,1,0:T(8,128)(2,1)S(1)}, u32[]{:S(2)}, u32[]{:S(2)}) collective-permute-start(bf16[16,16,256]{2,1,0:T(8,128)(2,1)S(1)} %collective-permute-done.24), channel_id=1, source_target_pairs={{0,2},{2,0},{4,6},{6,4},{8,10},{10,8},{12,14},{14,12},{1,3},{3,1},... | collective-permute-start | bytes 393224 | tf_op jit(solution)/shard_map/ppermute | solution.py:440
  54.6 8.4 %collective-permute-start.29 = (bf16[16,16,256]{2,1,0:T(8,128)(2,1)S(1)}, bf16[16,16,256]{2,1,0:T(8,128)(2,1)S(1)}, u32[]{:S(2)}, u32[]{:S(2)}) collective-permute-start(bf16[16,16,256]{2,1,0:T(8,128)(2,1)S(1)} %get-tuple-element.68.refs_2_), channel_id=1, source_target_pairs={{0,2},{2,0},{4,6},{6,4},{8,10},{10,8},{12,14},{14,12},{1,3},{3,1},... | collective-permute-start | bytes 393224 | tf_op jit(solution)/shard_map/ppermute | solution.py:440
  58.2 4.8 %collective-permute-start.28 = (bf16[16,16,256]{2,1,0:T(8,128)(2,1)S(1)}, bf16[16,16,256]{2,1,0:T(8,128)(2,1)S(1)}, u32[]{:S(2)}, u32[]{:S(2)}) collective-permute-start(bf16[16,16,256]{2,1,0:T(8,128)(2,1)S(1)} %get-tuple-element.67.refs_7_), channel_id=1, source_target_pairs={{0,1},{1,0},{2,3},{3,2},{4,5},{5,4},{6,7},{7,6},{8,9},{9,8},{10,11... | collective-permute-start | bytes 393224 | tf_op jit(solution)/shard_map/ppermute | solution.py:430
  61.4 11.2 %collective-permute-start.31 = (bf16[32,16,256]{2,1,0:T(8,128)(2,1)S(1)}, bf16[32,16,256]{2,1,0:T(8,128)(2,1)S(1)}, u32[]{:S(2)}, u32[]{:S(2)}) collective-permute-start(bf16[32,16,256]{2,1,0:T(8,128)(2,1)S(1)} %mode_sums.6), channel_id=1, source_target_pairs={{0,4},{2,6},{4,8},{6,10},{8,12},{10,14},{12,0},{14,2},{1,5},{3,7},... | collective-permute-start | bytes 786440 | tf_op jit(solution)/shard_map/ppermute | solution.py:435
  62.5 6.4 %collective-permute-start.21 = (bf16[16,16,256]{2,1,0:T(8,128)(2,1)S(1)}, bf16[16,16,256]{2,1,0:T(8,128)(2,1)S(1)}, u32[]{:S(2)}, u32[]{:S(2)}) collective-permute-start(bf16[16,16,256]{2,1,0:T(8,128)(2,1)S(1)} %collective-permute-done.19), channel_id=1, source_target_pairs={{0,2},{2,0},{4,6},{6,4},{8,10},{10,8},{12,14},{14,12},{1,3},{3,1},... | collective-permute-start | bytes 393224 | tf_op jit(solution)/shard_map/ppermute | solution.py:440
  63.0 9.1 %collective-permute-start.30 = (bf16[16,16,256]{2,1,0:T(8,128)(2,1)S(1)}, bf16[16,16,256]{2,1,0:T(8,128)(2,1)S(1)}, u32[]{:S(2)}, u32[]{:S(2)}) collective-permute-start(bf16[16,16,256]{2,1,0:T(8,128)(2,1)S(1)} %collective-permute-done.28), channel_id=1, source_target_pairs={{0,2},{2,0},{4,6},{6,4},{8,10},{10,8},{12,14},{14,12},{1,3},{3,1},... | collective-permute-start | bytes 393224 | tf_op jit(solution)/shard_map/ppermute | solution.py:440
  64.5 7.6 %collective-permute-start.26 = (bf16[16,16,256]{2,1,0:T(8,128)(2,1)S(1)}, bf16[16,16,256]{2,1,0:T(8,128)(2,1)S(1)}, u32[]{:S(2)}, u32[]{:S(2)}) collective-permute-start(bf16[16,16,256]{2,1,0:T(8,128)(2,1)S(1)} %get-tuple-element.65.refs_3_), channel_id=1, source_target_pairs={{0,2},{2,0},{4,6},{6,4},{8,10},{10,8},{12,14},{14,12},{1,3},{3,1},... | collective-permute-start | bytes 393224 | tf_op jit(solution)/shard_map/ppermute | solution.py:440
  65.0 9.6 %collective-permute-start.23 = (bf16[16,16,256]{2,1,0:T(8,128)(2,1)S(1)}, bf16[16,16,256]{2,1,0:T(8,128)(2,1)S(1)}, u32[]{:S(2)}, u32[]{:S(2)}) collective-permute-start(bf16[16,16,256]{2,1,0:T(8,128)(2,1)S(1)} %get-tuple-element.62.refs_4_), channel_id=1, source_target_pairs={{0,1},{1,0},{2,3},{3,2},{4,5},{5,4},{6,7},{7,6},{8,9},{9,8},{10,11... | collective-permute-start | bytes 393224 | tf_op jit(solution)/shard_map/ppermute | solution.py:430
  69.3 16.8 %copy-start.9 = (bf16[8,256,256]{2,1,0:T(8,128)(2,1)S(1)}, bf16[8,256,256]{2,1,0:T(8,128)(2,1)}, u32[]{:S(2)}) copy-start(bf16[8,256,256]{2,1,0:T(8,128)(2,1)} %get-tuple-element.72.grad_ref) | copy-start | bytes 3145732
  69.3 11.6 %collective-permute-start.33 = (bf16[32,16,256]{2,1,0:T(8,128)(2,1)S(1)}, bf16[32,16,256]{2,1,0:T(8,128)(2,1)S(1)}, u32[]{:S(2)}, u32[]{:S(2)}) collective-permute-start(bf16[32,16,256]{2,1,0:T(8,128)(2,1)S(1)} %mode_sums.7), channel_id=1, source_target_pairs={{0,12},{2,14},{4,0},{6,2},{8,4},{10,6},{12,8},{14,10},{1,13},{3,15... | collective-permute-start | bytes 786440 | tf_op jit(solution)/shard_map/ppermute | solution.py:435
  72.7 11.0 %collective-permute-start.32 = (bf16[32,16,256]{2,1,0:T(8,128)(2,1)S(1)}, bf16[32,16,256]{2,1,0:T(8,128)(2,1)S(1)}, u32[]{:S(2)}, u32[]{:S(2)}) collective-permute-start(bf16[32,16,256]{2,1,0:T(8,128)(2,1)S(1)} %add_convert_fusion), channel_id=1, source_target_pairs={{0,4},{2,6},{4,8},{6,10},{8,12},{10,14},{12,0},{14,2},{1,5},{3,7},... | collective-permute-start | bytes 786440 | tf_op jit(solution)/shard_map/ppermute | solution.py:435
  74.1 5.0 %collective-permute-start.22 = (bf16[16,16,256]{2,1,0:T(8,128)(2,1)S(1)}, bf16[16,16,256]{2,1,0:T(8,128)(2,1)S(1)}, u32[]{:S(2)}, u32[]{:S(2)}) collective-permute-start(bf16[16,16,256]{2,1,0:T(8,128)(2,1)S(1)} %get-tuple-element.61.refs_0_), channel_id=1, source_target_pairs={{0,2},{2,0},{4,6},{6,4},{8,10},{10,8},{12,14},{14,12},{1,3},{3,1},... | collective-permute-start | bytes 393224 | tf_op jit(solution)/shard_map/ppermute | solution.py:440
  74.6 5.9 %collective-permute-start.27 = (bf16[16,16,256]{2,1,0:T(8,128)(2,1)S(1)}, bf16[16,16,256]{2,1,0:T(8,128)(2,1)S(1)}, u32[]{:S(2)}, u32[]{:S(2)}) collective-permute-start(bf16[16,16,256]{2,1,0:T(8,128)(2,1)S(1)} %collective-permute-done.23), channel_id=1, source_target_pairs={{0,2},{2,0},{4,6},{6,4},{8,10},{10,8},{12,14},{14,12},{1,3},{3,1},... | collective-permute-start | bytes 393224 | tf_op jit(solution)/shard_map/ppermute | solution.py:440
  84.5 1.2 %collective-permute-start.34 = (f32[2,16,16]{2,1,0:T(8,128)S(1)}, f32[2,16,16]{2,1,0:T(8,128)S(1)}, u32[]{:S(2)}, u32[]{:S(2)}) collective-permute-start(f32[2,16,16]{2,1,0:T(8,128)S(1)} %get-tuple-element.70), channel_id=1, source_target_pairs={{0,1},{1,0},{2,3},{3,2},{4,5},{5,4},{6,7},{7,6},{8,9},{9,8},{10,11... | collective-permute-start | bytes 6152 | tf_op jit(solution)/shard_map/ppermute | solution.py:430
  85.8 3.7 %collective-permute-start.35 = (f32[2,16,16]{2,1,0:T(8,128)S(1)}, f32[2,16,16]{2,1,0:T(8,128)S(1)}, u32[]{:S(2)}, u32[]{:S(2)}) collective-permute-start(f32[2,16,16]{2,1,0:T(8,128)S(1)} %add.31), channel_id=1, source_target_pairs={{0,2},{2,0},{4,6},{6,4},{8,10},{10,8},{12,14},{14,12},{1,3},{3,1},... | collective-permute-start | bytes 6152 | tf_op jit(solution)/shard_map/ppermute | solution.py:538
  89.5 12.1 %collective-permute-start.36 = (f32[320,384]{1,0:T(8,128)S(1)}, f32[320,384]{1,0:T(8,128)S(1)}, u32[]{:S(2)}, u32[]{:S(2)}) collective-permute-start(f32[320,384]{1,0:T(8,128)S(1)} %get-tuple-element.76), channel_id=1, source_target_pairs={{0,1},{1,0},{2,3},{3,2},{4,5},{5,4},{6,7},{7,6},{8,9},{9,8},{10,11... | collective-permute-start | bytes 1474568 | tf_op jit(solution)/shard_map/ppermute | solution.py:430
  89.5 3.8 %collective-permute-start.37 = (f32[2,16,16]{2,1,0:T(8,128)S(1)}, f32[2,16,16]{2,1,0:T(8,128)S(1)}, u32[]{:S(2)}, u32[]{:S(2)}) collective-permute-start(f32[2,16,16]{2,1,0:T(8,128)S(1)} %add.33), channel_id=1, source_target_pairs={{0,4},{2,6},{4,0},{6,2},{8,12},{10,14},{12,8},{14,10},{1,5},{3,7},... | collective-permute-start | bytes 6152 | tf_op jit(solution)/shard_map/ppermute | solution.py:538
  93.3 8.3 %collective-permute-start.38 = (f32[320,384]{1,0:T(8,128)S(1)}, f32[320,384]{1,0:T(8,128)S(1)}, u32[]{:S(2)}, u32[]{:S(2)}) collective-permute-start(f32[320,384]{1,0:T(8,128)S(1)} %get-tuple-element.84), channel_id=1, source_target_pairs={{0,1},{1,0},{2,3},{3,2},{4,5},{5,4},{6,7},{7,6},{8,9},{9,8},{10,11... | collective-permute-start | bytes 1474568 | tf_op jit(solution)/shard_map/ppermute | solution.py:430
  93.3 4.7 %collective-permute-start.39 = (f32[2,16,16]{2,1,0:T(8,128)S(1)}, f32[2,16,16]{2,1,0:T(8,128)S(1)}, u32[]{:S(2)}, u32[]{:S(2)}) collective-permute-start(f32[2,16,16]{2,1,0:T(8,128)S(1)} %add.36), channel_id=1, source_target_pairs={{0,8},{2,10},{4,12},{6,14},{8,0},{10,2},{12,4},{14,6},{1,9},{3,11}... | collective-permute-start | bytes 6152 | tf_op jit(solution)/shard_map/ppermute | solution.py:538
  (5 other events, 41.5 us)

commit v5 on v3

--- a/solution.py
+++ b/solution.py
@@ -588,7 +588,7 @@
         keep0, keep1, cross0, cross1 = updated
         return new_weights_of((after(keep0, token), keep1, cross0, cross1), stash)
 
-    gram, (real, imag, new_weights) = sum_everywhere(gram, [put_back(0), put_back(1), project])
+    gram, (new_weights, real, imag) = sum_everywhere(gram, [project, put_back(0), put_back(1)])
     steps = [mine_sum + swap_tiles(other_sum) for mine_sum, other_sum in (real, imag)]
     new_object = object_field + OBJ_STEP * jnp.stack(steps)
     new_modes = new_modes_of(gram, summed, math.sqrt(pixels)).reshape(probe_modes.shape)

time: 103 us -> 103 us (level)
  no operation moved by 1% of the time
where the time goes in v5:
time: 103 us
  waiting for transfers between devices  36.2 us (35%)
  Pallas kernels  31.5 us (31%)
  starting transfers between devices  27.8 us (27%)
  other arithmetic  5.77 us (6%)
  between operations  1.07 us (1%)
    ppermute x13, waiting for transfers between devices, across(): return lax.ppermute(value, 'scan', [(i, i ^ 1) for i in range(count)])  18.3 us
    ppermute x13, starting transfers between devices, across(): return lax.ppermute(value, 'scan', [(i, i ^ 1) for i in range(count)])  13.4 us
    ppermute x6, starting transfers between devices, turn(): lax.ppermute(value, 'scan', [(i, (i + 2 * step) % count) for i in range(c...  10.5 us
    pallas_call x1, Pallas kernels, relax(): pl.pallas_call(relax_kernel, grid_spec=grid_spec, out_shape=[many, many,...  10 us
    ppermute x6, waiting for transfers between devices, turn(): lax.ppermute(value, 'scan', [(i, (i + 2 * step) % count) for i in range(c...  9.67 us
    pallas_call x1, Pallas kernels, cut_patches(): pl.pallas_call(cut_kernel, grid_spec=grid_spec, out_shape=jax.ShapeDtypeS...  6.17 us
    ppermute x18, waiting for transfers between devices, swap_tiles(): lax.ppermute(value, 'tile', [(i, (i + 1) % count) for i in range(count)])  5.9 us
    pallas_call x2, Pallas kernels, settle(): pl.pallas_call(settle_kernel, grid_spec=grid_spec, out_shape=[shape, shap...  5.24 us
  transfers between devices with their start and end apart: 40, of which 20 were waited for; matrix products, arithmetic and copies ran while one was open for 4% of the time, Pallas kernels for 20%

profile of v5, /device:TPU:0, one launch (start us, length us, event | category | flops | bytes accessed | tf_op | source)
XLA Modules:
  0.0 102.8 jit_solution(5954015304772734359)
XLA Ops:
  0.7 1.1 %convert_element_type.17 = bf16[2,16,4096]{2,1,0:T(8,128)(2,1)S(1)} convert(f32[2,16,4096]{2,1,0:T(8,128)} %param.11) | non-fusion elementwise | flops 131072 | bytes 786432 | tf_op jit(solution)/shard_map/convert_element_type | solution.py:560
  1.9 3.1 %collective-permute-start.2 = (bf16[32,16,256]{2,1,0:T(8,128)(2,1)S(1)}, bf16[32,16,256]{2,1,0:T(8,128)(2,1)S(1)}, u32[]{:S(2)}, u32[]{:S(2)}) collective-permute-start(bf16[32,16,256]{2,1,0:T(8,128)(2,1)S(1)} %bitcast.55), channel_id=1, source_target_pairs={{0,4},{2,6},{4,8},{6,10},{8,12},{10,14},{12,0},{14,2},{1,5},{3,7},... | collective-permute-start | bytes 786440 | tf_op jit(solution)/shard_map/ppermute | solution.py:436
  5.0 2.1 %collective-permute-start.3 = (bf16[32,16,256]{2,1,0:T(8,128)(2,1)S(1)}, bf16[32,16,256]{2,1,0:T(8,128)(2,1)S(1)}, u32[]{:S(2)}, u32[]{:S(2)}) collective-permute-start(bf16[32,16,256]{2,1,0:T(8,128)(2,1)S(1)} %bitcast.56), channel_id=1, source_target_pairs={{0,12},{2,14},{4,0},{6,2},{8,4},{10,6},{12,8},{14,10},{1,13},{3,15... | collective-permute-start | bytes 786440 | tf_op jit(solution)/shard_map/ppermute | solution.py:436
  7.0 1.7 %collective-permute-start.8 = (bf16[32,16,256]{2,1,0:T(8,128)(2,1)S(1)}, bf16[32,16,256]{2,1,0:T(8,128)(2,1)S(1)}, u32[]{:S(2)}, u32[]{:S(2)}) collective-permute-start(bf16[32,16,256]{2,1,0:T(8,128)(2,1)S(1)} %bitcast.57), channel_id=1, source_target_pairs={{0,2},{2,0},{4,6},{6,4},{8,10},{10,8},{12,14},{14,12},{1,3},{3,1},... | collective-permute-start | bytes 786440 | tf_op jit(solution)/shard_map/ppermute | solution.py:441
  8.7 1.3 %convert_element_type.16 = bf16[2,320,384]{2,1,0:T(8,128)(2,1)S(1)} convert(f32[2,320,384]{2,1,0:T(8,128)} %param.10) | non-fusion elementwise | flops 245760 | bytes 1474560 | tf_op jit(solution)/shard_map/convert_element_type | solution.py:561
  10.1 0.7 convert_element_type.15
  11.4 0.7 collective-permute-done.1
  12.0 1.1 %pad_maximum_fusion.obj_ref = bf16[2,2,320,384]{3,2,1,0:T(8,128)(2,1)S(1)} fusion(bf16[1,2,320,384]{3,2,1,0:T(8,128)(2,1)} %bitcast.6, bf16[1,2,320,384]{3,2,1,0:T(8,128)(2,1)S(1)} %convert_bitcast_fusion), kind=kLoop, calls=%fused_computation | loop fusion | flops 491520 | bytes 1966080 | tf_op jit(solution)/shard_map/stack | solution.py:451
  13.3 6.2 %cut_patches.1.refs_16_ = bf16[8,2,256,256]{3,2,1,0:T(8,128)(2,1)S(1)} custom-call(s32[4]{0:T(128)S(1)} %pad_add_fusion.meta_ref, s32[16]{0:T(128)S(1)} %copy-done.2, s32[16]{0:T(128)S(1)} %copy-done.3, s32[16]{0:T(128)S(1)} %copy-done.4, bf16[2,2,320,384]{3,2,1,0:T(8,128)(2,1)S(1)} %pad_maximum_fusion.obj_ref), custom_call_target="tpu_custom_call" | custom-call | flops 4294967296 | bytes 4194304 | tf_op jit(solution)/shard_map/cut_patches/pallas_call | solution.py:77
  19.6 1.4 %collective-permute-start.4 = (bf16[32,16,256]{2,1,0:T(8,128)(2,1)S(1)}, bf16[32,16,256]{2,1,0:T(8,128)(2,1)S(1)}, u32[]{:S(2)}, u32[]{:S(2)}) collective-permute-start(bf16[32,16,256]{2,1,0:T(8,128)(2,1)S(1)} %collective-permute-done.3.refs_3_), channel_id=1, source_target_pairs={{0,2},{2,0},{4,6},{6,4},{8,10},{10,8},{12,14},{14,12},{1,3},{3,1},... | collective-permute-start | bytes 786440 | tf_op jit(solution)/shard_map/ppermute | solution.py:441
  21.0 0.5 collective-permute-start.11
  21.5 0.6 collective-permute-done
  22.2 0.7 collective-permute-start.10
  22.8 6.9 %collective-permute-done.7.refs_1_ = bf16[32,16,256]{2,1,0:T(8,128)(2,1)S(1)} collective-permute-done((bf16[32,16,256]{2,1,0:T(8,128)(2,1)S(1)}, bf16[32,16,256]{2,1,0:T(8,128)(2,1)S(1)}, u32[]{:S(2)}, u32[]{:S(2)}) %collective-permute-start.7) | collective-permute-done | bytes 262176 | tf_op jit(solution)/shard_map/ppermute | solution.py:436
  30.1 1.5 %collective-permute-done.5.refs_15_ = bf16[32,16,256]{2,1,0:T(8,128)(2,1)S(1)} collective-permute-done((bf16[32,16,256]{2,1,0:T(8,128)(2,1)S(1)}, bf16[32,16,256]{2,1,0:T(8,128)(2,1)S(1)}, u32[]{:S(2)}, u32[]{:S(2)}) %collective-permute-start.5) | collective-permute-done | bytes 262176 | tf_op jit(solution)/shard_map/ppermute | solution.py:431
  31.6 1.7 %collective-permute-start.6 = (bf16[2,2,8,16]{3,2,1,0:T(8,128)(2,1)S(1)}, bf16[2,2,8,16]{3,2,1,0:T(8,128)(2,1)S(1)}, u32[]{:S(2)}, u32[]{:S(2)}) collective-permute-start(bf16[2,2,8,16]{3,2,1,0:T(8,128)(2,1)S(1)} %pad_maximum_fusion.1), channel_id=1, source_target_pairs={{0,2},{2,0},{4,6},{6,4},{8,10},{10,8},{12,14},{14,12},{1,3},{3,1},... | collective-permute-start | bytes 3080 | tf_op jit(solution)/shard_map/ppermute | solution.py:441
  33.8 0.6 collective-permute-done.10.refs_6_
  34.4 4.9 %collective-permute-done.9.refs_5_ = bf16[32,16,256]{2,1,0:T(8,128)(2,1)S(1)} collective-permute-done((bf16[32,16,256]{2,1,0:T(8,128)(2,1)S(1)}, bf16[32,16,256]{2,1,0:T(8,128)(2,1)S(1)}, u32[]{:S(2)}, u32[]{:S(2)}) %collective-permute-start.9) | collective-permute-done | bytes 262176 | tf_op jit(solution)/shard_map/ppermute | solution.py:441
  39.8 1.0 collective-permute-done.17.refs_14_
  41.2 10.0 %relax_positions.1 = (bf16[4,16,16,256]{3,2,1,0:T(8,128)(2,1)S(1)}, bf16[4,16,16,256]{3,2,1,0:T(8,128)(2,1)S(1)}, bf16[16,16,256]{2,1,0:T(8,128)(2,1)S(1)}, bf16...) custom-call(s32[4]{0:T(128)S(1)} %pad_add_fusion.meta_ref, ...), custom_call_target="tpu_custom_call" | custom-call | flops 8589934592 | bytes 16777216 | tf_op jit(solution)/shard_map/relax_positions/pallas_call | solution.py:217
  51.8 1.0 collective-permute-start.20
  52.9 0.5 collective-permute-done.24
  53.4 1.0 collective-permute-start.25
  54.6 1.1 %collective-permute-start.29 = (bf16[16,16,256]{2,1,0:T(8,128)(2,1)S(1)}, bf16[16,16,256]{2,1,0:T(8,128)(2,1)S(1)}, u32[]{:S(2)}, u32[]{:S(2)}) collective-permute-start(bf16[16,16,256]{2,1,0:T(8,128)(2,1)S(1)} %get-tuple-element.68.refs_2_), channel_id=1, source_target_pairs={{0,2},{2,0},{4,6},{6,4},{8,10},{10,8},{12,14},{14,12},{1,3},{3,1},... | collective-permute-start | bytes 393224 | tf_op jit(solution)/shard_map/ppermute | solution.py:441
  55.7 2.4 %collective-permute-done.20.far_ref = bf16[16,16,256]{2,1,0:T(8,128)(2,1)S(1)} collective-permute-done((bf16[16,16,256]{2,1,0:T(8,128)(2,1)S(1)}, bf16[16,16,256]{2,1,0:T(8,128)(2,1)S(1)}, u32[]{:S(2)}, u32[]{:S(2)}) %collective-permute-start.20) | collective-permute-done | bytes 131104 | tf_op jit(solution)/shard_map/ppermute | solution.py:441
  58.2 0.8 widen.3.wide_ref
  59.0 2.0 %collective-permute-done.25.far_twin_ref = bf16[16,16,256]{2,1,0:T(8,128)(2,1)S(1)} collective-permute-done((bf16[16,16,256]{2,1,0:T(8,128)(2,1)S(1)}, bf16[16,16,256]{2,1,0:T(8,128)(2,1)S(1)}, u32[]{:S(2)}, u32[]{:S(2)}) %collective-permute-start.25) | collective-permute-done | bytes 131104 | tf_op jit(solution)/shard_map/ppermute | solution.py:441
  61.4 1.0 %collective-permute-start.31 = (bf16[32,16,256]{2,1,0:T(8,128)(2,1)S(1)}, bf16[32,16,256]{2,1,0:T(8,128)(2,1)S(1)}, u32[]{:S(2)}, u32[]{:S(2)}) collective-permute-start(bf16[32,16,256]{2,1,0:T(8,128)(2,1)S(1)} %mode_sums.6), channel_id=1, source_target_pairs={{0,4},{2,6},{4,8},{6,10},{8,12},{10,14},{12,0},{14,2},{1,5},{3,7},... | collective-permute-start | bytes 786440 | tf_op jit(solution)/shard_map/ppermute | solution.py:436
  62.5 0.5 collective-permute-start.21
  63.0 1.5 %collective-permute-start.30 = (bf16[16,16,256]{2,1,0:T(8,128)(2,1)S(1)}, bf16[16,16,256]{2,1,0:T(8,128)(2,1)S(1)}, u32[]{:S(2)}, u32[]{:S(2)}) collective-permute-start(bf16[16,16,256]{2,1,0:T(8,128)(2,1)S(1)} %collective-permute-done.28), channel_id=1, source_target_pairs={{0,2},{2,0},{4,6},{6,4},{8,10},{10,8},{12,14},{14,12},{1,3},{3,1},... | collective-permute-start | bytes 393224 | tf_op jit(solution)/shard_map/ppermute | solution.py:441
  64.5 0.5 collective-permute-start.26
  65.0 3.8 %collective-permute-done.21.far_twin_ref = bf16[16,16,256]{2,1,0:T(8,128)(2,1)S(1)} collective-permute-done((bf16[16,16,256]{2,1,0:T(8,128)(2,1)S(1)}, bf16[16,16,256]{2,1,0:T(8,128)(2,1)S(1)}, u32[]{:S(2)}, u32[]{:S(2)}) %collective-permute-start.21) | collective-permute-done | bytes 131104 | tf_op jit(solution)/shard_map/ppermute | solution.py:441
  69.3 2.8 %collective-permute-start.33 = (bf16[32,16,256]{2,1,0:T(8,128)(2,1)S(1)}, bf16[32,16,256]{2,1,0:T(8,128)(2,1)S(1)}, u32[]{:S(2)}, u32[]{:S(2)}) collective-permute-start(bf16[32,16,256]{2,1,0:T(8,128)(2,1)S(1)} %mode_sums.7), channel_id=1, source_target_pairs={{0,12},{2,14},{4,0},{6,2},{8,4},{10,6},{12,8},{14,10},{1,13},{3,15... | collective-permute-start | bytes 786440 | tf_op jit(solution)/shard_map/ppermute | solution.py:436
  72.7 1.4 %collective-permute-start.32 = (bf16[32,16,256]{2,1,0:T(8,128)(2,1)S(1)}, bf16[32,16,256]{2,1,0:T(8,128)(2,1)S(1)}, u32[]{:S(2)}, u32[]{:S(2)}) collective-permute-start(bf16[32,16,256]{2,1,0:T(8,128)(2,1)S(1)} %add_convert_fusion), channel_id=1, source_target_pairs={{0,4},{2,6},{4,8},{6,10},{8,12},{10,14},{12,0},{14,2},{1,5},{3,7},... | collective-permute-start | bytes 786440 | tf_op jit(solution)/shard_map/ppermute | solution.py:436
  74.6 1.5 %collective-permute-start.27 = (bf16[16,16,256]{2,1,0:T(8,128)(2,1)S(1)}, bf16[16,16,256]{2,1,0:T(8,128)(2,1)S(1)}, u32[]{:S(2)}, u32[]{:S(2)}) collective-permute-start(bf16[16,16,256]{2,1,0:T(8,128)(2,1)S(1)} %collective-permute-done.23), channel_id=1, source_target_pairs={{0,2},{2,0},{4,6},{6,4},{8,10},{10,8},{12,14},{14,12},{1,3},{3,1},... | collective-permute-start | bytes 393224 | tf_op jit(solution)/shard_map/ppermute | solution.py:441
  76.1 2.9 %collective-permute-done.22.far_ref = bf16[16,16,256]{2,1,0:T(8,128)(2,1)S(1)} collective-permute-done((bf16[16,16,256]{2,1,0:T(8,128)(2,1)S(1)}, bf16[16,16,256]{2,1,0:T(8,128)(2,1)S(1)}, u32[]{:S(2)}, u32[]{:S(2)}) %collective-permute-start.22) | collective-permute-done | bytes 131104 | tf_op jit(solution)/shard_map/ppermute | solution.py:441
  79.1 1.4 %collective-permute-done.27.far_twin_ref = bf16[16,16,256]{2,1,0:T(8,128)(2,1)S(1)} collective-permute-done((bf16[16,16,256]{2,1,0:T(8,128)(2,1)S(1)}, bf16[16,16,256]{2,1,0:T(8,128)(2,1)S(1)}, u32[]{:S(2)}, u32[]{:S(2)}) %collective-permute-start.27) | collective-permute-done | bytes 131104 | tf_op jit(solution)/shard_map/ppermute | solution.py:441
  80.9 2.8 %collective-permute-done.32.refs_1_ = bf16[32,16,256]{2,1,0:T(8,128)(2,1)S(1)} collective-permute-done((bf16[32,16,256]{2,1,0:T(8,128)(2,1)S(1)}, bf16[32,16,256]{2,1,0:T(8,128)(2,1)S(1)}, u32[]{:S(2)}, u32[]{:S(2)}) %collective-permute-start.32) | collective-permute-done | bytes 262176 | tf_op jit(solution)/shard_map/ppermute | solution.py:436
  83.7 0.8 finish_sums.1
  84.6 1.2 %collective-permute-done.34 = f32[2,16,16]{2,1,0:T(8,128)S(1)} collective-permute-done((f32[2,16,16]{2,1,0:T(8,128)S(1)}, f32[2,16,16]{2,1,0:T(8,128)S(1)}, u32[]{:S(2)}, u32[]{:S(2)}) %collective-permute-start.34) | collective-permute-done | bytes 2080 | tf_op jit(solution)/shard_map/ppermute | solution.py:431
  86.1 2.9 %new_weights.1 = f32[2,8,16]{2,1,0:T(8,128)} custom-call(bf16[4,16,16,256]{3,2,1,0:T(8,128)(2,1)S(1)} %get-tuple-element.71.near_ref.keep0_ref, bf16[4,16,16,256]{3,2,1,0:T(8,128)(2,1)S(1)} %get-tuple-element.56.keep1_ref, bf16[16,16,256]{2,1,0:T(8,128)(2,1)S(1)} %get-tuple-element.61.refs_0_, bf16[16,16,256]{2,1,0:T(8,128)(2,1)S(1)} %get-tuple-element.59.refs_1_, ...), custom_call_target="tpu_custom_call" | custom-call | flops 2147483648 | bytes 6291456 | tf_op jit(solution)/shard_map/new_weights/pallas_call | solution.py:311
  89.5 2.6 %settle.2 = (f32[320,384]{1,0:T(8,128)S(1)}, f32[320,384]{1,0:T(8,128)S(1)}) custom-call(s32[4]{0:T(128)S(1)} %pad_add_fusion.meta_ref, s32[16]{0:T(128)S(1)} %copy-done.2, s32[16]{0:T(128)S(1)} %copy-done.3, s32[16]{0:T(128)S(1)} %copy-done.4, bf16[8,256,256]{2,1,0:T(8,128)(2,1)S(1)} %copy-done.9), custom_call_target="tpu_custom_call" | custom-call | flops 2147483648 | bytes 4194304 | tf_op jit(solution)/shard_map/settle/pallas_call | solution.py:261
  92.1 1.1 %collective-permute-done.36 = f32[2,16,16]{2,1,0:T(8,128)S(1)} collective-permute-done((f32[2,16,16]{2,1,0:T(8,128)S(1)}, f32[2,16,16]{2,1,0:T(8,128)S(1)}, u32[]{:S(2)}, u32[]{:S(2)}) %collective-permute-start.36) | collective-permute-done | bytes 2080 | tf_op jit(solution)/shard_map/ppermute | solution.py:539
  93.3 1.3 %collective-permute-start.38 = (f32[2,16,16]{2,1,0:T(8,128)S(1)}, f32[2,16,16]{2,1,0:T(8,128)S(1)}, u32[]{:S(2)}, u32[]{:S(2)}) collective-permute-start(f32[2,16,16]{2,1,0:T(8,128)S(1)} %add.34), channel_id=1, source_target_pairs={{0,8},{2,10},{4,12},{6,14},{8,0},{10,2},{12,4},{14,6},{1,9},{3,11}... | collective-permute-start | bytes 6152 | tf_op jit(solution)/shard_map/ppermute | solution.py:539
  94.6 2.6 %settle.3 = (f32[320,384]{1,0:T(8,128)S(1)}, f32[320,384]{1,0:T(8,128)S(1)}) custom-call(s32[4]{0:T(128)S(1)} %pad_add_fusion.meta_ref, s32[16]{0:T(128)S(1)} %copy-done.2, s32[16]{0:T(128)S(1)} %copy-done.3, s32[16]{0:T(128)S(1)} %copy-done.4, bf16[8,256,256]{2,1,0:T(8,128)(2,1)S(1)} %copy-done.8), custom_call_target="tpu_custom_call" | custom-call | flops 2147483648 | bytes 4194304 | tf_op jit(solution)/shard_map/settle/pallas_call | solution.py:261
  97.2 0.8 collective-permute-done.38
  98.1 3.6 %orthonormal_modes.1 = f32[32,4096]{1,0:T(8,128)} custom-call(f32[2,16,16]{2,1,0:T(8,128)S(1)} %add.37.gram_ref, f32[32,4096]{1,0:T(8,128)S(1)} %get-tuple-element.91.sum_ref), custom_call_target="tpu_custom_call" | custom-call | flops 134217728 | bytes 1048576 | tf_op jit(solution)/shard_map/orthonormal_modes/pallas_call | solution.py:420
  101.8 1.0 %fusion = f32[2,320,384]{2,1,0:T(8,128)} fusion(f32[2,320,384]{2,1,0:T(8,128)S(1)} %copy-done.11, f32[1,320,384]{2,1,0:T(8,128)S(1)} %add_bitcast_fusion, f32[1,320,384]{2,1,0:T(8,128)S(1)} %add_bitcast_fusion.1), kind=kLoop, calls=%fused_computation.2 | loop fusion | flops 737280 | bytes 2949120 | tf_op jit(solution)/shard_map/add | solution.py:593
  (102 shorter events, 6.9 us)
Async XLA Ops:
  0.6 12.5 %copy-start.2 = (s32[16]{0:T(128)S(1)}, s32[16]{0:T(128)}, u32[]{:S(2)}) copy-start(s32[16]{0:T(128)} %owner_ref.5) | copy-start | bytes 196
  0.7 12.5 %copy-start.3 = (s32[16]{0:T(128)S(1)}, s32[16]{0:T(128)}, u32[]{:S(2)}) copy-start(s32[16]{0:T(128)} %row_ref.5) | copy-start | bytes 196
  1.9 17.6 %collective-permute-start.2 = (bf16[32,16,256]{2,1,0:T(8,128)(2,1)S(1)}, bf16[32,16,256]{2,1,0:T(8,128)(2,1)S(1)}, u32[]{:S(2)}, u32[]{:S(2)}) collective-permute-start(bf16[32,16,256]{2,1,0:T(8,128)(2,1)S(1)} %bitcast.55), channel_id=1, source_target_pairs={{0,4},{2,6},{4,8},{6,10},{8,12},{10,14},{12,0},{14,2},{1,5},{3,7},... | collective-permute-start | bytes 786440 | tf_op jit(solution)/shard_map/ppermute | solution.py:436
  5.0 14.5 %collective-permute-start.3 = (bf16[32,16,256]{2,1,0:T(8,128)(2,1)S(1)}, bf16[32,16,256]{2,1,0:T(8,128)(2,1)S(1)}, u32[]{:S(2)}, u32[]{:S(2)}) collective-permute-start(bf16[32,16,256]{2,1,0:T(8,128)(2,1)S(1)} %bitcast.56), channel_id=1, source_target_pairs={{0,12},{2,14},{4,0},{6,2},{8,4},{10,6},{12,8},{14,10},{1,13},{3,15... | collective-permute-start | bytes 786440 | tf_op jit(solution)/shard_map/ppermute | solution.py:436
  7.0 14.5 %collective-permute-start.8 = (bf16[32,16,256]{2,1,0:T(8,128)(2,1)S(1)}, bf16[32,16,256]{2,1,0:T(8,128)(2,1)S(1)}, u32[]{:S(2)}, u32[]{:S(2)}) collective-permute-start(bf16[32,16,256]{2,1,0:T(8,128)(2,1)S(1)} %bitcast.57), channel_id=1, source_target_pairs={{0,2},{2,0},{4,6},{6,4},{8,10},{10,8},{12,14},{14,12},{1,3},{3,1},... | collective-permute-start | bytes 786440 | tf_op jit(solution)/shard_map/ppermute | solution.py:441
  10.0 2.1 %collective-permute-start.1 = (bf16[2,320,384]{2,1,0:T(8,128)(2,1)S(1)}, bf16[2,320,384]{2,1,0:T(8,128)(2,1)}, u32[]{:S(2)}, u32[]{:S(2)}) collective-permute-start(bf16[2,320,384]{2,1,0:T(8,128)(2,1)S(1)} %convert_element_type.16), channel_id=1, source_target_pairs={{0,1},{1,0},{2,3},{3,2},{4,5},{5,4},{6,7},{7,6},{8,9},{9,8},{10,11... | collective-permute-start | bytes 1474568 | tf_op jit(solution)/shard_map/ppermute | solution.py:431
  13.2 16.8 %copy-start.12 = (f32[2,8,16]{2,1,0:T(8,128)S(1)}, f32[2,8,16]{2,1,0:T(8,128)}, u32[]{:S(2)}) copy-start(f32[2,8,16]{2,1,0:T(8,128)} %param.12) | copy-start | bytes 3076
  13.2 28.0 %copy-start = (bf16[8,256,256]{2,1,0:T(8,128)(2,1)S(1)}, bf16[8,256,256]{2,1,0:T(8,128)(2,1)}, u32[]{:S(2)}) copy-start(bf16[8,256,256]{2,1,0:T(8,128)(2,1)} %refs_17_.1) | copy-start | bytes 3145732
  13.2 28.0 %copy-start.1 = (s32[2]{0:T(128)S(1)}, s32[2]{0:T(128)}, u32[]{:S(2)}) copy-start(s32[2]{0:T(128)} %live_ref.1) | copy-start | bytes 28
  13.3 27.9 %copy-start.5 = (bf16[512,512]{1,0:T(8,128)(2,1)S(1)}, bf16[512,512]{1,0:T(8,128)(2,1)}, u32[]{:S(2)}) copy-start(bf16[512,512]{1,0:T(8,128)(2,1)} %constant.38.clone.refs_18_) | copy-start | bytes 1572868
  13.3 27.9 %copy-start.6 = (bf16[512,512]{1,0:T(8,128)(2,1)S(1)}, bf16[512,512]{1,0:T(8,128)(2,1)}, u32[]{:S(2)}) copy-start(bf16[512,512]{1,0:T(8,128)(2,1)} %constant.39.clone.refs_19_) | copy-start | bytes 1572868
  19.5 10.2 %collective-permute-start.7 = (bf16[32,16,256]{2,1,0:T(8,128)(2,1)S(1)}, bf16[32,16,256]{2,1,0:T(8,128)(2,1)S(1)}, u32[]{:S(2)}, u32[]{:S(2)}) collective-permute-start(bf16[32,16,256]{2,1,0:T(8,128)(2,1)S(1)} %collective-permute-done.2.refs_2_), channel_id=1, source_target_pairs={{0,4},{2,6},{4,8},{6,10},{8,12},{10,14},{12,0},{14,2},{1,5},{3,7},... | collective-permute-start | bytes 786440 | tf_op jit(solution)/shard_map/ppermute | solution.py:436
  19.6 10.5 %collective-permute-start.4 = (bf16[32,16,256]{2,1,0:T(8,128)(2,1)S(1)}, bf16[32,16,256]{2,1,0:T(8,128)(2,1)S(1)}, u32[]{:S(2)}, u32[]{:S(2)}) collective-permute-start(bf16[32,16,256]{2,1,0:T(8,128)(2,1)S(1)} %collective-permute-done.3.refs_3_), channel_id=1, source_target_pairs={{0,2},{2,0},{4,6},{6,4},{8,10},{10,8},{12,14},{14,12},{1,3},{3,1},... | collective-permute-start | bytes 786440 | tf_op jit(solution)/shard_map/ppermute | solution.py:441
  21.0 1.2 %collective-permute-start = (bf16[2,8,16]{2,1,0:T(8,128)(2,1)S(1)}, bf16[2,8,16]{2,1,0:T(8,128)(2,1)S(1)}, u32[]{:S(2)}, u32[]{:S(2)}) collective-permute-start(bf16[2,8,16]{2,1,0:T(8,128)(2,1)S(1)} %convert_element_type.15), channel_id=1, source_target_pairs={{0,1},{1,0},{2,3},{3,2},{4,5},{5,4},{6,7},{7,6},{8,9},{9,8},{10,11... | collective-permute-start | bytes 1544 | tf_op jit(solution)/shard_map/ppermute | solution.py:431
  21.0 12.3 %collective-permute-start.11 = (bf16[32,16,256]{2,1,0:T(8,128)(2,1)S(1)}, bf16[32,16,256]{2,1,0:T(8,128)(2,1)S(1)}, u32[]{:S(2)}, u32[]{:S(2)}) collective-permute-start(bf16[32,16,256]{2,1,0:T(8,128)(2,1)S(1)} %bitcast.58), channel_id=1, source_target_pairs={{0,1},{1,0},{2,3},{3,2},{4,5},{5,4},{6,7},{7,6},{8,9},{9,8},{10,11... | collective-permute-start | bytes 786440 | tf_op jit(solution)/shard_map/ppermute | solution.py:431
  21.5 11.8 %collective-permute-start.15 = (bf16[32,16,256]{2,1,0:T(8,128)(2,1)S(1)}, bf16[32,16,256]{2,1,0:T(8,128)(2,1)S(1)}, u32[]{:S(2)}, u32[]{:S(2)}) collective-permute-start(bf16[32,16,256]{2,1,0:T(8,128)(2,1)S(1)} %collective-permute-done.8.refs_4_), channel_id=1, source_target_pairs={{0,1},{1,0},{2,3},{3,2},{4,5},{5,4},{6,7},{7,6},{8,9},{9,8},{10,11... | collective-permute-start | bytes 786440 | tf_op jit(solution)/shard_map/ppermute | solution.py:431
  22.2 12.2 %collective-permute-start.10 = (bf16[32,16,256]{2,1,0:T(8,128)(2,1)S(1)}, bf16[32,16,256]{2,1,0:T(8,128)(2,1)S(1)}, u32[]{:S(2)}, u32[]{:S(2)}) collective-permute-start(bf16[32,16,256]{2,1,0:T(8,128)(2,1)S(1)} %collective-permute-done.2.refs_2_), channel_id=1, source_target_pairs={{0,2},{2,0},{4,6},{6,4},{8,10},{10,8},{12,14},{14,12},{1,3},{3,1},... | collective-permute-start | bytes 786440 | tf_op jit(solution)/shard_map/ppermute | solution.py:441
  29.7 9.6 %collective-permute-start.9 = (bf16[32,16,256]{2,1,0:T(8,128)(2,1)S(1)}, bf16[32,16,256]{2,1,0:T(8,128)(2,1)S(1)}, u32[]{:S(2)}, u32[]{:S(2)}) collective-permute-start(bf16[32,16,256]{2,1,0:T(8,128)(2,1)S(1)} %collective-permute-done.7.refs_1_), channel_id=1, source_target_pairs={{0,2},{2,0},{4,6},{6,4},{8,10},{10,8},{12,14},{14,12},{1,3},{3,1},... | collective-permute-start | bytes 786440 | tf_op jit(solution)/shard_map/ppermute | solution.py:441
  30.0 1.5 %collective-permute-start.5 = (bf16[32,16,256]{2,1,0:T(8,128)(2,1)S(1)}, bf16[32,16,256]{2,1,0:T(8,128)(2,1)S(1)}, u32[]{:S(2)}, u32[]{:S(2)}) collective-permute-start(bf16[32,16,256]{2,1,0:T(8,128)(2,1)S(1)} %collective-permute-done.4.refs_7_), channel_id=1, source_target_pairs={{0,1},{1,0},{2,3},{3,2},{4,5},{5,4},{6,7},{7,6},{8,9},{9,8},{10,11... | collective-permute-start | bytes 786440 | tf_op jit(solution)/shard_map/ppermute | solution.py:431
  31.6 7.8 %collective-permute-start.6 = (bf16[2,2,8,16]{3,2,1,0:T(8,128)(2,1)S(1)}, bf16[2,2,8,16]{3,2,1,0:T(8,128)(2,1)S(1)}, u32[]{:S(2)}, u32[]{:S(2)}) collective-permute-start(bf16[2,2,8,16]{3,2,1,0:T(8,128)(2,1)S(1)} %pad_maximum_fusion.1), channel_id=1, source_target_pairs={{0,2},{2,0},{4,6},{6,4},{8,10},{10,8},{12,14},{14,12},{1,3},{3,1},... | collective-permute-start | bytes 3080 | tf_op jit(solution)/shard_map/ppermute | solution.py:441
  33.3 6.6 %collective-permute-start.13 = (bf16[32,16,256]{2,1,0:T(8,128)(2,1)S(1)}, bf16[32,16,256]{2,1,0:T(8,128)(2,1)S(1)}, u32[]{:S(2)}, u32[]{:S(2)}) collective-permute-start(bf16[32,16,256]{2,1,0:T(8,128)(2,1)S(1)} %collective-permute-done.2.refs_2_), channel_id=1, source_target_pairs={{0,1},{1,0},{2,3},{3,2},{4,5},{5,4},{6,7},{7,6},{8,9},{9,8},{10,11... | collective-permute-start | bytes 786440 | tf_op jit(solution)/shard_map/ppermute | solution.py:431
  33.3 6.6 %collective-permute-start.14 = (bf16[32,16,256]{2,1,0:T(8,128)(2,1)S(1)}, bf16[32,16,256]{2,1,0:T(8,128)(2,1)S(1)}, u32[]{:S(2)}, u32[]{:S(2)}) collective-permute-start(bf16[32,16,256]{2,1,0:T(8,128)(2,1)S(1)} %collective-permute-done.3.refs_3_), channel_id=1, source_target_pairs={{0,1},{1,0},{2,3},{3,2},{4,5},{5,4},{6,7},{7,6},{8,9},{9,8},{10,11... | collective-permute-start | bytes 786440 | tf_op jit(solution)/shard_map/ppermute | solution.py:431
  34.4 5.4 %collective-permute-start.12 = (bf16[32,16,256]{2,1,0:T(8,128)(2,1)S(1)}, bf16[32,16,256]{2,1,0:T(8,128)(2,1)S(1)}, u32[]{:S(2)}, u32[]{:S(2)}) collective-permute-start(bf16[32,16,256]{2,1,0:T(8,128)(2,1)S(1)} %collective-permute-done.7.refs_1_), channel_id=1, source_target_pairs={{0,1},{1,0},{2,3},{3,2},{4,5},{5,4},{6,7},{7,6},{8,9},{9,8},{10,11... | collective-permute-start | bytes 786440 | tf_op jit(solution)/shard_map/ppermute | solution.py:431
  39.3 1.5 %collective-permute-start.17 = (bf16[32,16,256]{2,1,0:T(8,128)(2,1)S(1)}, bf16[32,16,256]{2,1,0:T(8,128)(2,1)S(1)}, u32[]{:S(2)}, u32[]{:S(2)}) collective-permute-start(bf16[32,16,256]{2,1,0:T(8,128)(2,1)S(1)} %collective-permute-done.10.refs_6_), channel_id=1, source_target_pairs={{0,1},{1,0},{2,3},{3,2},{4,5},{5,4},{6,7},{7,6},{8,9},{9,8},{10,11... | collective-permute-start | bytes 786440 | tf_op jit(solution)/shard_map/ppermute | solution.py:431
  39.4 1.8 %collective-permute-start.16 = (bf16[32,16,256]{2,1,0:T(8,128)(2,1)S(1)}, bf16[32,16,256]{2,1,0:T(8,128)(2,1)S(1)}, u32[]{:S(2)}, u32[]{:S(2)}) collective-permute-start(bf16[32,16,256]{2,1,0:T(8,128)(2,1)S(1)} %collective-permute-done.9.refs_5_), channel_id=1, source_target_pairs={{0,1},{1,0},{2,3},{3,2},{4,5},{5,4},{6,7},{7,6},{8,9},{9,8},{10,11... | collective-permute-start | bytes 786440 | tf_op jit(solution)/shard_map/ppermute | solution.py:431
  51.2 9.7 %collective-permute-start.18 = (bf16[4,16,16,256]{3,2,1,0:T(8,128)(2,1)S(1)}, bf16[4,16,16,256]{3,2,1,0:T(8,128)(2,1)S(1)}, u32[]{:S(2)}, u32[]{:S(2)}) collective-permute-start(bf16[4,16,16,256]{3,2,1,0:T(8,128)(2,1)S(1)} %get-tuple-element.56.keep1_ref), channel_id=1, source_target_pairs={{0,1},{1,0},{2,3},{3,2},{4,5},{5,4},{6,7},{7,6},{8,9},{9,8},{10,11... | collective-permute-start | bytes 1572872 | tf_op jit(solution)/shard_map/ppermute | solution.py:431
  51.5 2.0 %collective-permute-start.24 = (bf16[16,16,256]{2,1,0:T(8,128)(2,1)S(1)}, bf16[16,16,256]{2,1,0:T(8,128)(2,1)S(1)}, u32[]{:S(2)}, u32[]{:S(2)}) collective-permute-start(bf16[16,16,256]{2,1,0:T(8,128)(2,1)S(1)} %get-tuple-element.64.refs_5_), channel_id=1, source_target_pairs={{0,1},{1,0},{2,3},{3,2},{4,5},{5,4},{6,7},{7,6},{8,9},{9,8},{10,11... | collective-permute-start | bytes 393224 | tf_op jit(solution)/shard_map/ppermute | solution.py:431
  51.8 6.3 %collective-permute-start.20 = (bf16[16,16,256]{2,1,0:T(8,128)(2,1)S(1)}, bf16[16,16,256]{2,1,0:T(8,128)(2,1)S(1)}, u32[]{:S(2)}, u32[]{:S(2)}) collective-permute-start(bf16[16,16,256]{2,1,0:T(8,128)(2,1)S(1)} %get-tuple-element.59.refs_1_), channel_id=1, source_target_pairs={{0,2},{2,0},{4,6},{6,4},{8,10},{10,8},{12,14},{14,12},{1,3},{3,1},... | collective-permute-start | bytes 393224 | tf_op jit(solution)/shard_map/ppermute | solution.py:441
  52.8 9.7 %collective-permute-start.19 = (bf16[16,16,256]{2,1,0:T(8,128)(2,1)S(1)}, bf16[16,16,256]{2,1,0:T(8,128)(2,1)S(1)}, u32[]{:S(2)}, u32[]{:S(2)}) collective-permute-start(bf16[16,16,256]{2,1,0:T(8,128)(2,1)S(1)} %get-tuple-element.58.refs_6_), channel_id=1, source_target_pairs={{0,1},{1,0},{2,3},{3,2},{4,5},{5,4},{6,7},{7,6},{8,9},{9,8},{10,11... | collective-permute-start | bytes 393224 | tf_op jit(solution)/shard_map/ppermute | solution.py:431
  53.4 7.6 %collective-permute-start.25 = (bf16[16,16,256]{2,1,0:T(8,128)(2,1)S(1)}, bf16[16,16,256]{2,1,0:T(8,128)(2,1)S(1)}, u32[]{:S(2)}, u32[]{:S(2)}) collective-permute-start(bf16[16,16,256]{2,1,0:T(8,128)(2,1)S(1)} %collective-permute-done.24), channel_id=1, source_target_pairs={{0,2},{2,0},{4,6},{6,4},{8,10},{10,8},{12,14},{14,12},{1,3},{3,1},... | collective-permute-start | bytes 393224 | tf_op jit(solution)/shard_map/ppermute | solution.py:441
  54.6 8.4 %collective-permute-start.29 = (bf16[16,16,256]{2,1,0:T(8,128)(2,1)S(1)}, bf16[16,16,256]{2,1,0:T(8,128)(2,1)S(1)}, u32[]{:S(2)}, u32[]{:S(2)}) collective-permute-start(bf16[16,16,256]{2,1,0:T(8,128)(2,1)S(1)} %get-tuple-element.68.refs_2_), channel_id=1, source_target_pairs={{0,2},{2,0},{4,6},{6,4},{8,10},{10,8},{12,14},{14,12},{1,3},{3,1},... | collective-permute-start | bytes 393224 | tf_op jit(solution)/shard_map/ppermute | solution.py:441
  58.2 4.8 %collective-permute-start.28 = (bf16[16,16,256]{2,1,0:T(8,128)(2,1)S(1)}, bf16[16,16,256]{2,1,0:T(8,128)(2,1)S(1)}, u32[]{:S(2)}, u32[]{:S(2)}) collective-permute-start(bf16[16,16,256]{2,1,0:T(8,128)(2,1)S(1)} %get-tuple-element.67.refs_7_), channel_id=1, source_target_pairs={{0,1},{1,0},{2,3},{3,2},{4,5},{5,4},{6,7},{7,6},{8,9},{9,8},{10,11... | collective-permute-start | bytes 393224 | tf_op jit(solution)/shard_map/ppermute | solution.py:431
  61.4 11.2 %collective-permute-start.31 = (bf16[32,16,256]{2,1,0:T(8,128)(2,1)S(1)}, bf16[32,16,256]{2,1,0:T(8,128)(2,1)S(1)}, u32[]{:S(2)}, u32[]{:S(2)}) collective-permute-start(bf16[32,16,256]{2,1,0:T(8,128)(2,1)S(1)} %mode_sums.6), channel_id=1, source_target_pairs={{0,4},{2,6},{4,8},{6,10},{8,12},{10,14},{12,0},{14,2},{1,5},{3,7},... | collective-permute-start | bytes 786440 | tf_op jit(solution)/shard_map/ppermute | solution.py:436
  62.5 6.4 %collective-permute-start.21 = (bf16[16,16,256]{2,1,0:T(8,128)(2,1)S(1)}, bf16[16,16,256]{2,1,0:T(8,128)(2,1)S(1)}, u32[]{:S(2)}, u32[]{:S(2)}) collective-permute-start(bf16[16,16,256]{2,1,0:T(8,128)(2,1)S(1)} %collective-permute-done.19), channel_id=1, source_target_pairs={{0,2},{2,0},{4,6},{6,4},{8,10},{10,8},{12,14},{14,12},{1,3},{3,1},... | collective-permute-start | bytes 393224 | tf_op jit(solution)/shard_map/ppermute | solution.py:441
  63.0 9.1 %collective-permute-start.30 = (bf16[16,16,256]{2,1,0:T(8,128)(2,1)S(1)}, bf16[16,16,256]{2,1,0:T(8,128)(2,1)S(1)}, u32[]{:S(2)}, u32[]{:S(2)}) collective-permute-start(bf16[16,16,256]{2,1,0:T(8,128)(2,1)S(1)} %collective-permute-done.28), channel_id=1, source_target_pairs={{0,2},{2,0},{4,6},{6,4},{8,10},{10,8},{12,14},{14,12},{1,3},{3,1},... | collective-permute-start | bytes 393224 | tf_op jit(solution)/shard_map/ppermute | solution.py:441
  64.5 7.6 %collective-permute-start.26 = (bf16[16,16,256]{2,1,0:T(8,128)(2,1)S(1)}, bf16[16,16,256]{2,1,0:T(8,128)(2,1)S(1)}, u32[]{:S(2)}, u32[]{:S(2)}) collective-permute-start(bf16[16,16,256]{2,1,0:T(8,128)(2,1)S(1)} %get-tuple-element.65.refs_3_), channel_id=1, source_target_pairs={{0,2},{2,0},{4,6},{6,4},{8,10},{10,8},{12,14},{14,12},{1,3},{3,1},... | collective-permute-start | bytes 393224 | tf_op jit(solution)/shard_map/ppermute | solution.py:441
  65.0 9.6 %collective-permute-start.23 = (bf16[16,16,256]{2,1,0:T(8,128)(2,1)S(1)}, bf16[16,16,256]{2,1,0:T(8,128)(2,1)S(1)}, u32[]{:S(2)}, u32[]{:S(2)}) collective-permute-start(bf16[16,16,256]{2,1,0:T(8,128)(2,1)S(1)} %get-tuple-element.62.refs_4_), channel_id=1, source_target_pairs={{0,1},{1,0},{2,3},{3,2},{4,5},{5,4},{6,7},{7,6},{8,9},{9,8},{10,11... | collective-permute-start | bytes 393224 | tf_op jit(solution)/shard_map/ppermute | solution.py:431
  69.3 16.8 %copy-start.7 = (bf16[16,32,16,256]{3,2,1,0:T(8,128)(2,1)S(1)}, bf16[16,32,16,256]{3,2,1,0:T(8,128)(2,1)}, u32[]{:S(2)}) copy-start(bf16[16,32,16,256]{3,2,1,0:T(8,128)(2,1)} %get-tuple-element.72.refs_8_) | copy-start | bytes 12582916
  69.3 11.6 %collective-permute-start.33 = (bf16[32,16,256]{2,1,0:T(8,128)(2,1)S(1)}, bf16[32,16,256]{2,1,0:T(8,128)(2,1)S(1)}, u32[]{:S(2)}, u32[]{:S(2)}) collective-permute-start(bf16[32,16,256]{2,1,0:T(8,128)(2,1)S(1)} %mode_sums.7), channel_id=1, source_target_pairs={{0,12},{2,14},{4,0},{6,2},{8,4},{10,6},{12,8},{14,10},{1,13},{3,15... | collective-permute-start | bytes 786440 | tf_op jit(solution)/shard_map/ppermute | solution.py:436
  72.7 11.0 %collective-permute-start.32 = (bf16[32,16,256]{2,1,0:T(8,128)(2,1)S(1)}, bf16[32,16,256]{2,1,0:T(8,128)(2,1)S(1)}, u32[]{:S(2)}, u32[]{:S(2)}) collective-permute-start(bf16[32,16,256]{2,1,0:T(8,128)(2,1)S(1)} %add_convert_fusion), channel_id=1, source_target_pairs={{0,4},{2,6},{4,8},{6,10},{8,12},{10,14},{12,0},{14,2},{1,5},{3,7},... | collective-permute-start | bytes 786440 | tf_op jit(solution)/shard_map/ppermute | solution.py:436
  74.1 5.0 %collective-permute-start.22 = (bf16[16,16,256]{2,1,0:T(8,128)(2,1)S(1)}, bf16[16,16,256]{2,1,0:T(8,128)(2,1)S(1)}, u32[]{:S(2)}, u32[]{:S(2)}) collective-permute-start(bf16[16,16,256]{2,1,0:T(8,128)(2,1)S(1)} %get-tuple-element.61.refs_0_), channel_id=1, source_target_pairs={{0,2},{2,0},{4,6},{6,4},{8,10},{10,8},{12,14},{14,12},{1,3},{3,1},... | collective-permute-start | bytes 393224 | tf_op jit(solution)/shard_map/ppermute | solution.py:441
  74.6 5.9 %collective-permute-start.27 = (bf16[16,16,256]{2,1,0:T(8,128)(2,1)S(1)}, bf16[16,16,256]{2,1,0:T(8,128)(2,1)S(1)}, u32[]{:S(2)}, u32[]{:S(2)}) collective-permute-start(bf16[16,16,256]{2,1,0:T(8,128)(2,1)S(1)} %collective-permute-done.23), channel_id=1, source_target_pairs={{0,2},{2,0},{4,6},{6,4},{8,10},{10,8},{12,14},{14,12},{1,3},{3,1},... | collective-permute-start | bytes 393224 | tf_op jit(solution)/shard_map/ppermute | solution.py:441
  84.5 1.2 %collective-permute-start.34 = (f32[2,16,16]{2,1,0:T(8,128)S(1)}, f32[2,16,16]{2,1,0:T(8,128)S(1)}, u32[]{:S(2)}, u32[]{:S(2)}) collective-permute-start(f32[2,16,16]{2,1,0:T(8,128)S(1)} %get-tuple-element.70), channel_id=1, source_target_pairs={{0,1},{1,0},{2,3},{3,2},{4,5},{5,4},{6,7},{7,6},{8,9},{9,8},{10,11... | collective-permute-start | bytes 6152 | tf_op jit(solution)/shard_map/ppermute | solution.py:431
  85.8 3.7 %collective-permute-start.35 = (f32[2,16,16]{2,1,0:T(8,128)S(1)}, f32[2,16,16]{2,1,0:T(8,128)S(1)}, u32[]{:S(2)}, u32[]{:S(2)}) collective-permute-start(f32[2,16,16]{2,1,0:T(8,128)S(1)} %add.31), channel_id=1, source_target_pairs={{0,2},{2,0},{4,6},{6,4},{8,10},{10,8},{12,14},{14,12},{1,3},{3,1},... | collective-permute-start | bytes 6152 | tf_op jit(solution)/shard_map/ppermute | solution.py:539
  89.5 3.7 %collective-permute-start.36 = (f32[2,16,16]{2,1,0:T(8,128)S(1)}, f32[2,16,16]{2,1,0:T(8,128)S(1)}, u32[]{:S(2)}, u32[]{:S(2)}) collective-permute-start(f32[2,16,16]{2,1,0:T(8,128)S(1)} %add.32), channel_id=1, source_target_pairs={{0,4},{2,6},{4,0},{6,2},{8,12},{10,14},{12,8},{14,10},{1,5},{3,7},... | collective-permute-start | bytes 6152 | tf_op jit(solution)/shard_map/ppermute | solution.py:539
  93.2 8.4 %collective-permute-start.37 = (f32[320,384]{1,0:T(8,128)S(1)}, f32[320,384]{1,0:T(8,128)S(1)}, u32[]{:S(2)}, u32[]{:S(2)}) collective-permute-start(f32[320,384]{1,0:T(8,128)S(1)} %get-tuple-element.80), channel_id=1, source_target_pairs={{0,1},{1,0},{2,3},{3,2},{4,5},{5,4},{6,7},{7,6},{8,9},{9,8},{10,11... | collective-permute-start | bytes 1474568 | tf_op jit(solution)/shard_map/ppermute | solution.py:431
  93.3 4.8 %collective-permute-start.38 = (f32[2,16,16]{2,1,0:T(8,128)S(1)}, f32[2,16,16]{2,1,0:T(8,128)S(1)}, u32[]{:S(2)}, u32[]{:S(2)}) collective-permute-start(f32[2,16,16]{2,1,0:T(8,128)S(1)} %add.34), channel_id=1, source_target_pairs={{0,8},{2,10},{4,12},{6,14},{8,0},{10,2},{12,4},{14,6},{1,9},{3,11}... | collective-permute-start | bytes 6152 | tf_op jit(solution)/shard_map/ppermute | solution.py:539
  98.0 3.6 %collective-permute-start.39 = (f32[320,384]{1,0:T(8,128)S(1)}, f32[320,384]{1,0:T(8,128)S(1)}, u32[]{:S(2)}, u32[]{:S(2)}) collective-permute-start(f32[320,384]{1,0:T(8,128)S(1)} %get-tuple-element.88), channel_id=1, source_target_pairs={{0,1},{1,0},{2,3},{3,2},{4,5},{5,4},{6,7},{7,6},{8,9},{9,8},{10,11... | collective-permute-start | bytes 1474568 | tf_op jit(solution)/shard_map/ppermute | solution.py:431
  (5 other events, 41.0 us)
